TPU v7x, 32 devices: a whole 2x2x4 slice. The times are simulated.
32 devices in a mesh: corpus: 8 (over z, y), vocab: 4 (over x, core).
Axes of the slice: x: 2, y: 2, z: 4, core: 2. Of those that a mesh axis runs over, the one named last changes fastest.
Arguments:
- eval_tiles: bfloat16 [8, 12, 128, 512], P('corpus', 'vocab'), may hold values from 0.019897461 to 2
- eval_tile_list: int32 [8, 12], P(None, 'vocab'), may hold values from 0 to 128, as said below
- corpus_tiles: bfloat16 [32, 12, 128, 512], P('corpus', 'vocab'), may hold values from 0.019897461 to 2
- corpus_tile_list: int32 [32, 12], P('corpus', 'vocab'), may hold values from 0 to 128, as said below
- pair_eval_block: int32 [768], P('corpus'), may hold values from 0 to 7
- pair_corpus_block: int32 [768], P('corpus'), may hold values from 0 to 3
- pair_count: int32 [8], P('corpus'), may hold values from 12 to 96, as said below
- eval_norm: float32 [1024], replicated, may hold values from 8 to 32
- corpus_norm: float32 [4096], P('corpus'), may hold values from 8 to 32
Outputs:
- cosine_tiles: float32 [768, 128, 128], P(('corpus', 'vocab'))
Inputs may be any that keep to these rules, and one draw needn't show every extreme that they name: `eval_tile_list`: value 128 marks an empty slot; other ids of one row block in one slice are distinct. Slot 0 of a block and slice is never empty. `corpus_tile_list`: value 128 marks an empty slot; other ids of one row block in one slice are distinct. Slot 0 of a block and slice is never empty. Shard c's live pair slots are its first pair_count[c] slots. Some shard is full.
All inputs are finite; a program needn't handle non-finite values.
Results may differ from a plain program's by a relative error of at most 0.0003.
Values may be sent and summed in bfloat16 or wider, within the bound.
No kernel may reach another device: no remote copies, remote signals or barrier semaphores. Data moves between devices by JAX's collectives and lax.ppermute only.
A program may use at most 128 MiB of HBM per device.

v0:
```python
import jax
import jax.numpy as jnp
from jax import lax
from jax.sharding import PartitionSpec as P

VOCAB = 262144
GROUP = 8


def local(
    eval_tiles,
    eval_tile_list,
    corpus_tiles,
    corpus_tile_list,
    pair_eval_block,
    pair_corpus_block,
    pair_count,
    eval_norm,
    corpus_norm,
):
    slices = lax.axis_size("vocab")
    term_width = corpus_tiles.shape[3]
    tile_rows = corpus_tiles.shape[2]
    tiles_slice = VOCAB // (term_width * slices)
    pair_slots = pair_eval_block.shape[0]
    quarter = pair_slots // slices
    every_eval = lax.all_gather(eval_tiles, "corpus", axis=0, tiled=True)
    position = jnp.arange(pair_slots, dtype=jnp.int32)
    own_live = position < pair_count[0]
    groups = quarter * lax.axis_size("vocab") // GROUP

    def one_group(group_index, totals):
        first_slot = group_index * GROUP
        living = lax.dynamic_slice_in_dim(own_live, first_slot, GROUP)

        def compute(current):
            eval_index = lax.dynamic_slice_in_dim(pair_eval_block, first_slot, GROUP)
            block_index = lax.dynamic_slice_in_dim(pair_corpus_block, first_slot, GROUP)
            eval_part = every_eval[eval_index]
            eval_list = eval_tile_list[eval_index]
            corpus_part = corpus_tiles[block_index]
            corpus_list = corpus_tile_list[block_index]
            matched = (eval_list[:, :, None] == corpus_list[:, None, :]) & (
                eval_list[:, :, None] < tiles_slice
            )
            aligned = jnp.einsum(
                "gij,gjrt->girt",
                matched.astype(jnp.bfloat16),
                corpus_part,
                preferred_element_type=jnp.float32,
            ).astype(jnp.bfloat16)
            products = jnp.einsum(
                "girt,gist->grs", eval_part, aligned, preferred_element_type=jnp.float32
            )
            products = jnp.where(living[:, None, None], products, 0.0)
            return lax.dynamic_update_slice_in_dim(current, products, group_index * GROUP, 0)

        return lax.cond(jnp.any(living), compute, lambda current: current, totals)

    start_totals = jnp.zeros((quarter * lax.axis_size("vocab"), tile_rows, tile_rows), jnp.float32)
    summed = lax.psum_scatter(
        lax.fori_loop(0, groups, one_group, start_totals), "vocab", scatter_dimension=0, tiled=True
    )
    vocab_index = lax.axis_index("vocab")
    first_pair = vocab_index * quarter
    mine_eval = lax.dynamic_slice_in_dim(pair_eval_block, first_pair, quarter)
    mine_block = lax.dynamic_slice_in_dim(pair_corpus_block, first_pair, quarter)
    mine_live = lax.dynamic_slice_in_dim(own_live, first_pair, quarter)
    eval_scale = eval_norm.reshape(-1, tile_rows)[mine_eval]
    corpus_scale = corpus_norm.reshape(-1, tile_rows)[mine_block]
    cosine = summed / (eval_scale[:, :, None] * corpus_scale[:, None, :])
    return jnp.where(mine_live[:, None, None], cosine, 0.0)


def solution(mesh):
    in_specs = (
        P("corpus", "vocab", None, None),
        P(None, "vocab"),
        P("corpus", "vocab", None, None),
        P("corpus", "vocab"),
        P("corpus"),
        P("corpus"),
        P("corpus"),
        P(),
        P("corpus"),
    )
    out_specs = P(("corpus", "vocab"), None, None)
    return jax.shard_map(local, mesh=mesh, in_specs=in_specs, out_specs=out_specs, check_vma=False)
```

profile of v0, /device:TPU:0, one launch (start us, length us, event | category | flops | bytes accessed | tf_op | source)
XLA Modules:
  0.0 338.7 jit_solution(12847975143170615195)
XLA Ops:
  8.0 0.8 copy.11
  8.7 64.0 %all-gather.2.cloned.1.call-done = bf16[8,3,128,512]{3,2,1,0:T(8,128)(2,1)} async-done(((bf16[1,3,128,512]{3,2,1,0:T(8,128)(2,1)}), bf16[8,3,128,512]{3,2,1,0:T(8,128)(2,1)}) %all-gather.2.cloned.1.call-update) | async-done | bytes 3145744 | tf_op jit(solution)/shard_map/all_gather | solution.py:27
  72.7 3.4 %broadcast_in_dim.49 = f32[96,128,128]{2,1,0:T(8,128)} broadcast(f32[]{:T(128)} %constant.63.clone.1), dimensions={} | broadcast | bytes 6291460 | tf_op jit(solution)/shard_map/broadcast_in_dim | solution.py:60
  76.2 106.6 %while.16 = (s32[]{:T(128)}, f32[96,128,128]{2,1,0:T(8,128)}, pred[96]{0:T(512)(128)(4,1)S(1)}, s32[96]{0:T(128)S(1)}, bf16[8,3,128,512]{3,2,1,0:T(8,128)(2,1)},...) while((s32[]{:T(128)}, f32[96,128,128]{2,1,0:T(8,128)}, ...), condition=%wide.region_4.5_spmd, body=%wide.region_0.4_spmd.sunk | while | flops 412223712 | bytes 38282672 | solution.py:62
  76.2 0.8 fusion.15
  77.6 14.9 %conditional.2 = (f32[96,128,128]{2,1,0:T(8,128)}) conditional(s32[]{:T(128)} %convert_element_type.20, f32[96,128,128]{2,1,0:T(8,128)} %get-tuple-element.313, (pred[8]{0:T(512)(128)(4,1)S(1)}, s32[]{:T(128)}, s32[96]{0:T(128)S(1)}, bf16[8,3,128,512]{3,2,1,0:T(8,128)(2,1)}, s32[8,3]{1,0:T(8,128)S(1)}, /*index=5*/s32[96]{0:T(128)S(1)}, ...), branch_computations={%region_2.0_spmd, %region_3.3_spmd} | conditional | flops 412223712 | bytes 38282388 | solution.py:58
  77.7 4.3 %gather_fusion = bf16[8,3,128,512]{3,2,1,0:T(8,128)(2,1)} fusion(bf16[8,3,128,512]{3,2,1,0:T(8,128)(2,1)} %get-tuple-element.178, s32[1024]{0:T(1024)S(1)} %pad_clamp_fusion.1), kind=kCustom, calls=%fused_computation | custom fusion | bytes 6291488 | tf_op jit(solution)/shard_map/while/body/eval_jaxpr/cond/branch_1_fun/gather | solution.py:39
  82.0 2.4 gather_fusion.3
  85.5 4.9 %fusion = bf16[8,3,128,512]{3,1,2,0:T(4,128)(2,1)S(1)} fusion(bf16[8,3,128,512]{3,2,1,0:T(8,128)(2,1)} %gather_fusion.3, s32[8,3]{1,0:T(8,128)S(1)} %gather_fusion.2, s32[8,3]{1,0:T(8,128)S(1)} %gather_fusion.1, pred[8,3]{1,0:T(8,128)(4,1)S(1)} %broadcast_compare_fusion), kind=kOutput, calls=%fused_computation.7 | convolution fusion | flops 9437328 | bytes 6291672 | tf_op jit(solution)/shard_map/while/body/eval_jaxpr/cond/branch_1_fun/gij,gjrt->girt/dot_general | solution.py:46
  90.5 2.0 fusion.5
  92.5 0.8 fusion.15
  93.9 14.9 %conditional.2 = (f32[96,128,128]{2,1,0:T(8,128)}) conditional(s32[]{:T(128)} %convert_element_type.20, f32[96,128,128]{2,1,0:T(8,128)} %get-tuple-element.313, (pred[8]{0:T(512)(128)(4,1)S(1)}, s32[]{:T(128)}, s32[96]{0:T(128)S(1)}, bf16[8,3,128,512]{3,2,1,0:T(8,128)(2,1)}, s32[8,3]{1,0:T(8,128)S(1)}, /*index=5*/s32[96]{0:T(128)S(1)}, ...), branch_computations={%region_2.0_spmd, %region_3.3_spmd} | conditional | flops 412223712 | bytes 38282388 | solution.py:58
  94.0 4.3 %gather_fusion = bf16[8,3,128,512]{3,2,1,0:T(8,128)(2,1)} fusion(bf16[8,3,128,512]{3,2,1,0:T(8,128)(2,1)} %get-tuple-element.178, s32[1024]{0:T(1024)S(1)} %pad_clamp_fusion.1), kind=kCustom, calls=%fused_computation | custom fusion | bytes 6291488 | tf_op jit(solution)/shard_map/while/body/eval_jaxpr/cond/branch_1_fun/gather | solution.py:39
  98.3 2.4 gather_fusion.3
  101.8 4.9 %fusion = bf16[8,3,128,512]{3,1,2,0:T(4,128)(2,1)S(1)} fusion(bf16[8,3,128,512]{3,2,1,0:T(8,128)(2,1)} %gather_fusion.3, s32[8,3]{1,0:T(8,128)S(1)} %gather_fusion.2, s32[8,3]{1,0:T(8,128)S(1)} %gather_fusion.1, pred[8,3]{1,0:T(8,128)(4,1)S(1)} %broadcast_compare_fusion), kind=kOutput, calls=%fused_computation.7 | convolution fusion | flops 9437328 | bytes 6291672 | tf_op jit(solution)/shard_map/while/body/eval_jaxpr/cond/branch_1_fun/gij,gjrt->girt/dot_general | solution.py:46
  106.8 2.0 fusion.5
  108.8 0.8 fusion.15
  110.2 15.0 %conditional.2 = (f32[96,128,128]{2,1,0:T(8,128)}) conditional(s32[]{:T(128)} %convert_element_type.20, f32[96,128,128]{2,1,0:T(8,128)} %get-tuple-element.313, (pred[8]{0:T(512)(128)(4,1)S(1)}, s32[]{:T(128)}, s32[96]{0:T(128)S(1)}, bf16[8,3,128,512]{3,2,1,0:T(8,128)(2,1)}, s32[8,3]{1,0:T(8,128)S(1)}, /*index=5*/s32[96]{0:T(128)S(1)}, ...), branch_computations={%region_2.0_spmd, %region_3.3_spmd} | conditional | flops 412223712 | bytes 38282388 | solution.py:58
  110.3 4.3 %gather_fusion = bf16[8,3,128,512]{3,2,1,0:T(8,128)(2,1)} fusion(bf16[8,3,128,512]{3,2,1,0:T(8,128)(2,1)} %get-tuple-element.178, s32[1024]{0:T(1024)S(1)} %pad_clamp_fusion.1), kind=kCustom, calls=%fused_computation | custom fusion | bytes 6291488 | tf_op jit(solution)/shard_map/while/body/eval_jaxpr/cond/branch_1_fun/gather | solution.py:39
  114.6 2.4 gather_fusion.3
  118.2 4.9 %fusion = bf16[8,3,128,512]{3,1,2,0:T(4,128)(2,1)S(1)} fusion(bf16[8,3,128,512]{3,2,1,0:T(8,128)(2,1)} %gather_fusion.3, s32[8,3]{1,0:T(8,128)S(1)} %gather_fusion.2, s32[8,3]{1,0:T(8,128)S(1)} %gather_fusion.1, pred[8,3]{1,0:T(8,128)(4,1)S(1)} %broadcast_compare_fusion), kind=kOutput, calls=%fused_computation.7 | convolution fusion | flops 9437328 | bytes 6291672 | tf_op jit(solution)/shard_map/while/body/eval_jaxpr/cond/branch_1_fun/gij,gjrt->girt/dot_general | solution.py:46
  123.1 2.1 fusion.5
  125.2 0.8 fusion.15
  126.6 14.9 %conditional.2 = (f32[96,128,128]{2,1,0:T(8,128)}) conditional(s32[]{:T(128)} %convert_element_type.20, f32[96,128,128]{2,1,0:T(8,128)} %get-tuple-element.313, (pred[8]{0:T(512)(128)(4,1)S(1)}, s32[]{:T(128)}, s32[96]{0:T(128)S(1)}, bf16[8,3,128,512]{3,2,1,0:T(8,128)(2,1)}, s32[8,3]{1,0:T(8,128)S(1)}, /*index=5*/s32[96]{0:T(128)S(1)}, ...), branch_computations={%region_2.0_spmd, %region_3.3_spmd} | conditional | flops 412223712 | bytes 38282388 | solution.py:58
  126.7 4.3 %gather_fusion = bf16[8,3,128,512]{3,2,1,0:T(8,128)(2,1)} fusion(bf16[8,3,128,512]{3,2,1,0:T(8,128)(2,1)} %get-tuple-element.178, s32[1024]{0:T(1024)S(1)} %pad_clamp_fusion.1), kind=kCustom, calls=%fused_computation | custom fusion | bytes 6291488 | tf_op jit(solution)/shard_map/while/body/eval_jaxpr/cond/branch_1_fun/gather | solution.py:39
  131.0 2.4 gather_fusion.3
  134.5 4.9 %fusion = bf16[8,3,128,512]{3,1,2,0:T(4,128)(2,1)S(1)} fusion(bf16[8,3,128,512]{3,2,1,0:T(8,128)(2,1)} %gather_fusion.3, s32[8,3]{1,0:T(8,128)S(1)} %gather_fusion.2, s32[8,3]{1,0:T(8,128)S(1)} %gather_fusion.1, pred[8,3]{1,0:T(8,128)(4,1)S(1)} %broadcast_compare_fusion), kind=kOutput, calls=%fused_computation.7 | convolution fusion | flops 9437328 | bytes 6291672 | tf_op jit(solution)/shard_map/while/body/eval_jaxpr/cond/branch_1_fun/gij,gjrt->girt/dot_general | solution.py:46
  139.5 2.1 fusion.5
  141.5 0.8 fusion.15
  142.9 14.9 %conditional.2 = (f32[96,128,128]{2,1,0:T(8,128)}) conditional(s32[]{:T(128)} %convert_element_type.20, f32[96,128,128]{2,1,0:T(8,128)} %get-tuple-element.313, (pred[8]{0:T(512)(128)(4,1)S(1)}, s32[]{:T(128)}, s32[96]{0:T(128)S(1)}, bf16[8,3,128,512]{3,2,1,0:T(8,128)(2,1)}, s32[8,3]{1,0:T(8,128)S(1)}, /*index=5*/s32[96]{0:T(128)S(1)}, ...), branch_computations={%region_2.0_spmd, %region_3.3_spmd} | conditional | flops 412223712 | bytes 38282388 | solution.py:58
  143.0 4.3 %gather_fusion = bf16[8,3,128,512]{3,2,1,0:T(8,128)(2,1)} fusion(bf16[8,3,128,512]{3,2,1,0:T(8,128)(2,1)} %get-tuple-element.178, s32[1024]{0:T(1024)S(1)} %pad_clamp_fusion.1), kind=kCustom, calls=%fused_computation | custom fusion | bytes 6291488 | tf_op jit(solution)/shard_map/while/body/eval_jaxpr/cond/branch_1_fun/gather | solution.py:39
  147.3 2.4 gather_fusion.3
  150.8 4.9 %fusion = bf16[8,3,128,512]{3,1,2,0:T(4,128)(2,1)S(1)} fusion(bf16[8,3,128,512]{3,2,1,0:T(8,128)(2,1)} %gather_fusion.3, s32[8,3]{1,0:T(8,128)S(1)} %gather_fusion.2, s32[8,3]{1,0:T(8,128)S(1)} %gather_fusion.1, pred[8,3]{1,0:T(8,128)(4,1)S(1)} %broadcast_compare_fusion), kind=kOutput, calls=%fused_computation.7 | convolution fusion | flops 9437328 | bytes 6291672 | tf_op jit(solution)/shard_map/while/body/eval_jaxpr/cond/branch_1_fun/gij,gjrt->girt/dot_general | solution.py:46
  155.8 2.0 fusion.5
  157.8 0.8 fusion.15
  159.2 14.9 %conditional.2 = (f32[96,128,128]{2,1,0:T(8,128)}) conditional(s32[]{:T(128)} %convert_element_type.20, f32[96,128,128]{2,1,0:T(8,128)} %get-tuple-element.313, (pred[8]{0:T(512)(128)(4,1)S(1)}, s32[]{:T(128)}, s32[96]{0:T(128)S(1)}, bf16[8,3,128,512]{3,2,1,0:T(8,128)(2,1)}, s32[8,3]{1,0:T(8,128)S(1)}, /*index=5*/s32[96]{0:T(128)S(1)}, ...), branch_computations={%region_2.0_spmd, %region_3.3_spmd} | conditional | flops 412223712 | bytes 38282388 | solution.py:58
  159.3 4.3 %gather_fusion = bf16[8,3,128,512]{3,2,1,0:T(8,128)(2,1)} fusion(bf16[8,3,128,512]{3,2,1,0:T(8,128)(2,1)} %get-tuple-element.178, s32[1024]{0:T(1024)S(1)} %pad_clamp_fusion.1), kind=kCustom, calls=%fused_computation | custom fusion | bytes 6291488 | tf_op jit(solution)/shard_map/while/body/eval_jaxpr/cond/branch_1_fun/gather | solution.py:39
  163.6 2.4 gather_fusion.3
  167.2 4.9 %fusion = bf16[8,3,128,512]{3,1,2,0:T(4,128)(2,1)S(1)} fusion(bf16[8,3,128,512]{3,2,1,0:T(8,128)(2,1)} %gather_fusion.3, s32[8,3]{1,0:T(8,128)S(1)} %gather_fusion.2, s32[8,3]{1,0:T(8,128)S(1)} %gather_fusion.1, pred[8,3]{1,0:T(8,128)(4,1)S(1)} %broadcast_compare_fusion), kind=kOutput, calls=%fused_computation.7 | convolution fusion | flops 9437328 | bytes 6291672 | tf_op jit(solution)/shard_map/while/body/eval_jaxpr/cond/branch_1_fun/gij,gjrt->girt/dot_general | solution.py:46
  172.1 2.1 fusion.5
  174.2 0.8 fusion.15
  175.6 0.8 fusion.15
  177.0 0.8 fusion.15
  178.5 0.8 fusion.15
  179.9 0.8 fusion.15
  181.3 0.8 fusion.15
  184.6 144.2 %reduce-scatter.2.cloned.1.call-done = f32[24,128,128]{2,1,0:T(8,128)} async-done(((f32[96,128,128]{2,1,0:T(8,128)}), f32[24,128,128]{2,1,0:T(8,128)}) %reduce-scatter.2.cloned.1.call-update) | async-done | bytes 1572880 | tf_op jit(solution)/shard_map/reduce_scatter | solution.py:61
  328.8 3.1 divide_select_fusion
  (77 shorter events, 9.9 us)
Async XLA Ops:
  6.5 177.5 %copy-start = (f32[1024]{0:T(1024)S(1)}, f32[1024]{0:T(1024)}, u32[]{:S(2)}) copy-start(f32[1024]{0:T(1024)} %param.20) | copy-start | bytes 12292
  6.5 66.2 %all-gather.2.cloned.1.call-start = ((), (), s32[]{:S(2)}) async-start(), calls=%async_computation.1 | async-start | bytes 3538944 | tf_op jit(solution)/shard_map/all_gather | solution.py:27
  7.3 321.5 %reduce-scatter.2.cloned.1.call-start = ((), (), s32[]{:S(2)}) async-start(), calls=%async_computation.2 | async-start | bytes 7864320 | tf_op jit(solution)/shard_map/reduce_scatter | solution.py:61
  8.7 67.4 %copy-start.1 = (bf16[4,3,128,512]{3,2,1,0:T(8,128)(2,1)S(1)}, bf16[4,3,128,512]{3,2,1,0:T(8,128)(2,1)}, u32[]{:S(2)}) copy-start(bf16[4,3,128,512]{3,2,1,0:T(8,128)(2,1)} %param.15) | copy-start | bytes 4718596
  8.7 67.4 %copy-start.3 = (s32[4,3]{1,0:T(4,128)S(1)}, s32[4,3]{1,0:T(4,128)}, u32[]{:S(2)}) copy-start(s32[4,3]{1,0:T(4,128)} %param.16) | copy-start | bytes 148
  8.7 67.4 %copy-start.5 = (s32[96]{0:T(128)S(1)}, s32[96]{0:T(128)}, u32[]{:S(2)}) copy-start(s32[96]{0:T(128)} %param.17) | copy-start | bytes 1156
  8.7 67.4 %copy-start.6 = (s32[96]{0:T(128)S(1)}, s32[96]{0:T(128)}, u32[]{:S(2)}) copy-start(s32[96]{0:T(128)} %param.18) | copy-start | bytes 1156
  85.5 4.9 %copy-start.2 = (bf16[8,3,128,512]{3,2,1,0:T(8,128)(2,1)S(1)}, bf16[8,3,128,512]{3,2,1,0:T(8,128)(2,1)}, u32[]{:S(2)}) copy-start(bf16[8,3,128,512]{3,2,1,0:T(8,128)(2,1)} %gather_fusion) | copy-start | bytes 9437188 | tf_op jit(solution)/shard_map/while/body/eval_jaxpr/cond
  101.8 4.9 %copy-start.2 = (bf16[8,3,128,512]{3,2,1,0:T(8,128)(2,1)S(1)}, bf16[8,3,128,512]{3,2,1,0:T(8,128)(2,1)}, u32[]{:S(2)}) copy-start(bf16[8,3,128,512]{3,2,1,0:T(8,128)(2,1)} %gather_fusion) | copy-start | bytes 9437188 | tf_op jit(solution)/shard_map/while/body/eval_jaxpr/cond
  118.2 4.9 %copy-start.2 = (bf16[8,3,128,512]{3,2,1,0:T(8,128)(2,1)S(1)}, bf16[8,3,128,512]{3,2,1,0:T(8,128)(2,1)}, u32[]{:S(2)}) copy-start(bf16[8,3,128,512]{3,2,1,0:T(8,128)(2,1)} %gather_fusion) | copy-start | bytes 9437188 | tf_op jit(solution)/shard_map/while/body/eval_jaxpr/cond
  134.5 4.9 %copy-start.2 = (bf16[8,3,128,512]{3,2,1,0:T(8,128)(2,1)S(1)}, bf16[8,3,128,512]{3,2,1,0:T(8,128)(2,1)}, u32[]{:S(2)}) copy-start(bf16[8,3,128,512]{3,2,1,0:T(8,128)(2,1)} %gather_fusion) | copy-start | bytes 9437188 | tf_op jit(solution)/shard_map/while/body/eval_jaxpr/cond
  150.8 4.9 %copy-start.2 = (bf16[8,3,128,512]{3,2,1,0:T(8,128)(2,1)S(1)}, bf16[8,3,128,512]{3,2,1,0:T(8,128)(2,1)}, u32[]{:S(2)}) copy-start(bf16[8,3,128,512]{3,2,1,0:T(8,128)(2,1)} %gather_fusion) | copy-start | bytes 9437188 | tf_op jit(solution)/shard_map/while/body/eval_jaxpr/cond
  167.2 4.9 %copy-start.2 = (bf16[8,3,128,512]{3,2,1,0:T(8,128)(2,1)S(1)}, bf16[8,3,128,512]{3,2,1,0:T(8,128)(2,1)}, u32[]{:S(2)}) copy-start(bf16[8,3,128,512]{3,2,1,0:T(8,128)(2,1)} %gather_fusion) | copy-start | bytes 9437188 | tf_op jit(solution)/shard_map/while/body/eval_jaxpr/cond
  182.7 0.7 copy-start.4
Sparse Core Ops, SparseCore 0:
  9.5 63.1 all-gather.1
  182.9 145.8 reduce-scatter.1
where the time goes:
time: 340 us; the launch traced here: 339 us
  waiting for transfers between devices  209 us (61%)
  local copies, waits for them, and re-layouts  52.7 us (16%)
  matrix products  41.9 us (12%)
  between operations  14.1 us (4%)
  other arithmetic  12.8 us (4%)
  loops' own time  8.26 us (2%)
    reduce_scatter x1, waiting for transfers between devices, local(): lax.psum_scatter(lax.fori_loop(0, groups, one_group, start_totals), 'voca...  144 us
    all_gather x1, waiting for transfers between devices, local(): every_eval = lax.all_gather(eval_tiles, 'corpus', axis=0, tiled=True)  64 us
    dot_general x6, matrix products, compute(): jnp.einsum('gij,gjrt->girt', matched.astype(jnp.bfloat16), corpus_part, p...  29.5 us
    gather x6, local copies, waits for them, and re-layouts, compute(): eval_part = every_eval[eval_index]  25.8 us
    gather x6, local copies, waits for them, and re-layouts, compute(): corpus_part = corpus_tiles[block_index]  14.3 us
    dot_general x6, matrix products, compute(): jnp.einsum('girt,gist->grs', eval_part, aligned, preferred_element_type=j...  12.3 us
    reduce_or x12, other arithmetic, one_group(): return lax.cond(jnp.any(living), compute, lambda current: current, totals)  9.07 us
    another operation x1, loops' own time, local(): lax.fori_loop(0, groups, one_group, start_totals)  7.77 us
  transfers between devices with their start and end apart: 2, of which 2 were waited for; matrix products, arithmetic and copies ran while one was open for 1% of the time, Pallas kernels for 0%

commit v1 on v0

--- a/solution.py
+++ b/solution.py
@@ -1,13 +1,24 @@
+import functools
+
 import jax
 import jax.numpy as jnp
 from jax import lax
+from jax.experimental import pallas as pl
+from jax.experimental.pallas import tpu as pltpu
 from jax.sharding import PartitionSpec as P
 
 VOCAB = 262144
 GROUP = 8
-
-
-def local(
+VMEM = pl.BlockSpec(memory_space=pltpu.VMEM)
+SMEM = pl.BlockSpec(memory_space=pltpu.SMEM)
+LIMIT = 24 * 1024 * 1024
+
+
+def tiles_in_slice(corpus_tiles):
+    return VOCAB // (corpus_tiles.shape[3] * lax.axis_size("vocab"))
+
+
+def general(
     eval_tiles,
     eval_tile_list,
     corpus_tiles,
@@ -19,15 +30,14 @@
     corpus_norm,
 ):
     slices = lax.axis_size("vocab")
-    term_width = corpus_tiles.shape[3]
     tile_rows = corpus_tiles.shape[2]
-    tiles_slice = VOCAB // (term_width * slices)
+    tiles_slice = tiles_in_slice(corpus_tiles)
     pair_slots = pair_eval_block.shape[0]
     quarter = pair_slots // slices
     every_eval = lax.all_gather(eval_tiles, "corpus", axis=0, tiled=True)
     position = jnp.arange(pair_slots, dtype=jnp.int32)
     own_live = position < pair_count[0]
-    groups = quarter * lax.axis_size("vocab") // GROUP
+    groups = pair_slots // GROUP
 
     def one_group(group_index, totals):
         first_slot = group_index * GROUP
@@ -53,16 +63,15 @@
                 "girt,gist->grs", eval_part, aligned, preferred_element_type=jnp.float32
             )
             products = jnp.where(living[:, None, None], products, 0.0)
-            return lax.dynamic_update_slice_in_dim(current, products, group_index * GROUP, 0)
+            return lax.dynamic_update_slice_in_dim(current, products, first_slot, 0)
 
         return lax.cond(jnp.any(living), compute, lambda current: current, totals)
 
-    start_totals = jnp.zeros((quarter * lax.axis_size("vocab"), tile_rows, tile_rows), jnp.float32)
+    start_totals = jnp.zeros((pair_slots, tile_rows, tile_rows), jnp.float32)
     summed = lax.psum_scatter(
         lax.fori_loop(0, groups, one_group, start_totals), "vocab", scatter_dimension=0, tiled=True
     )
-    vocab_index = lax.axis_index("vocab")
-    first_pair = vocab_index * quarter
+    first_pair = lax.axis_index("vocab") * quarter
     mine_eval = lax.dynamic_slice_in_dim(pair_eval_block, first_pair, quarter)
     mine_block = lax.dynamic_slice_in_dim(pair_corpus_block, first_pair, quarter)
     mine_live = lax.dynamic_slice_in_dim(own_live, first_pair, quarter)
@@ -72,6 +81,195 @@
     return jnp.where(mine_live[:, None, None], cosine, 0.0)
 
 
+def dots_kernel(tiles_slice, place_ref, eval_list_ref, corpus_list_ref, *refs, arrivals):
+    eval_refs, corpus_ref = refs[: len(arrivals)], refs[len(arrivals)]
+    keep_ref, send_ref = refs[len(arrivals) + 1 :]
+    blocks, slots = corpus_ref.shape[:2]
+    half = blocks // 2
+    core = place_ref[0]
+    for at, (arrival, eval_ref) in enumerate(zip(arrivals, eval_refs)):
+        e = place_ref[1 + arrival]
+        ids = [eval_list_ref[e, i] for i in range(slots)]
+        for side, out_ref in ((0, keep_ref), (1, send_ref)):
+            for q in range(half):
+                d = ((core + side) % 2) * half + q
+                total = None
+                for i in range(slots):
+                    column, hit = 0, jnp.float32(0.0)
+                    for j in range(slots):
+                        same = (ids[i] == corpus_list_ref[d, j]) & (ids[i] < tiles_slice)
+                        column = jnp.where(same, j, column)
+                        hit = jnp.where(same, 1.0, hit)
+                    left = eval_ref[0, i] * hit.astype(jnp.bfloat16)
+                    product = lax.dot_general(
+                        left,
+                        corpus_ref[d, column],
+                        (((1,), (1,)), ((), ())),
+                        preferred_element_type=jnp.float32,
+                    )
+                    total = product if total is None else total + product
+                out_ref[at * half + q] = total
+
+
+def dots(place, eval_tile_list, corpus_tile_list, corpus_tiles, eval_blocks, arrivals):
+    blocks, slots, rows, terms = corpus_tiles.shape
+    shape = jax.ShapeDtypeStruct((len(arrivals) * (blocks // 2), rows, rows), jnp.float32)
+    return pl.pallas_call(
+        functools.partial(dots_kernel, tiles_in_slice(corpus_tiles), arrivals=arrivals),
+        out_shape=(shape, shape),
+        in_specs=[SMEM] * 3 + [VMEM] * (len(arrivals) + 1),
+        out_specs=(VMEM, VMEM),
+        compiler_params=pltpu.CompilerParams(vmem_limit_bytes=LIMIT),
+        cost_estimate=pl.CostEstimate(
+            flops=2 * len(arrivals) * blocks * slots * rows * rows * terms,
+            bytes_accessed=2 * (corpus_tiles.size + sum(b.size for b in eval_blocks)),
+            transcendentals=0,
+        ),
+    )(place, eval_tile_list, corpus_tile_list, *eval_blocks, corpus_tiles)
+
+
+def scale_kernel(eval_ref, corpus_ref, live_ref, out_ref):
+    for p in range(out_ref.shape[0]):
+        factor = 1.0 / (eval_ref[:, p : p + 1] * corpus_ref[p : p + 1, :])
+        out_ref[p] = jnp.where(live_ref[p] > 0, factor, 0.0)
+
+
+def spread_kernel(chunks, item_ref, scale_ref, *refs):
+    sums, (out_ref, table, staged, sem) = refs[:-4], refs[-4:]
+    half_items = table.shape[0] // 2
+    base = 0
+    for t in range(chunks):
+        mine, other = sums[2 * t], sums[2 * t + 1]
+        n = mine.shape[0]
+        table[base : base + n] = mine[...]
+        table[half_items + base : half_items + base + n] = other[...]
+        base += n
+    copies = []
+    group = 6 if out_ref.shape[0] % 6 == 0 else out_ref.shape[0]
+    for p in range(out_ref.shape[0]):
+        staged[p] = table[item_ref[p]] * scale_ref[p]
+        if (p + 1) % group == 0:
+            part = pl.ds(p + 1 - group, group)
+            copy = pltpu.make_async_copy(staged.at[part], out_ref.at[part], sem.at[p // group])
+            copy.start()
+            copies.append(copy)
+    for copy in copies:
+        copy.wait()
+
+
+def few_items(
+    eval_tiles,
+    eval_tile_list,
+    corpus_tiles,
+    corpus_tile_list,
+    pair_eval_block,
+    pair_corpus_block,
+    pair_count,
+    eval_norm,
+    corpus_norm,
+):
+    shards, slices = lax.axis_size("corpus"), lax.axis_size("vocab")
+    rows = corpus_tiles.shape[2]
+    blocks = corpus_tiles.shape[0]
+    half = blocks // 2
+    pair_slots = pair_eval_block.shape[0]
+    quarter = pair_slots // slices
+    lines = shards // 2
+
+    ring = list(range(0, lines, 2)) + list(range(1, lines, 2))[::-1]
+    along = [(ring[i] * 2 + y, ring[(i + 1) % lines] * 2 + y) for i in range(lines) for y in range(2)]
+    across = [(c, c ^ 1) for c in range(shards)]
+    to_core = [(v, v ^ 1) for v in range(slices)]
+    to_chip = [(v, v ^ 2) for v in range(slices)]
+
+    order = [(0, 0)]
+    for step in range(1, lines):
+        order += [(step, 0), (step - 1, 1)]
+    order.append((lines - 1, 1))
+
+    shard, vocab = lax.axis_index("corpus"), lax.axis_index("vocab")
+    core = vocab % 2
+    ring_at = jnp.asarray(ring, jnp.int32)
+    line_of = jnp.arange(lines, dtype=jnp.int32)
+    my_ring = jnp.sum(jnp.where(ring_at == shard // 2, line_of, 0))
+    steps = jnp.asarray([k for k, _ in order], jnp.int32)
+    flips = jnp.asarray([f for _, f in order], jnp.int32)
+    from_ring = (my_ring - steps + lines) % lines
+    from_line = jnp.sum(jnp.where(from_ring[:, None] == line_of[None, :], ring_at[None, :], 0), axis=1)
+    from_shard = from_line * 2 + (shard % 2 ^ flips)
+    place = jnp.concatenate([core[None].astype(jnp.int32), from_shard.astype(jnp.int32)])
+
+    first_pair = vocab * quarter
+    mine_eval = lax.dynamic_slice_in_dim(pair_eval_block, first_pair, quarter)
+    mine_block = lax.dynamic_slice_in_dim(pair_corpus_block, first_pair, quarter)
+    arrival_of = jnp.sum(
+        jnp.where(mine_eval[:, None] == from_shard[None, :], jnp.arange(shards, dtype=jnp.int32)[None, :], 0), axis=1
+    )
+    other_side = (mine_block // half) ^ core
+    item = other_side * (shards * half) + arrival_of * half + mine_block % half
+    live = ((first_pair + jnp.arange(quarter, dtype=jnp.int32)) < pair_count[0]).astype(jnp.int32)
+    eval_scale = jnp.sum(
+        jnp.where(
+            mine_eval[None, :, None] == jnp.arange(shards, dtype=jnp.int32)[None, None, :],
+            eval_norm.reshape(shards, rows).T[:, None, :],
+            0.0,
+        ),
+        axis=2,
+    )
+    corpus_scale = jnp.sum(
+        jnp.where(
+            mine_block[:, None, None] == jnp.arange(blocks, dtype=jnp.int32)[None, :, None],
+            corpus_norm.reshape(blocks, rows)[None],
+            0.0,
+        ),
+        axis=1,
+    )
+    scale = pl.pallas_call(
+        scale_kernel,
+        out_shape=jax.ShapeDtypeStruct((quarter, rows, rows), jnp.float32),
+        in_specs=[VMEM, VMEM, SMEM],
+        out_specs=VMEM,
+        compiler_params=pltpu.CompilerParams(vmem_limit_bytes=LIMIT),
+    )(eval_scale, corpus_scale, live)
+
+    work = functools.partial(dots, place, eval_tile_list, corpus_tile_list, corpus_tiles)
+
+    def reduce(keep, send):
+        chip = keep + lax.ppermute(send, "vocab", to_core)
+        total = chip + lax.ppermute(chip, "vocab", to_chip)
+        return total, lax.ppermute(total, "vocab", to_core)
+
+    held = eval_tiles
+    arrived, names = [eval_tiles], [0]
+    sums = []
+    for step in range(lines):
+        exchanged = lax.ppermute(held, "corpus", across)
+        if step < lines - 1:
+            moved = lax.ppermute(held, "corpus", along)
+            if step > 0:
+                sums += reduce(*work(arrived, tuple(names)))
+                names = []
+                arrived = []
+            held, exchanged = lax.optimization_barrier((moved, exchanged))
+            names += [1 + 2 * step, 2 + 2 * step]
+            arrived += [held, exchanged]
+        else:
+            sums += reduce(*work(arrived, tuple(names)))
+            sums += reduce(*work([exchanged], (2 * lines - 1,)))
+    return pl.pallas_call(
+        functools.partial(spread_kernel, len(sums) // 2),
+        out_shape=jax.ShapeDtypeStruct((quarter, rows, rows), jnp.float32),
+        in_specs=[SMEM] + [VMEM] * (1 + len(sums)),
+        out_specs=pl.BlockSpec(memory_space=pl.ANY),
+        scratch_shapes=[
+            pltpu.VMEM((shards * blocks, rows, rows), jnp.float32),
+            pltpu.VMEM((quarter, rows, rows), jnp.float32),
+            pltpu.SemaphoreType.DMA((quarter,)),
+        ],
+        compiler_params=pltpu.CompilerParams(vmem_limit_bytes=LIMIT),
+    )(item, scale, *sums)
+
+
 def solution(mesh):
     in_specs = (
         P("corpus", "vocab", None, None),
@@ -85,4 +283,12 @@
         P("corpus"),
     )
     out_specs = P(("corpus", "vocab"), None, None)
-    return jax.shard_map(local, mesh=mesh, in_specs=in_specs, out_specs=out_specs, check_vma=False)
+
+    def program(*arrays):
+        shards, slices = mesh.shape["corpus"], mesh.shape["vocab"]
+        evals, blocks, slots = arrays[0].shape[0], arrays[2].shape[0] // shards, arrays[4].shape[0] // shards
+        few = slices == 4 and shards == evals and shards % 2 == 0 and blocks % 2 == 0 and evals * blocks <= slots
+        local = few_items if few else general
+        return jax.shard_map(local, mesh=mesh, in_specs=in_specs, out_specs=out_specs, check_vma=False)(*arrays)
+
+    return program

time: 340 us -> 62.5 us (0.18)
  waiting for transfers between devices: 209 us -> 20.1 us
  local copies, waits for them, and re-layouts: 52.7 us -> 4.78 us
  matrix products: 41.9 us -> 0 us
  starting transfers between devices: 0.04 us -> 20.3 us
  between operations: 14.1 us -> 0.87 us
  Pallas kernels: 0 us -> 10.4 us
  loops' own time: 8.26 us -> 0 us
  other arithmetic: 12.8 us -> 5.71 us
    reduce_scatter x1 -> x0, waiting for transfers between devices: 144 us -> none  [local(): lax.psum_scatter(lax.fori_loop(0, groups, one_group, start_totals), 'voca...]
    all_gather x1 -> x0, waiting for transfers between devices: 64 us -> none  [local(): every_eval = lax.all_gather(eval_tiles, 'corpus', axis=0, tiled=True)]
    gather x26 -> x0, local copies, waits for them, and re-layouts: 47.9 us -> none  [the longest x6 25.8 us: compute(): eval_part = every_eval[eval_index]]
    dot_general x12 -> x0, matrix products: 41.9 us -> none  [the longest x6 29.5 us: compute(): jnp.einsum('gij,gjrt->girt', matched.astype(jnp.bfloat16), corpus_part, p...]
    ppermute x0 -> x19, starting transfers between devices: none -> 20.3 us  [the longest x3 8.09 us: few_items(): moved = lax.ppermute(held, 'corpus', along)]
    ppermute x0 -> x19, waiting for transfers between devices: none -> 20.1 us  [the longest x4 7.78 us: reduce(): total = chip + lax.ppermute(chip, 'vocab', to_chip)]
    pallas_call x0 -> x6, Pallas kernels: none -> 10.4 us  [the longest x4 7.29 us: dots(): pl.pallas_call(functools.partial(dots_kernel, tiles_in_slice(corpus_tiles...]
    reduce_or x12 -> x0, other arithmetic: 9.07 us -> none  [one_group(): return lax.cond(jnp.any(living), compute, lambda current: current, totals)]
  transfers between devices with their start and end apart: 2 -> 19, of which waited for: 2 -> 10; matrix products, arithmetic and copies ran while one was open for 1% -> 12% of each run, Pallas kernels for 0% -> 13%
where the time goes in v1:
time: 62.5 us; the launch traced here: 62.1 us
  starting transfers between devices  20.3 us (32%)
  waiting for transfers between devices  20.1 us (32%)
  Pallas kernels  10.4 us (17%)
  other arithmetic  5.71 us (9%)
  local copies, waits for them, and re-layouts  4.78 us (8%)
  between operations  0.87 us (1%)
    ppermute x3, starting transfers between devices, few_items(): moved = lax.ppermute(held, 'corpus', along)  8.09 us
    ppermute x4, waiting for transfers between devices, reduce(): total = chip + lax.ppermute(chip, 'vocab', to_chip)  7.78 us
    pallas_call x4, Pallas kernels, dots(): pl.pallas_call(functools.partial(dots_kernel, tiles_in_slice(corpus_tiles...  7.29 us
    ppermute x4, waiting for transfers between devices, few_items(): exchanged = lax.ppermute(held, 'corpus', across)  7.16 us
    ppermute x4, starting transfers between devices, reduce(): total = chip + lax.ppermute(chip, 'vocab', to_chip)  5.69 us
    ppermute x4, starting transfers between devices, few_items(): exchanged = lax.ppermute(held, 'corpus', across)  5.07 us
    ppermute x3, waiting for transfers between devices, few_items(): moved = lax.ppermute(held, 'corpus', along)  4.46 us
    unnamed x17, local copies, waits for them, and re-layouts  3.86 us
  transfers between devices with their start and end apart: 19, of which 10 were waited for; matrix products, arithmetic and copies ran while one was open for 12% of the time, Pallas kernels for 13%

profile of v1, /device:TPU:0, one launch (start us, length us, event | category | flops | bytes accessed | tf_op | source)
XLA Modules:
  0.0 62.1 jit_solution(7600608870377733184)
XLA Ops:
  0.0 4.0 %collective-permute-start = (bf16[1,3,128,512]{3,2,1,0:T(8,128)(2,1)}, bf16[1,3,128,512]{3,2,1,0:T(8,128)(2,1)S(1)}, u32[]{:S(2)}, u32[]{:S(2)}) collective-permute-start(bf16[1,3,128,512]{3,2,1,0:T(8,128)(2,1)} %refs_0_.1), channel_id=1, source_target_pairs={{0,16},{4,20},{16,24},{20,28},{24,8},{28,12},{8,0},{12,4},{1,17},{... | collective-permute-start | bytes 1179656 | tf_op jit(solution)/shard_map/ppermute | solution.py:248
  4.0 1.5 %collective-permute-start.1 = (bf16[1,3,128,512]{3,2,1,0:T(8,128)(2,1)}, bf16[1,3,128,512]{3,2,1,0:T(8,128)(2,1)S(1)}, u32[]{:S(2)}, u32[]{:S(2)}) collective-permute-start(bf16[1,3,128,512]{3,2,1,0:T(8,128)(2,1)} %refs_0_.1), channel_id=1, source_target_pairs={{0,4},{4,0},{8,12},{12,8},{16,20},{20,16},{24,28},{28,24},{1,5},{5... | collective-permute-start | bytes 1179656 | tf_op jit(solution)/shard_map/ppermute | solution.py:246
  5.6 1.3 %fusion.1 = s32[]{:T(128)} fusion(s32[4]{0:T(128)} %constant.86.clone, s32[]{:T(128)S(6)} %select_n.59), kind=kLoop, calls=%fused_computation.18 | loop fusion | flops 11 | bytes 24 | tf_op jit(solution)/shard_map/reduce_sum | solution.py:194
  6.8 0.8 %copy.24.eval_list_ref = s32[8,3]{1,0:T(8,128)S(1)} copy(s32[8,3]{0,1:T(4,128)} %param.13) | data formatting | bytes 192 | tf_op args[1]
  7.6 1.3 %and_select_fusion.1 = s32[8]{0:T(128)S(1)} fusion(s32[8]{0:T(128)} %constant.94, s32[]{:T(128)} %fusion.1), kind=kLoop, calls=%fused_computation.11 | loop fusion | flops 104 | bytes 68 | tf_op jit(solution)/shard_map/jit(remainder)/select_n | solution.py:197
  8.9 0.7 %select_reduce_fusion.3 = s32[8]{0:T(128)S(1)} fusion(s32[4]{0:T(128)} %constant.86.clone, s32[8]{0:T(128)S(1)} %and_select_fusion.1), kind=kLoop, calls=%fused_computation.7 | loop fusion | flops 88 | bytes 80 | tf_op jit(solution)/shard_map/reduce_sum | solution.py:198
  9.7 3.1 %collective-permute-done.refs_1_ = bf16[1,3,128,512]{3,2,1,0:T(8,128)(2,1)S(1)} collective-permute-done((bf16[1,3,128,512]{3,2,1,0:T(8,128)(2,1)}, bf16[1,3,128,512]{3,2,1,0:T(8,128)(2,1)S(1)}, u32[]{:S(2)}, u32[]{:S(2)}) %collective-permute-start) | collective-permute-done | bytes 393248 | tf_op jit(solution)/shard_map/ppermute | solution.py:248
  12.7 2.1 %collective-permute-done.1.refs_2_ = bf16[1,3,128,512]{3,2,1,0:T(8,128)(2,1)S(1)} collective-permute-done((bf16[1,3,128,512]{3,2,1,0:T(8,128)(2,1)}, bf16[1,3,128,512]{3,2,1,0:T(8,128)(2,1)S(1)}, u32[]{:S(2)}, u32[]{:S(2)}) %collective-permute-start.1) | collective-permute-done | bytes 393248 | tf_op jit(solution)/shard_map/ppermute | solution.py:246
  14.8 1.5 %collective-permute-start.6 = (bf16[1,3,128,512]{3,2,1,0:T(8,128)(2,1)S(1)}, bf16[1,3,128,512]{3,2,1,0:T(8,128)(2,1)S(1)}, u32[]{:S(2)}, u32[]{:S(2)}) collective-permute-start(bf16[1,3,128,512]{3,2,1,0:T(8,128)(2,1)S(1)} %collective-permute-done.refs_1_), channel_id=1, source_target_pairs={{0,4},{4,0},{8,12},{12,8},{16,20},{20,16},{24,28},{28,24},{1,5},{5... | collective-permute-start | bytes 1179656 | tf_op jit(solution)/shard_map/ppermute | solution.py:246
  16.3 1.6 %collective-permute-start.5 = (bf16[1,3,128,512]{3,2,1,0:T(8,128)(2,1)S(1)}, bf16[1,3,128,512]{3,2,1,0:T(8,128)(2,1)S(1)}, u32[]{:S(2)}, u32[]{:S(2)}) collective-permute-start(bf16[1,3,128,512]{3,2,1,0:T(8,128)(2,1)S(1)} %collective-permute-done.refs_1_), channel_id=1, source_target_pairs={{0,16},{4,20},{16,24},{20,28},{24,8},{28,12},{8,0},{12,4},{1,17},{... | collective-permute-start | bytes 1179656 | tf_op jit(solution)/shard_map/ppermute | solution.py:248
  17.9 0.7 %xor_add_fusion = s32[8]{0:T(128)S(1)} fusion(s32[8]{0:T(128)} %constant.88.clone, s32[8]{0:T(128)S(1)} %select_reduce_fusion.3, s32[]{:T(128)S(6)} %select_n.63), kind=kLoop, calls=%fused_computation.22 | loop fusion | flops 24 | bytes 100 | tf_op jit(solution)/shard_map/add | solution.py:199
  18.6 0.1 pad_add_fusion.place_ref
  18.7 1.4 %copy-done = bf16[4,3,128,512]{3,2,1,0:T(8,128)(2,1)S(1)} copy-done((bf16[4,3,128,512]{3,2,1,0:T(8,128)(2,1)S(1)}, bf16[4,3,128,512]{3,2,1,0:T(8,128)(2,1)}, u32[]{:S(2)}) %copy-start) | copy-done | bytes 1572888
  20.1 1.0 %copy-done.2 = bf16[1,3,128,512]{3,2,1,0:T(8,128)(2,1)S(1)} copy-done((bf16[1,3,128,512]{3,2,1,0:T(8,128)(2,1)S(1)}, bf16[1,3,128,512]{3,2,1,0:T(8,128)(2,1)}, u32[]{:S(2)}) %copy-start.2) | copy-done | bytes 393240
  21.1 0.7 %copy-done.3 = s32[4,3]{1,0:T(4,128)S(1)} copy-done((s32[4,3]{1,0:T(4,128)S(1)}, s32[4,3]{1,0:T(4,128)}, u32[]{:S(2)}) %copy-start.3) | copy-done | bytes 72
  21.7 2.8 %shard_map.119 = (f32[6,128,128]{2,1,0:T(8,128)S(1)}, f32[6,128,128]{2,1,0:T(8,128)}) custom-call(s32[9]{0:T(128)S(1)} %pad_add_fusion.place_ref, s32[8,3]{1,0:T(8,128)S(1)} %copy.24.eval_list_ref, s32[4,3]{1,0:T(4,128)S(1)} %copy-done.3, bf16[1,3,128,512]{3,2,1,0:T(8,128)(2,1)S(1)} %copy-done.2, bf16[1,3,128,512]{3,2,1,0:T(8,128)(2,1)S(1)} %collective-permute-done.refs_1_, ...), custom_call_target="tpu_custom_call" | custom-call | flops 603979776 | bytes 2752512 | tf_op jit(solution)/shard_map/pallas_call | solution.py:117
  24.6 1.2 %collective-permute-done.5.refs_0_ = bf16[1,3,128,512]{3,2,1,0:T(8,128)(2,1)S(1)} collective-permute-done((bf16[1,3,128,512]{3,2,1,0:T(8,128)(2,1)S(1)}, bf16[1,3,128,512]{3,2,1,0:T(8,128)(2,1)S(1)}, u32[]{:S(2)}, u32[]{:S(2)}) %collective-permute-start.5) | collective-permute-done | bytes 393248 | tf_op jit(solution)/shard_map/ppermute | solution.py:248
  25.7 0.5 collective-permute-start.11
  26.2 2.5 %collective-permute-start.10 = (bf16[1,3,128,512]{3,2,1,0:T(8,128)(2,1)S(1)}, bf16[1,3,128,512]{3,2,1,0:T(8,128)(2,1)S(1)}, u32[]{:S(2)}, u32[]{:S(2)}) collective-permute-start(bf16[1,3,128,512]{3,2,1,0:T(8,128)(2,1)S(1)} %collective-permute-done.5.refs_0_), channel_id=1, source_target_pairs={{0,16},{4,20},{16,24},{20,28},{24,8},{28,12},{8,0},{12,4},{1,17},{... | collective-permute-start | bytes 1179656 | tf_op jit(solution)/shard_map/ppermute | solution.py:248
  28.7 0.7 %dynamic_slice.7 = s32[24]{0:T(128)S(1)} dynamic-slice(s32[96]{0:T(128)} %param.16, s32[]{:T(128)S(6)} %select_n.56), dynamic_slice_sizes={24} | dynamic-slice | bytes 196 | tf_op jit(solution)/shard_map/dynamic_slice | solution.py:203
  29.4 1.0 %add.78 = f32[6,128,128]{2,1,0:T(8,128)S(1)} add(f32[6,128,128]{2,1,0:T(8,128)S(1)} %get-tuple-element.21, f32[6,128,128]{2,1,0:T(8,128)} %collective-permute-done.2) | non-fusion elementwise | flops 98304 | bytes 1179648 | tf_op jit(solution)/shard_map/add | solution.py:238
  30.5 1.6 %collective-permute-start.3 = (f32[6,128,128]{2,1,0:T(8,128)S(1)}, f32[6,128,128]{2,1,0:T(8,128)S(1)}, u32[]{:S(2)}, u32[]{:S(2)}) collective-permute-start(f32[6,128,128]{2,1,0:T(8,128)S(1)} %add.78), channel_id=1, source_target_pairs={{0,2},{1,3},{2,0},{3,1},{4,6},{5,7},{6,4},{7,5},{8,10},{9,11},{10,... | collective-permute-start | bytes 1179656 | tf_op jit(solution)/shard_map/ppermute | solution.py:239
  32.0 4.1 %collective-permute-done.11.refs_1_ = bf16[1,3,128,512]{3,2,1,0:T(8,128)(2,1)S(1)} collective-permute-done((bf16[1,3,128,512]{3,2,1,0:T(8,128)(2,1)S(1)}, bf16[1,3,128,512]{3,2,1,0:T(8,128)(2,1)S(1)}, u32[]{:S(2)}, u32[]{:S(2)}) %collective-permute-start.11) | collective-permute-done | bytes 393248 | tf_op jit(solution)/shard_map/ppermute | solution.py:246
  36.1 0.2 collective-permute-done.10.refs_0_
  36.3 1.5 %collective-permute-start.15 = (bf16[1,3,128,512]{3,2,1,0:T(8,128)(2,1)S(1)}, bf16[1,3,128,512]{3,2,1,0:T(8,128)(2,1)S(1)}, u32[]{:S(2)}, u32[]{:S(2)}) collective-permute-start(bf16[1,3,128,512]{3,2,1,0:T(8,128)(2,1)S(1)} %collective-permute-done.10.refs_0_), channel_id=1, source_target_pairs={{0,4},{4,0},{8,12},{12,8},{16,20},{20,16},{24,28},{28,24},{1,5},{5... | collective-permute-start | bytes 1179656 | tf_op jit(solution)/shard_map/ppermute | solution.py:246
  37.8 1.6 %shard_map.120 = (f32[4,128,128]{2,1,0:T(8,128)S(1)}, f32[4,128,128]{2,1,0:T(8,128)S(1)}) custom-call(s32[9]{0:T(128)S(1)} %pad_add_fusion.place_ref, s32[8,3]{1,0:T(8,128)S(1)} %copy.24.eval_list_ref, s32[4,3]{1,0:T(4,128)S(1)} %copy-done.4, bf16[1,3,128,512]{3,2,1,0:T(8,128)(2,1)S(1)} %collective-permute-done.5.refs_0_, ...), custom_call_target="tpu_custom_call" | custom-call | flops 402653184 | bytes 2359296 | tf_op jit(solution)/shard_map/pallas_call | solution.py:117
  39.5 0.1 collective-permute-start.7
  39.6 1.6 %shard_map.121 = (f32[4,128,128]{2,1,0:T(8,128)S(1)}, f32[4,128,128]{2,1,0:T(8,128)S(1)}) custom-call(s32[9]{0:T(128)S(1)} %pad_add_fusion.place_ref, s32[8,3]{1,0:T(8,128)S(1)} %copy.24.eval_list_ref, s32[4,3]{1,0:T(4,128)S(1)} %copy-done.4, bf16[1,3,128,512]{3,2,1,0:T(8,128)(2,1)S(1)} %collective-permute-done.10.refs_0_, ...), custom_call_target="tpu_custom_call" | custom-call | flops 402653184 | bytes 2359296 | tf_op jit(solution)/shard_map/pallas_call | solution.py:117
  41.2 0.6 collective-permute-start.12
  41.8 0.1 select_reduce_fusion.2
  41.9 1.6 %collective-permute-start.8 = (f32[4,128,128]{2,1,0:T(8,128)S(1)}, f32[4,128,128]{2,1,0:T(8,128)S(1)}, u32[]{:S(2)}, u32[]{:S(2)}) collective-permute-start(f32[4,128,128]{2,1,0:T(8,128)S(1)} %add.80), channel_id=1, source_target_pairs={{0,2},{1,3},{2,0},{3,1},{4,6},{5,7},{6,4},{7,5},{8,10},{9,11},{10,... | collective-permute-start | bytes 786440 | tf_op jit(solution)/shard_map/ppermute | solution.py:239
  43.5 1.0 %collective-permute-start.13 = (f32[4,128,128]{2,1,0:T(8,128)S(1)}, f32[4,128,128]{2,1,0:T(8,128)S(1)}, u32[]{:S(2)}, u32[]{:S(2)}) collective-permute-start(f32[4,128,128]{2,1,0:T(8,128)S(1)} %add.82), channel_id=1, source_target_pairs={{0,2},{1,3},{2,0},{3,1},{4,6},{5,7},{6,4},{7,5},{8,10},{9,11},{10,... | collective-permute-start | bytes 786440 | tf_op jit(solution)/shard_map/ppermute | solution.py:239
  44.5 1.0 %collective-permute-done.15.refs_0_ = bf16[1,3,128,512]{3,2,1,0:T(8,128)(2,1)S(1)} collective-permute-done((bf16[1,3,128,512]{3,2,1,0:T(8,128)(2,1)S(1)}, bf16[1,3,128,512]{3,2,1,0:T(8,128)(2,1)S(1)}, u32[]{:S(2)}, u32[]{:S(2)}) %collective-permute-start.15) | collective-permute-done | bytes 393248 | tf_op jit(solution)/shard_map/ppermute | solution.py:246
  45.5 1.2 %shard_map.122 = (f32[2,128,128]{2,1,0:T(8,128)S(1)}, f32[2,128,128]{2,1,0:T(8,128)S(1)}) custom-call(s32[9]{0:T(128)S(1)} %pad_add_fusion.place_ref, s32[8,3]{1,0:T(8,128)S(1)} %copy.24.eval_list_ref, s32[4,3]{1,0:T(4,128)S(1)} %copy-done.4, bf16[1,3,128,512]{3,2,1,0:T(8,128)(2,1)S(1)} %collective-permute-done.15.refs_0_, bf16[4,3,128,512]{3,2,1,0:T(8,128)(2,1)S(1)} %copy-done.1), custom_call_target="tpu_custom_call" | custom-call | flops 201326592 | bytes 1966080 | tf_op jit(solution)/shard_map/pallas_call | solution.py:117
  46.8 0.1 collective-permute-start.16
  46.9 0.1 fusion
  47.0 0.5 collective-permute-start.4
  47.6 0.6 collective-permute-done.16
  48.2 1.6 %collective-permute-start.17 = (f32[2,128,128]{2,1,0:T(8,128)S(1)}, f32[2,128,128]{2,1,0:T(8,128)S(1)}, u32[]{:S(2)}, u32[]{:S(2)}) collective-permute-start(f32[2,128,128]{2,1,0:T(8,128)S(1)} %add.84), channel_id=1, source_target_pairs={{0,2},{1,3},{2,0},{3,1},{4,6},{5,7},{6,4},{7,5},{8,10},{9,11},{10,... | collective-permute-start | bytes 393224 | tf_op jit(solution)/shard_map/ppermute | solution.py:239
  49.8 0.1 copy.22
  49.9 1.3 %collective-permute-done.8 = f32[4,128,128]{2,1,0:T(8,128)S(1)} collective-permute-done((f32[4,128,128]{2,1,0:T(8,128)S(1)}, f32[4,128,128]{2,1,0:T(8,128)S(1)}, u32[]{:S(2)}, u32[]{:S(2)}) %collective-permute-start.8) | collective-permute-done | bytes 262176 | tf_op jit(solution)/shard_map/ppermute | solution.py:239
  51.3 5.5 %collective-permute-done.13 = f32[4,128,128]{2,1,0:T(8,128)S(1)} collective-permute-done((f32[4,128,128]{2,1,0:T(8,128)S(1)}, f32[4,128,128]{2,1,0:T(8,128)S(1)}, u32[]{:S(2)}, u32[]{:S(2)}) %collective-permute-start.13) | collective-permute-done | bytes 262176 | tf_op jit(solution)/shard_map/ppermute | solution.py:239
  56.9 0.1 select_reduce_fusion
  57.6 1.0 %collective-permute-done.17 = f32[2,128,128]{2,1,0:T(8,128)S(1)} collective-permute-done((f32[2,128,128]{2,1,0:T(8,128)S(1)}, f32[2,128,128]{2,1,0:T(8,128)S(1)}, u32[]{:S(2)}, u32[]{:S(2)}) %collective-permute-start.17) | collective-permute-done | bytes 131104 | tf_op jit(solution)/shard_map/ppermute | solution.py:239
  58.7 0.1 copy.23.eval_ref
  58.9 0.1 select_reduce_fusion.1.corpus_ref
  58.9 1.0 %shard_map.118.scale_ref = f32[24,128,128]{2,1,0:T(8,128)S(1)} custom-call(f32[128,24]{1,0:T(8,128)S(1)} %copy.23.eval_ref, f32[24,128]{1,0:T(8,128)S(1)} %select_reduce_fusion.1.corpus_ref, s32[24]{0:T(128)S(1)} %compare_convert_fusion.live_ref), custom_call_target="tpu_custom_call" | custom-call | tf_op jit(solution)/shard_map/pallas_call | solution.py:227
  60.1 2.1 %shard_map.123 = f32[24,128,128]{2,1,0:T(8,128)} custom-call(s32[24]{0:T(128)S(1)} %get-tuple-element.33.item_ref, f32[24,128,128]{2,1,0:T(8,128)S(1)} %shard_map.118.scale_ref, f32[6,128,128]{2,1,0:T(8,128)S(1)} %add.79.refs_0_, f32[6,128,128]{2,1,0:T(8,128)S(1)} %collective-permute-done.4.refs_1_, f32[4,128,128]{2,1,0:T(8,128)S(1)} %add.81.refs_2_, ...), custom_call_target="tpu_custom_call" | custom-call | tf_op jit(solution)/shard_map/pallas_call | solution.py:259
  (36 shorter events, 0.5 us)
Async XLA Ops:
  0.0 12.7 %collective-permute-start = (bf16[1,3,128,512]{3,2,1,0:T(8,128)(2,1)}, bf16[1,3,128,512]{3,2,1,0:T(8,128)(2,1)S(1)}, u32[]{:S(2)}, u32[]{:S(2)}) collective-permute-start(bf16[1,3,128,512]{3,2,1,0:T(8,128)(2,1)} %refs_0_.1), channel_id=1, source_target_pairs={{0,16},{4,20},{16,24},{20,28},{24,8},{28,12},{8,0},{12,4},{1,17},{... | collective-permute-start | bytes 1179656 | tf_op jit(solution)/shard_map/ppermute | solution.py:248
  4.0 10.8 %collective-permute-start.1 = (bf16[1,3,128,512]{3,2,1,0:T(8,128)(2,1)}, bf16[1,3,128,512]{3,2,1,0:T(8,128)(2,1)S(1)}, u32[]{:S(2)}, u32[]{:S(2)}) collective-permute-start(bf16[1,3,128,512]{3,2,1,0:T(8,128)(2,1)} %refs_0_.1), channel_id=1, source_target_pairs={{0,4},{4,0},{8,12},{12,8},{16,20},{20,16},{24,28},{28,24},{1,5},{5... | collective-permute-start | bytes 1179656 | tf_op jit(solution)/shard_map/ppermute | solution.py:246
  14.8 9.7 %collective-permute-start.6 = (bf16[1,3,128,512]{3,2,1,0:T(8,128)(2,1)S(1)}, bf16[1,3,128,512]{3,2,1,0:T(8,128)(2,1)S(1)}, u32[]{:S(2)}, u32[]{:S(2)}) collective-permute-start(bf16[1,3,128,512]{3,2,1,0:T(8,128)(2,1)S(1)} %collective-permute-done.refs_1_), channel_id=1, source_target_pairs={{0,4},{4,0},{8,12},{12,8},{16,20},{20,16},{24,28},{28,24},{1,5},{5... | collective-permute-start | bytes 1179656 | tf_op jit(solution)/shard_map/ppermute | solution.py:246
  16.3 9.4 %collective-permute-start.5 = (bf16[1,3,128,512]{3,2,1,0:T(8,128)(2,1)S(1)}, bf16[1,3,128,512]{3,2,1,0:T(8,128)(2,1)S(1)}, u32[]{:S(2)}, u32[]{:S(2)}) collective-permute-start(bf16[1,3,128,512]{3,2,1,0:T(8,128)(2,1)S(1)} %collective-permute-done.refs_1_), channel_id=1, source_target_pairs={{0,16},{4,20},{16,24},{20,28},{24,8},{28,12},{8,0},{12,4},{1,17},{... | collective-permute-start | bytes 1179656 | tf_op jit(solution)/shard_map/ppermute | solution.py:248
  18.7 1.4 %copy-start = (bf16[4,3,128,512]{3,2,1,0:T(8,128)(2,1)S(1)}, bf16[4,3,128,512]{3,2,1,0:T(8,128)(2,1)}, u32[]{:S(2)}) copy-start(bf16[4,3,128,512]{3,2,1,0:T(8,128)(2,1)} %refs_1_.1) | copy-start | bytes 4718596
  20.1 1.0 %copy-start.2 = (bf16[1,3,128,512]{3,2,1,0:T(8,128)(2,1)S(1)}, bf16[1,3,128,512]{3,2,1,0:T(8,128)(2,1)}, u32[]{:S(2)}) copy-start(bf16[1,3,128,512]{3,2,1,0:T(8,128)(2,1)} %refs_0_.1) | copy-start | bytes 1179652
  21.1 0.7 %copy-start.3 = (s32[4,3]{1,0:T(4,128)S(1)}, s32[4,3]{1,0:T(4,128)}, u32[]{:S(2)}) copy-start(s32[4,3]{1,0:T(4,128)} %corpus_list_ref.7) | copy-start | bytes 148
  21.7 16.1 %copy-start.1 = (bf16[4,3,128,512]{3,2,1,0:T(8,128)(2,1)S(1)}, bf16[4,3,128,512]{3,2,1,0:T(8,128)(2,1)}, u32[]{:S(2)}) copy-start(bf16[4,3,128,512]{3,2,1,0:T(8,128)(2,1)} %refs_1_.1) | copy-start | bytes 4718596
  21.7 16.1 %copy-start.4 = (s32[4,3]{1,0:T(4,128)S(1)}, s32[4,3]{1,0:T(4,128)}, u32[]{:S(2)}) copy-start(s32[4,3]{1,0:T(4,128)} %corpus_list_ref.7) | copy-start | bytes 148
  24.6 4.9 %collective-permute-start.2 = (f32[6,128,128]{2,1,0:T(8,128)}, f32[6,128,128]{2,1,0:T(8,128)}, u32[]{:S(2)}, u32[]{:S(2)}) collective-permute-start(f32[6,128,128]{2,1,0:T(8,128)} %get-tuple-element.22), channel_id=1, source_target_pairs={{0,1},{1,0},{2,3},{3,2},{4,5},{5,4},{6,7},{7,6},{8,9},{9,8},{10,11... | collective-permute-start | bytes 1179656 | tf_op jit(solution)/shard_map/ppermute | solution.py:238
  25.7 10.4 %collective-permute-start.11 = (bf16[1,3,128,512]{3,2,1,0:T(8,128)(2,1)S(1)}, bf16[1,3,128,512]{3,2,1,0:T(8,128)(2,1)S(1)}, u32[]{:S(2)}, u32[]{:S(2)}) collective-permute-start(bf16[1,3,128,512]{3,2,1,0:T(8,128)(2,1)S(1)} %collective-permute-done.5.refs_0_), channel_id=1, source_target_pairs={{0,4},{4,0},{8,12},{12,8},{16,20},{20,16},{24,28},{28,24},{1,5},{5... | collective-permute-start | bytes 1179656 | tf_op jit(solution)/shard_map/ppermute | solution.py:246
  26.2 10.1 %collective-permute-start.10 = (bf16[1,3,128,512]{3,2,1,0:T(8,128)(2,1)S(1)}, bf16[1,3,128,512]{3,2,1,0:T(8,128)(2,1)S(1)}, u32[]{:S(2)}, u32[]{:S(2)}) collective-permute-start(bf16[1,3,128,512]{3,2,1,0:T(8,128)(2,1)S(1)} %collective-permute-done.5.refs_0_), channel_id=1, source_target_pairs={{0,16},{4,20},{16,24},{20,28},{24,8},{28,12},{8,0},{12,4},{1,17},{... | collective-permute-start | bytes 1179656 | tf_op jit(solution)/shard_map/ppermute | solution.py:248
  30.5 16.5 %collective-permute-start.3 = (f32[6,128,128]{2,1,0:T(8,128)S(1)}, f32[6,128,128]{2,1,0:T(8,128)S(1)}, u32[]{:S(2)}, u32[]{:S(2)}) collective-permute-start(f32[6,128,128]{2,1,0:T(8,128)S(1)} %add.78), channel_id=1, source_target_pairs={{0,2},{1,3},{2,0},{3,1},{4,6},{5,7},{6,4},{7,5},{8,10},{9,11},{10,... | collective-permute-start | bytes 1179656 | tf_op jit(solution)/shard_map/ppermute | solution.py:239
  36.3 9.2 %collective-permute-start.15 = (bf16[1,3,128,512]{3,2,1,0:T(8,128)(2,1)S(1)}, bf16[1,3,128,512]{3,2,1,0:T(8,128)(2,1)S(1)}, u32[]{:S(2)}, u32[]{:S(2)}) collective-permute-start(bf16[1,3,128,512]{3,2,1,0:T(8,128)(2,1)S(1)} %collective-permute-done.10.refs_0_), channel_id=1, source_target_pairs={{0,4},{4,0},{8,12},{12,8},{16,20},{20,16},{24,28},{28,24},{1,5},{5... | collective-permute-start | bytes 1179656 | tf_op jit(solution)/shard_map/ppermute | solution.py:246
  39.5 2.4 %collective-permute-start.7 = (f32[4,128,128]{2,1,0:T(8,128)S(1)}, f32[4,128,128]{2,1,0:T(8,128)S(1)}, u32[]{:S(2)}, u32[]{:S(2)}) collective-permute-start(f32[4,128,128]{2,1,0:T(8,128)S(1)} %get-tuple-element.26), channel_id=1, source_target_pairs={{0,1},{1,0},{2,3},{3,2},{4,5},{5,4},{6,7},{7,6},{8,9},{9,8},{10,11... | collective-permute-start | bytes 786440 | tf_op jit(solution)/shard_map/ppermute | solution.py:238
  41.2 2.3 %collective-permute-start.12 = (f32[4,128,128]{2,1,0:T(8,128)S(1)}, f32[4,128,128]{2,1,0:T(8,128)S(1)}, u32[]{:S(2)}, u32[]{:S(2)}) collective-permute-start(f32[4,128,128]{2,1,0:T(8,128)S(1)} %get-tuple-element.30), channel_id=1, source_target_pairs={{0,1},{1,0},{2,3},{3,2},{4,5},{5,4},{6,7},{7,6},{8,9},{9,8},{10,11... | collective-permute-start | bytes 786440 | tf_op jit(solution)/shard_map/ppermute | solution.py:238
  41.9 5.0 %copy-start.7 = (s32[96]{0:T(128)S(1)}, s32[96]{0:T(128)}, u32[]{:S(2)}) copy-start(s32[96]{0:T(128)} %param.17) | copy-start | bytes 1156
  41.9 9.2 %collective-permute-start.8 = (f32[4,128,128]{2,1,0:T(8,128)S(1)}, f32[4,128,128]{2,1,0:T(8,128)S(1)}, u32[]{:S(2)}, u32[]{:S(2)}) collective-permute-start(f32[4,128,128]{2,1,0:T(8,128)S(1)} %add.80), channel_id=1, source_target_pairs={{0,2},{1,3},{2,0},{3,1},{4,6},{5,7},{6,4},{7,5},{8,10},{9,11},{10,... | collective-permute-start | bytes 786440 | tf_op jit(solution)/shard_map/ppermute | solution.py:239
  43.5 13.3 %collective-permute-start.13 = (f32[4,128,128]{2,1,0:T(8,128)S(1)}, f32[4,128,128]{2,1,0:T(8,128)S(1)}, u32[]{:S(2)}, u32[]{:S(2)}) collective-permute-start(f32[4,128,128]{2,1,0:T(8,128)S(1)} %add.82), channel_id=1, source_target_pairs={{0,2},{1,3},{2,0},{3,1},{4,6},{5,7},{6,4},{7,5},{8,10},{9,11},{10,... | collective-permute-start | bytes 786440 | tf_op jit(solution)/shard_map/ppermute | solution.py:239
  46.8 1.4 %collective-permute-start.16 = (f32[2,128,128]{2,1,0:T(8,128)S(1)}, f32[2,128,128]{2,1,0:T(8,128)S(1)}, u32[]{:S(2)}, u32[]{:S(2)}) collective-permute-start(f32[2,128,128]{2,1,0:T(8,128)S(1)} %get-tuple-element.32), channel_id=1, source_target_pairs={{0,1},{1,0},{2,3},{3,2},{4,5},{5,4},{6,7},{7,6},{8,9},{9,8},{10,11... | collective-permute-start | bytes 393224 | tf_op jit(solution)/shard_map/ppermute | solution.py:238
  47.0 9.9 %copy-start.5 = (f32[1024]{0:T(1024)S(1)}, f32[1024]{0:T(1024)}, u32[]{:S(2)}) copy-start(f32[1024]{0:T(1024)} %param.19) | copy-start | bytes 12292
  47.0 11.9 %copy-start.6 = (f32[512]{0:T(512)S(1)}, f32[512]{0:T(512)}, u32[]{:S(2)}) copy-start(f32[512]{0:T(512)} %param.20) | copy-start | bytes 6148
  47.0 13.0 %collective-permute-start.4 = (f32[6,128,128]{2,1,0:T(8,128)S(1)}, f32[6,128,128]{2,1,0:T(8,128)S(1)}, u32[]{:S(2)}, u32[]{:S(2)}) collective-permute-start(f32[6,128,128]{2,1,0:T(8,128)S(1)} %add.79.refs_0_), channel_id=1, source_target_pairs={{0,1},{1,0},{2,3},{3,2},{4,5},{5,4},{6,7},{7,6},{8,9},{9,8},{10,11... | collective-permute-start | bytes 1179656 | tf_op jit(solution)/shard_map/ppermute | solution.py:240
  48.2 10.4 %collective-permute-start.17 = (f32[2,128,128]{2,1,0:T(8,128)S(1)}, f32[2,128,128]{2,1,0:T(8,128)S(1)}, u32[]{:S(2)}, u32[]{:S(2)}) collective-permute-start(f32[2,128,128]{2,1,0:T(8,128)S(1)} %add.84), channel_id=1, source_target_pairs={{0,2},{1,3},{2,0},{3,1},{4,6},{5,7},{6,4},{7,5},{8,10},{9,11},{10,... | collective-permute-start | bytes 393224 | tf_op jit(solution)/shard_map/ppermute | solution.py:239
  51.2 8.8 %collective-permute-start.9 = (f32[4,128,128]{2,1,0:T(8,128)S(1)}, f32[4,128,128]{2,1,0:T(8,128)S(1)}, u32[]{:S(2)}, u32[]{:S(2)}) collective-permute-start(f32[4,128,128]{2,1,0:T(8,128)S(1)} %add.81.refs_2_), channel_id=1, source_target_pairs={{0,1},{1,0},{2,3},{3,2},{4,5},{5,4},{6,7},{7,6},{8,9},{9,8},{10,11... | collective-permute-start | bytes 786440 | tf_op jit(solution)/shard_map/ppermute | solution.py:240
  56.8 3.2 %collective-permute-start.14 = (f32[4,128,128]{2,1,0:T(8,128)S(1)}, f32[4,128,128]{2,1,0:T(8,128)S(1)}, u32[]{:S(2)}, u32[]{:S(2)}) collective-permute-start(f32[4,128,128]{2,1,0:T(8,128)S(1)} %add.83.refs_4_), channel_id=1, source_target_pairs={{0,1},{1,0},{2,3},{3,2},{4,5},{5,4},{6,7},{7,6},{8,9},{9,8},{10,11... | collective-permute-start | bytes 786440 | tf_op jit(solution)/shard_map/ppermute | solution.py:240
  58.7 1.4 %collective-permute-start.18 = (f32[2,128,128]{2,1,0:T(8,128)S(1)}, f32[2,128,128]{2,1,0:T(8,128)S(1)}, u32[]{:S(2)}, u32[]{:S(2)}) collective-permute-start(f32[2,128,128]{2,1,0:T(8,128)S(1)} %add.85.refs_6_), channel_id=1, source_target_pairs={{0,1},{1,0},{2,3},{3,2},{4,5},{5,4},{6,7},{7,6},{8,9},{9,8},{10,11... | collective-permute-start | bytes 393224 | tf_op jit(solution)/shard_map/ppermute | solution.py:240

commit v2 on v0

--- a/solution.py
+++ b/solution.py
@@ -1,13 +1,26 @@
+import functools
+
 import jax
 import jax.numpy as jnp
 from jax import lax
+from jax.experimental import pallas as pl
+from jax.experimental.pallas import tpu as pltpu
 from jax.sharding import PartitionSpec as P
 
 VOCAB = 262144
 GROUP = 8
-
-
-def local(
+VMEM = pl.BlockSpec(memory_space=pltpu.VMEM)
+SMEM = pl.BlockSpec(memory_space=pltpu.SMEM)
+LIMIT = 24 * 1024 * 1024
+TOP = 32767.0
+SCALE_ROWS = 16
+
+
+def tiles_in_slice(corpus_tiles):
+    return VOCAB // (corpus_tiles.shape[3] * lax.axis_size("vocab"))
+
+
+def general(
     eval_tiles,
     eval_tile_list,
     corpus_tiles,
@@ -19,15 +32,14 @@
     corpus_norm,
 ):
     slices = lax.axis_size("vocab")
-    term_width = corpus_tiles.shape[3]
     tile_rows = corpus_tiles.shape[2]
-    tiles_slice = VOCAB // (term_width * slices)
+    tiles_slice = tiles_in_slice(corpus_tiles)
     pair_slots = pair_eval_block.shape[0]
     quarter = pair_slots // slices
     every_eval = lax.all_gather(eval_tiles, "corpus", axis=0, tiled=True)
     position = jnp.arange(pair_slots, dtype=jnp.int32)
     own_live = position < pair_count[0]
-    groups = quarter * lax.axis_size("vocab") // GROUP
+    groups = pair_slots // GROUP
 
     def one_group(group_index, totals):
         first_slot = group_index * GROUP
@@ -53,16 +65,15 @@
                 "girt,gist->grs", eval_part, aligned, preferred_element_type=jnp.float32
             )
             products = jnp.where(living[:, None, None], products, 0.0)
-            return lax.dynamic_update_slice_in_dim(current, products, group_index * GROUP, 0)
+            return lax.dynamic_update_slice_in_dim(current, products, first_slot, 0)
 
         return lax.cond(jnp.any(living), compute, lambda current: current, totals)
 
-    start_totals = jnp.zeros((quarter * lax.axis_size("vocab"), tile_rows, tile_rows), jnp.float32)
+    start_totals = jnp.zeros((pair_slots, tile_rows, tile_rows), jnp.float32)
     summed = lax.psum_scatter(
         lax.fori_loop(0, groups, one_group, start_totals), "vocab", scatter_dimension=0, tiled=True
     )
-    vocab_index = lax.axis_index("vocab")
-    first_pair = vocab_index * quarter
+    first_pair = lax.axis_index("vocab") * quarter
     mine_eval = lax.dynamic_slice_in_dim(pair_eval_block, first_pair, quarter)
     mine_block = lax.dynamic_slice_in_dim(pair_corpus_block, first_pair, quarter)
     mine_live = lax.dynamic_slice_in_dim(own_live, first_pair, quarter)
@@ -70,6 +81,317 @@
     corpus_scale = corpus_norm.reshape(-1, tile_rows)[mine_block]
     cosine = summed / (eval_scale[:, :, None] * corpus_scale[:, None, :])
     return jnp.where(mine_live[:, None, None], cosine, 0.0)
+
+
+def ring_of(shards):
+    return list(range(0, shards, 2)) + list(range(1, shards, 2))[::-1]
+
+
+def look_up(values, at):
+    found = jnp.int32(0)
+    for n, value in enumerate(values):
+        found = jnp.where(at == n, jnp.int32(value), found)
+    return found
+
+
+def ring_place(shards):
+    ring = ring_of(shards)
+    core = lax.axis_index("vocab") % 2
+    return look_up([ring.index(c) for c in range(shards)], lax.axis_index("corpus")), 2 * core - 1, core
+
+
+def encode(tiles, code_ref):
+    rows = tiles[0].shape[0]
+    scales = []
+    for q, tile in enumerate(tiles):
+        scale = jnp.maximum(jnp.ceil(jnp.max(tile, axis=0, keepdims=True) * 2.0), 1.0)
+        scales.append(scale)
+        whole = jnp.floor(tile * (TOP * 2.0 / scale) + 0.5)
+        code_ref[q * rows : (q + 1) * rows] = jnp.minimum(whole, TOP).astype(jnp.int32).astype(jnp.int16)
+    scales.append(jnp.zeros((SCALE_ROWS - len(scales), rows), jnp.float32))
+    code_ref[len(tiles) * rows :] = jnp.concatenate(scales, axis=0).astype(jnp.int32).astype(jnp.int16)
+
+
+def decode(code_ref):
+    rows = code_ref.shape[1]
+    count = code_ref.shape[0] // rows
+    scales = code_ref[count * rows :].astype(jnp.int32).astype(jnp.float32) * (0.5 / TOP)
+    for q in range(count):
+        whole = code_ref[q * rows : (q + 1) * rows].astype(jnp.int32).astype(jnp.float32)
+        yield whole * scales[q : q + 1]
+
+
+def code_shape(count, rows):
+    return jax.ShapeDtypeStruct((count * rows + SCALE_ROWS, rows), jnp.int16)
+
+
+def dots_kernel(tiles_slice, step, halved, carried, coded, *refs):
+    outs = len(halved) + coded
+    sources = [refs[4 * n : 4 * n + 4] for n in range((len(refs) - outs - carried) // 4)]
+    carried_refs = refs[4 * len(sources) : len(refs) - outs]
+    out_refs = refs[len(refs) - outs :]
+    slots, shards = sources[0][2].shape
+    ring = ring_of(shards)
+    place, way, core = ring_place(shards)
+    e = look_up(ring, (place + way * step + shards) % shards)
+    tiles = []
+    for out_ref, half in zip(out_refs, halved):
+        count = out_ref.shape[0]
+        first = 0 if half is None else (core ^ half) * count
+        for q in range(count):
+            d = first + q
+            total = None
+            for eval_ref, corpus_ref, eval_ids, corpus_ids in sources:
+                for i in range(slots):
+                    own = eval_ids[i, e]
+                    column, hit = 0, jnp.float32(0.0)
+                    for j in range(slots):
+                        same = (own == corpus_ids[d, j]) & (own < tiles_slice)
+                        column = jnp.where(same, j, column)
+                        hit = jnp.where(same, 1.0, hit)
+                    product = lax.dot_general(
+                        eval_ref[0, i] * hit.astype(jnp.bfloat16),
+                        corpus_ref[d, column],
+                        (((1,), (1,)), ((), ())),
+                        preferred_element_type=jnp.float32,
+                    )
+                    total = product if total is None else total + product
+            out_ref[q] = total
+            tiles.append(total)
+    if coded:
+        encode([ref[q] for ref in carried_refs for q in range(ref.shape[0])] + tiles, out_refs[-1])
+
+
+def dots(step, sources, halved, carried=(), coded=True):
+    blocks, slots, rows, terms = sources[0][1].shape
+    counts = [blocks if half is None else blocks // 2 for half in halved]
+    outs = [jax.ShapeDtypeStruct((count, rows, rows), jnp.float32) for count in counts]
+    if coded:
+        outs.append(code_shape(sum(c.shape[0] for c in carried) + counts[0], rows))
+    tiles_slice = tiles_in_slice(sources[0][1])
+    return pl.pallas_call(
+        functools.partial(dots_kernel, tiles_slice, step, halved, len(carried), coded),
+        out_shape=tuple(outs),
+        in_specs=[VMEM, VMEM, SMEM, SMEM] * len(sources) + [VMEM] * len(carried),
+        out_specs=(VMEM,) * len(outs),
+        compiler_params=pltpu.CompilerParams(vmem_limit_bytes=LIMIT),
+        cost_estimate=pl.CostEstimate(
+            flops=2 * sum(counts) * len(sources) * slots * rows * rows * terms,
+            bytes_accessed=2 * len(sources) * (blocks + 1) * slots * rows * terms,
+            transcendentals=0,
+        ),
+    )(*[array for source in sources for array in source], *carried)
+
+
+def add_kernel(near_ref, far_ref, out_ref, code_ref):
+    tiles = [near_ref[q] + far_ref[q] for q in range(out_ref.shape[0])]
+    for q, tile in enumerate(tiles):
+        out_ref[q] = tile
+    encode(tiles, code_ref)
+
+
+def add_and_code(near, far):
+    return pl.pallas_call(
+        add_kernel,
+        out_shape=(jax.ShapeDtypeStruct(near.shape, near.dtype), code_shape(*near.shape[:2])),
+        in_specs=[VMEM] * 2,
+        out_specs=(VMEM, VMEM),
+        compiler_params=pltpu.CompilerParams(vmem_limit_bytes=LIMIT),
+    )(near, far)
+
+
+def joined(parts):
+    for *near, code_ref in parts:
+        tiles = [ref[q] for ref in near for q in range(ref.shape[0])]
+        for tile, there in zip(tiles, decode(code_ref)):
+            yield tile + there
+
+
+def grouped(refs, counts):
+    refs = list(refs)
+    return [[refs.pop(0) for _ in range(count)] for count in counts]
+
+
+def join_kernel(counts, *refs):
+    *refs, out_ref = refs
+    for q, tile in enumerate(joined(grouped(refs, counts))):
+        out_ref[q] = tile
+
+
+def join(parts):
+    arrays = [array for part in parts for array in part]
+    tiles = [array for part in parts for array in part[:-1]]
+    count = sum(array.shape[0] for array in tiles)
+    return pl.pallas_call(
+        functools.partial(join_kernel, [len(part) for part in parts]),
+        out_shape=jax.ShapeDtypeStruct((count, *tiles[0].shape[1:]), jnp.float32),
+        in_specs=[VMEM] * len(arrays),
+        out_specs=VMEM,
+        compiler_params=pltpu.CompilerParams(vmem_limit_bytes=LIMIT),
+    )(*arrays)
+
+
+def load_kernel(count, *refs):
+    norms = 2
+    arrays = refs[: count + norms]
+    copied = refs[count + norms : 2 * count + norms]
+    scale_ref, *norm_refs, sem = refs[2 * count + norms :]
+    targets = [*copied, *norm_refs]
+    copies = [pltpu.make_async_copy(src, dst, sem.at[n]) for n, (src, dst) in enumerate(zip(arrays, targets))]
+    for copy in copies:
+        copy.start()
+    for copy in copies[-norms:]:
+        copy.wait()
+    eval_norm_ref, corpus_norm_ref = norm_refs
+    shards, blocks = eval_norm_ref.shape[0], corpus_norm_ref.shape[0]
+    eval_norm = eval_norm_ref[...].T
+    for e in range(shards):
+        for d in range(blocks):
+            scale_ref[e * blocks + d] = 1.0 / (eval_norm[:, e : e + 1] * corpus_norm_ref[d : d + 1, :])
+    for copy in copies[:-norms]:
+        copy.wait()
+
+
+def load(arrays, eval_norm, corpus_norm):
+    items = eval_norm.shape[0] * corpus_norm.shape[0]
+    rows = eval_norm.shape[1]
+    given = [pltpu.with_memory_space_constraint(array, pltpu.HBM) for array in (*arrays, eval_norm, corpus_norm)]
+    return pl.pallas_call(
+        functools.partial(load_kernel, len(arrays)),
+        out_shape=[jax.ShapeDtypeStruct(array.shape, array.dtype) for array in arrays]
+        + [jax.ShapeDtypeStruct((items, rows, rows), jnp.float32)],
+        in_specs=[pl.BlockSpec(memory_space=pltpu.HBM)] * len(given),
+        out_specs=[VMEM] * (len(arrays) + 1),
+        scratch_shapes=[
+            pltpu.VMEM(eval_norm.shape, jnp.float32),
+            pltpu.VMEM(corpus_norm.shape, jnp.float32),
+            pltpu.SemaphoreType.DMA((len(given),)),
+        ],
+        compiler_params=pltpu.CompilerParams(vmem_limit_bytes=LIMIT),
+    )(*given)
+
+
+def spread_kernel(shards, blocks, counts, pair_eval_ref, pair_corpus_ref, pair_count_ref, scale_ref, *refs):
+    sums, (out_ref, table, staged, sem) = list(refs[:-4]), refs[-4:]
+    quarter = out_ref.shape[0]
+    ring, far, half = ring_of(shards), shards // 2, blocks // 2
+    place, way, core = ring_place(shards)
+    for side in range(2):
+        early, *late = sums[side * (len(sums) // 2) : (side + 1) * (len(sums) // 2)]
+        tiles = [early[q] for q in range(early.shape[0])] + list(joined(grouped(late, counts)))
+        at = 0
+        for step in range(far + 1):
+            e = look_up(ring, (place + (1 - 2 * side) * way * step + shards) % shards)
+            shared = step in (0, far)
+            for q in range(half if shared else blocks):
+                table[e * blocks + ((core ^ side) * half + q if shared else q)] = tiles[at]
+                at += 1
+    copies = []
+    group = 6 if quarter % 6 == 0 else quarter
+    for p in range(quarter):
+        slot = lax.axis_index("vocab") * quarter + p
+        row = pair_eval_ref[slot] * blocks + pair_corpus_ref[slot]
+        staged[p] = jnp.where(slot < pair_count_ref[0], table[row] * scale_ref[row], 0.0)
+        if (p + 1) % group == 0:
+            part = pl.ds(p + 1 - group, group)
+            copy = pltpu.make_async_copy(staged.at[part], out_ref.at[part], sem.at[p // group])
+            copy.start()
+            copies.append(copy)
+    for copy in copies:
+        copy.wait()
+
+
+def after(array, *others):
+    return lax.optimization_barrier((array, *others))[0]
+
+
+def few_items(
+    eval_tiles,
+    eval_tile_list,
+    corpus_tiles,
+    corpus_tile_list,
+    pair_eval_block,
+    pair_corpus_block,
+    pair_count,
+    eval_norm,
+    corpus_norm,
+):
+    shards, slices = lax.axis_size("corpus"), lax.axis_size("vocab")
+    blocks, slots, rows = corpus_tiles.shape[:3]
+    quarter = pair_eval_block.shape[0] // slices
+    far = shards // 2
+
+    ring = ring_of(shards)
+    onward = []
+    for at in range(shards):
+        for v in range(slices):
+            to = ring[(at + (1 if v % 2 == 0 else -1)) % shards]
+            onward.append((ring[at] * slices + v, to * slices + v))
+    to_core = [(v, v ^ 1) for v in range(slices)]
+    to_chip = [(v, v ^ 2) for v in range(slices)]
+
+    def move(block):
+        return lax.ppermute(block, ("corpus", "vocab"), onward)
+
+    def swap(array):
+        return lax.ppermute(array, "vocab", to_core)
+
+    def cross(array):
+        return lax.ppermute(array, "vocab", to_chip)
+
+    near, also = [eval_tiles], [swap(eval_tiles)]
+    near.append(move(near[0]))
+    also.append(move(also[0]))
+    corpus_also = swap(corpus_tiles)
+    ids = (eval_tile_list.T, corpus_tile_list)
+    ids_also = tuple(swap(array) for array in ids)
+    given = (corpus_tiles, eval_tiles, *ids, pair_eval_block, pair_corpus_block)
+    corpus_tiles, near[0], *ids, pair_eval_block, pair_corpus_block, scale = load(
+        given, eval_norm.reshape(shards, rows), corpus_norm.reshape(blocks, rows)
+    )
+    near[1] = after(near[1], scale)
+
+    def work(step, halved, **more):
+        sources = [(near[step], corpus_tiles, *ids)]
+        if step < len(also):
+            sources.append((also[step], corpus_also, *ids_also))
+        return dots(step, sources, halved, **more)
+
+    parts = []
+    for step in range(far):
+        if step > 0:
+            near.append(move(near[step]))
+            if step + 1 < far:
+                also.append(move(also[step]))
+        if step == 0:
+            (own,) = work(0, (0,), coded=False)
+            also[1] = after(also[1], own)
+            continue
+        chip, code = work(step, (None,), carried=(own,) if step == 1 else ())
+        code_there = cross(code)
+        parts.append([own, chip, code_there] if step == 1 else [chip, code_there])
+        near[step + 1] = after(near[step + 1], chip)
+        if step + 1 < far:
+            also[step + 1] = after(also[step + 1], code_there)
+    keep, send = work(far, (0, 1), coded=False)
+    last, last_code = add_and_code(keep, swap(send))
+    parts.append([last, cross(last_code)])
+    parts[-3][-1] = after(parts[-3][-1], keep)
+    early, late = join(parts[:-2]), parts[-2:]
+    mine = [early] + [array for part in late for array in part]
+    sums = mine + [swap(array) for array in mine]
+    return pl.pallas_call(
+        functools.partial(spread_kernel, shards, blocks, [len(part) for part in late]),
+        out_shape=jax.ShapeDtypeStruct((quarter, rows, rows), jnp.float32),
+        in_specs=[SMEM] * 3 + [VMEM] * (1 + len(sums)),
+        out_specs=pl.BlockSpec(memory_space=pl.ANY),
+        scratch_shapes=[
+            pltpu.VMEM((shards * blocks, rows, rows), jnp.float32),
+            pltpu.VMEM((quarter, rows, rows), jnp.float32),
+            pltpu.SemaphoreType.DMA((quarter,)),
+        ],
+        compiler_params=pltpu.CompilerParams(vmem_limit_bytes=LIMIT),
+    )(pair_eval_block, pair_corpus_block, pair_count, scale, *sums)
 
 
 def solution(mesh):
@@ -85,4 +407,12 @@
         P("corpus"),
     )
     out_specs = P(("corpus", "vocab"), None, None)
-    return jax.shard_map(local, mesh=mesh, in_specs=in_specs, out_specs=out_specs, check_vma=False)
+
+    def program(*arrays):
+        shards, slices = mesh.shape["corpus"], mesh.shape["vocab"]
+        evals, blocks, slots = arrays[0].shape[0], arrays[2].shape[0] // shards, arrays[4].shape[0] // shards
+        few = slices == 4 and shards == evals and shards % 2 == 0 and blocks % 2 == 0 and evals * blocks <= slots
+        local = few_items if few else general
+        return jax.shard_map(local, mesh=mesh, in_specs=in_specs, out_specs=out_specs, check_vma=False)(*arrays)
+
+    return program

time: 340 us -> 50.3 us (0.15)
  waiting for transfers between devices: 209 us -> 14.4 us
  local copies, waits for them, and re-layouts: 52.7 us -> 0.01 us
  matrix products: 41.9 us -> 0 us
  starting transfers between devices: 0.04 us -> 23 us
  between operations: 14.1 us -> 0.76 us
  other arithmetic: 12.8 us -> 0 us
  Pallas kernels: 0 us -> 11.9 us
  loops' own time: 8.26 us -> 0 us
    reduce_scatter x1 -> x0, waiting for transfers between devices: 144 us -> none  [local(): lax.psum_scatter(lax.fori_loop(0, groups, one_group, start_totals), 'voca...]
    all_gather x1 -> x0, waiting for transfers between devices: 64 us -> none  [local(): every_eval = lax.all_gather(eval_tiles, 'corpus', axis=0, tiled=True)]
    gather x26 -> x0, local copies, waits for them, and re-layouts: 47.9 us -> none  [the longest x6 25.8 us: compute(): eval_part = every_eval[eval_index]]
    dot_general x12 -> x0, matrix products: 41.9 us -> none  [the longest x6 29.5 us: compute(): jnp.einsum('gij,gjrt->girt', matched.astype(jnp.bfloat16), corpus_part, p...]
    ppermute x0 -> x21, starting transfers between devices: none -> 23 us  [the longest x7 14.9 us: move(): return lax.ppermute(block, ('corpus', 'vocab'), onward)]
    ppermute x0 -> x21, waiting for transfers between devices: none -> 14.4 us  [the longest x4 11 us: cross(): return lax.ppermute(array, 'vocab', to_chip)]
    pallas_call x0 -> x9, Pallas kernels: none -> 11.9 us  [the longest x5 7.71 us: dots(): pl.pallas_call(functools.partial(dots_kernel, tiles_slice, step, halved,...]
    reduce_or x12 -> x0, other arithmetic: 9.07 us -> none  [one_group(): return lax.cond(jnp.any(living), compute, lambda current: current, totals)]
  transfers between devices with their start and end apart: 2 -> 21, of which waited for: 2 -> 12; matrix products, arithmetic and copies ran while one was open for 1% -> 0% of each run, Pallas kernels for 0% -> 17%
where the time goes in v2:
time: 50.3 us; the launch traced here: 50.1 us
  starting transfers between devices  23 us (46%)
  waiting for transfers between devices  14.4 us (29%)
  Pallas kernels  11.9 us (24%)
  between operations  0.76 us (2%)
    ppermute x7, starting transfers between devices, move(): return lax.ppermute(block, ('corpus', 'vocab'), onward)  14.9 us
    ppermute x4, waiting for transfers between devices, cross(): return lax.ppermute(array, 'vocab', to_chip)  11 us
    pallas_call x5, Pallas kernels, dots(): pl.pallas_call(functools.partial(dots_kernel, tiles_slice, step, halved,...  7.71 us
    ppermute x4, starting transfers between devices, cross(): return lax.ppermute(array, 'vocab', to_chip)  6.03 us
    ppermute x10, waiting for transfers between devices, swap(): return lax.ppermute(array, 'vocab', to_core)  2.44 us
    pallas_call x1, Pallas kernels, few_items(): pl.pallas_call(functools.partial(spread_kernel, shards, blocks, [len(part...  2.19 us
    ppermute x10, starting transfers between devices, swap(): return lax.ppermute(array, 'vocab', to_core)  2.12 us
    pallas_call x1, Pallas kernels, load(): pl.pallas_call(functools.partial(load_kernel, len(arrays)), out_shape=[ja...  1.84 us
  transfers between devices with their start and end apart: 21, of which 12 were waited for; matrix products, arithmetic and copies ran while one was open for 0% of the time, Pallas kernels for 17%

profile of v2, /device:TPU:0, one launch (start us, length us, event | category | flops | bytes accessed | tf_op | source)
XLA Modules:
  0.0 50.1 jit_solution(12447321413887526808)
XLA Ops:
  0.0 0.5 collective-permute-start.1
  0.5 0.1 collective-permute-start
  0.5 3.0 %collective-permute-start.4 = (bf16[1,3,128,512]{3,2,1,0:T(8,128)(2,1)}, bf16[1,3,128,512]{3,2,1,0:T(8,128)(2,1)S(1)}, u32[]{:S(2)}, u32[]{:S(2)}) collective-permute-start(bf16[1,3,128,512]{3,2,1,0:T(8,128)(2,1)} %refs_1_.1), channel_id=1, source_target_pairs={{0,8},{1,5},{2,10},{3,7},{8,16},{9,1},{10,18},{11,3},{16,24},{17,9... | collective-permute-start | bytes 1179656 | tf_op jit(solution)/shard_map/ppermute | solution.py:334
  3.5 0.7 %collective-permute-done.refs_4_ = bf16[1,3,128,512]{3,2,1,0:T(8,128)(2,1)S(1)} collective-permute-done((bf16[1,3,128,512]{3,2,1,0:T(8,128)(2,1)}, bf16[1,3,128,512]{3,2,1,0:T(8,128)(2,1)S(1)}, u32[]{:S(2)}, u32[]{:S(2)}) %collective-permute-start) | collective-permute-done | bytes 393248 | tf_op jit(solution)/shard_map/ppermute | solution.py:337
  4.3 2.9 %collective-permute-start.5 = (bf16[1,3,128,512]{3,2,1,0:T(8,128)(2,1)S(1)}, bf16[1,3,128,512]{3,2,1,0:T(8,128)(2,1)S(1)}, u32[]{:S(2)}, u32[]{:S(2)}) collective-permute-start(bf16[1,3,128,512]{3,2,1,0:T(8,128)(2,1)S(1)} %collective-permute-done.refs_4_), channel_id=1, source_target_pairs={{0,8},{1,5},{2,10},{3,7},{8,16},{9,1},{10,18},{11,3},{16,24},{17,9... | collective-permute-start | bytes 1179656 | tf_op jit(solution)/shard_map/ppermute | solution.py:334
  7.2 1.8 %shard_map.91 = (bf16[4,3,128,512]{3,2,1,0:T(8,128)(2,1)S(1)}, bf16[1,3,128,512]{3,2,1,0:T(8,128)(2,1)S(1)}, s32[3,8]{1,0:T(4,128)S(1)}, s32[4,3]{1,0:T(4,128)S(...) custom-call(bf16[4,3,128,512]{3,2,1,0:T(8,128)(2,1)} %refs_0_.1, bf16[1,3,128,512]{3,2,1,0:T(8,128)(2,1)} %refs_1_.1, ...), custom_call_target="tpu_custom_call" | custom-call | tf_op jit(solution)/shard_map/pallas_call | solution.py:259
  9.1 0.4 collective-permute-done.4.refs_0_
  9.4 2.1 %collective-permute-start.7 = (bf16[1,3,128,512]{3,2,1,0:T(8,128)(2,1)S(1)}, bf16[1,3,128,512]{3,2,1,0:T(8,128)(2,1)S(1)}, u32[]{:S(2)}, u32[]{:S(2)}) collective-permute-start(bf16[1,3,128,512]{3,2,1,0:T(8,128)(2,1)S(1)} %collective-permute-done.4.refs_0_), channel_id=1, source_target_pairs={{0,8},{1,5},{2,10},{3,7},{8,16},{9,1},{10,18},{11,3},{16,24},{17,9... | collective-permute-start | bytes 1179656 | tf_op jit(solution)/shard_map/ppermute | solution.py:334
  11.5 0.0 collective-permute-start.2
  11.5 0.5 %collective-permute-start.3 = (s32[4,3]{1,0:T(4,128)S(1)}, s32[4,3]{1,0:T(4,128)S(1)}, u32[]{:S(2)}, u32[]{:S(2)}) collective-permute-start(s32[4,3]{1,0:T(4,128)S(1)} %copy-done), channel_id=1, source_target_pairs={{0,1},{1,0},{2,3},{3,2},{4,5},{5,4},{6,7},{7,6},{8,9},{9,8},{10,11... | collective-permute-start | bytes 152 | tf_op jit(solution)/shard_map/ppermute | solution.py:337
  12.0 0.8 %collective-permute-done.3.refs_7_ = s32[4,3]{1,0:T(4,128)S(1)} collective-permute-done((s32[4,3]{1,0:T(4,128)S(1)}, s32[4,3]{1,0:T(4,128)S(1)}, u32[]{:S(2)}, u32[]{:S(2)}) %collective-permute-start.3) | collective-permute-done | bytes 80 | tf_op jit(solution)/shard_map/ppermute | solution.py:337
  12.9 0.0 collective-permute-done.2.refs_6_
  12.9 0.0 collective-permute-done.1.refs_5_
  12.9 1.3 %shard_map.92.refs_8_.refs_0_ = f32[2,128,128]{2,1,0:T(8,128)S(1)} custom-call(bf16[1,3,128,512]{3,2,1,0:T(8,128)(2,1)S(1)} %get-tuple-element.33.refs_0_, bf16[4,3,128,512]{3,2,1,0:T(8,128)(2,1)S(1)} %get-tuple-element.34.refs_1_, s32[3,8]{1,0:T(4,128)S(1)} %get-tuple-element.35.refs_2_, s32[4,3]{1,0:T(4,128)S(1)} %get-tuple-element.36.refs_3_, ...), custom_call_target="tpu_custom_call" | custom-call | flops 201326592 | bytes 3932160 | tf_op jit(solution)/shard_map/pallas_call | solution.py:172
  14.2 1.6 %collective-permute-start.8 = (bf16[1,3,128,512]{3,2,1,0:T(8,128)(2,1)S(1)}, bf16[1,3,128,512]{3,2,1,0:T(8,128)(2,1)S(1)}, u32[]{:S(2)}, u32[]{:S(2)}) collective-permute-start(bf16[1,3,128,512]{3,2,1,0:T(8,128)(2,1)S(1)} %collective-permute-done.5.refs_4_), channel_id=1, source_target_pairs={{0,8},{1,5},{2,10},{3,7},{8,16},{9,1},{10,18},{11,3},{16,24},{17,9... | collective-permute-start | bytes 1179656 | tf_op jit(solution)/shard_map/ppermute | solution.py:334
  15.8 1.7 %shard_map.93 = (f32[4,128,128]{2,1,0:T(8,128)S(1)}, s16[784,128]{1,0:T(8,128)(2,1)S(1)}) custom-call(bf16[1,3,128,512]{3,2,1,0:T(8,128)(2,1)S(1)} %collective-permute-done.4.refs_0_, bf16[4,3,128,512]{3,2,1,0:T(8,128)(2,1)S(1)} %get-tuple-element.34.refs_1_, s32[3,8]{1,0:T(4,128)S(1)} %get-tuple-element.35.refs_2_, s32[4,3]{1,0:T(4,128)S(1)} %get-tuple-element.36.refs_3_, ...), custom_call_target="tpu_custom_call" | custom-call | flops 402653184 | bytes 3932160 | tf_op jit(solution)/shard_map/pallas_call | solution.py:172
  17.5 0.3 collective-permute-done.7.refs_0_
  17.9 2.1 %collective-permute-start.10 = (bf16[1,3,128,512]{3,2,1,0:T(8,128)(2,1)S(1)}, bf16[1,3,128,512]{3,2,1,0:T(8,128)(2,1)S(1)}, u32[]{:S(2)}, u32[]{:S(2)}) collective-permute-start(bf16[1,3,128,512]{3,2,1,0:T(8,128)(2,1)S(1)} %collective-permute-done.7.refs_0_), channel_id=1, source_target_pairs={{0,8},{1,5},{2,10},{3,7},{8,16},{9,1},{10,18},{11,3},{16,24},{17,9... | collective-permute-start | bytes 1179656 | tf_op jit(solution)/shard_map/ppermute | solution.py:334
  20.0 1.5 %collective-permute-start.6 = (s16[784,128]{1,0:T(8,128)(2,1)S(1)}, s16[784,128]{1,0:T(8,128)(2,1)S(1)}, u32[]{:S(2)}, u32[]{:S(2)}) collective-permute-start(s16[784,128]{1,0:T(8,128)(2,1)S(1)} %get-tuple-element.40), channel_id=1, source_target_pairs={{0,2},{1,3},{2,0},{3,1},{4,6},{5,7},{6,4},{7,5},{8,10},{9,11},{10,... | collective-permute-start | bytes 602120 | tf_op jit(solution)/shard_map/ppermute | solution.py:340
  21.4 4.3 %collective-permute-done.6.refs_2_ = s16[784,128]{1,0:T(8,128)(2,1)S(1)} collective-permute-done((s16[784,128]{1,0:T(8,128)(2,1)S(1)}, s16[784,128]{1,0:T(8,128)(2,1)S(1)}, u32[]{:S(2)}, u32[]{:S(2)}) %collective-permute-start.6) | collective-permute-done | bytes 200736 | tf_op jit(solution)/shard_map/ppermute | solution.py:340
  25.7 1.5 %collective-permute-start.12 = (bf16[1,3,128,512]{3,2,1,0:T(8,128)(2,1)S(1)}, bf16[1,3,128,512]{3,2,1,0:T(8,128)(2,1)S(1)}, u32[]{:S(2)}, u32[]{:S(2)}) collective-permute-start(bf16[1,3,128,512]{3,2,1,0:T(8,128)(2,1)S(1)} %collective-permute-done.8.refs_4_), channel_id=1, source_target_pairs={{0,8},{1,5},{2,10},{3,7},{8,16},{9,1},{10,18},{11,3},{16,24},{17,9... | collective-permute-start | bytes 1179656 | tf_op jit(solution)/shard_map/ppermute | solution.py:334
  27.2 1.7 %shard_map.94 = (f32[4,128,128]{2,1,0:T(8,128)S(1)}, s16[528,128]{1,0:T(8,128)(2,1)S(1)}) custom-call(bf16[1,3,128,512]{3,2,1,0:T(8,128)(2,1)S(1)} %collective-permute-done.7.refs_0_, bf16[4,3,128,512]{3,2,1,0:T(8,128)(2,1)S(1)} %get-tuple-element.34.refs_1_, s32[3,8]{1,0:T(4,128)S(1)} %get-tuple-element.35.refs_2_, s32[4,3]{1,0:T(4,128)S(1)} %get-tuple-element.36.refs_3_, ...), custom_call_target="tpu_custom_call" | custom-call | flops 402653184 | bytes 3932160 | tf_op jit(solution)/shard_map/pallas_call | solution.py:172
  29.0 0.0 collective-permute-done.10.refs_0_
  29.0 1.6 %collective-permute-start.11 = (bf16[1,3,128,512]{3,2,1,0:T(8,128)(2,1)S(1)}, bf16[1,3,128,512]{3,2,1,0:T(8,128)(2,1)S(1)}, u32[]{:S(2)}, u32[]{:S(2)}) collective-permute-start(bf16[1,3,128,512]{3,2,1,0:T(8,128)(2,1)S(1)} %collective-permute-done.10.refs_0_), channel_id=1, source_target_pairs={{0,8},{1,5},{2,10},{3,7},{8,16},{9,1},{10,18},{11,3},{16,24},{17,9... | collective-permute-start | bytes 1179656 | tf_op jit(solution)/shard_map/ppermute | solution.py:334
  30.6 1.5 %collective-permute-start.9 = (s16[528,128]{1,0:T(8,128)(2,1)S(1)}, s16[528,128]{1,0:T(8,128)(2,1)S(1)}, u32[]{:S(2)}, u32[]{:S(2)}) collective-permute-start(s16[528,128]{1,0:T(8,128)(2,1)S(1)} %get-tuple-element.44), channel_id=1, source_target_pairs={{0,2},{1,3},{2,0},{3,1},{4,6},{5,7},{6,4},{7,5},{8,10},{9,11},{10,... | collective-permute-start | bytes 405512 | tf_op jit(solution)/shard_map/ppermute | solution.py:340
  32.1 3.5 %collective-permute-done.9.refs_4_ = s16[528,128]{1,0:T(8,128)(2,1)S(1)} collective-permute-done((s16[528,128]{1,0:T(8,128)(2,1)S(1)}, s16[528,128]{1,0:T(8,128)(2,1)S(1)}, u32[]{:S(2)}, u32[]{:S(2)}) %collective-permute-start.9) | collective-permute-done | bytes 135200 | tf_op jit(solution)/shard_map/ppermute | solution.py:340
  35.6 0.0 collective-permute-done.12.refs_4_
  35.7 1.8 %shard_map.95 = (f32[4,128,128]{2,1,0:T(8,128)S(1)}, s16[528,128]{1,0:T(8,128)(2,1)S(1)}) custom-call(bf16[1,3,128,512]{3,2,1,0:T(8,128)(2,1)S(1)} %collective-permute-done.10.refs_0_, bf16[4,3,128,512]{3,2,1,0:T(8,128)(2,1)S(1)} %get-tuple-element.34.refs_1_, s32[3,8]{1,0:T(4,128)S(1)} %get-tuple-element.35.refs_2_, s32[4,3]{1,0:T(4,128)S(1)} %get-tuple-element.36.refs_3_, ...), custom_call_target="tpu_custom_call" | custom-call | flops 402653184 | bytes 3932160 | tf_op jit(solution)/shard_map/pallas_call | solution.py:172
  37.4 0.3 collective-permute-done.11.refs_0_
  37.7 1.2 %shard_map.96 = (f32[2,128,128]{2,1,0:T(8,128)S(1)}, f32[2,128,128]{2,1,0:T(8,128)S(1)}) custom-call(bf16[1,3,128,512]{3,2,1,0:T(8,128)(2,1)S(1)} %collective-permute-done.11.refs_0_, bf16[4,3,128,512]{3,2,1,0:T(8,128)(2,1)S(1)} %get-tuple-element.34.refs_1_, s32[3,8]{1,0:T(4,128)S(1)} %get-tuple-element.35.refs_2_, s32[4,3]{1,0:T(4,128)S(1)} %get-tuple-element.36.refs_3_), custom_call_target="tpu_custom_call" | custom-call | flops 201326592 | bytes 1966080 | tf_op jit(solution)/shard_map/pallas_call | solution.py:172
  38.9 0.1 shard_map.97.refs_0_
  39.0 0.1 collective-permute-start.16
  39.1 0.5 collective-permute-start.14
  39.6 1.5 %collective-permute-start.13 = (s16[528,128]{1,0:T(8,128)(2,1)S(1)}, s16[528,128]{1,0:T(8,128)(2,1)S(1)}, u32[]{:S(2)}, u32[]{:S(2)}) collective-permute-start(s16[528,128]{1,0:T(8,128)(2,1)S(1)} %get-tuple-element.51), channel_id=1, source_target_pairs={{0,2},{1,3},{2,0},{3,1},{4,6},{5,7},{6,4},{7,5},{8,10},{9,11},{10,... | collective-permute-start | bytes 405512 | tf_op jit(solution)/shard_map/ppermute | solution.py:340
  41.1 0.0 collective-permute-start.17
  41.1 0.3 collective-permute-done.14.far_ref
  41.4 0.1 shard_map.98
  41.5 1.6 %collective-permute-start.15 = (s16[272,128]{1,0:T(8,128)(2,1)S(1)}, s16[272,128]{1,0:T(8,128)(2,1)S(1)}, u32[]{:S(2)}, u32[]{:S(2)}) collective-permute-start(s16[272,128]{1,0:T(8,128)(2,1)S(1)} %get-tuple-element.54), channel_id=1, source_target_pairs={{0,2},{1,3},{2,0},{3,1},{4,6},{5,7},{6,4},{7,5},{8,10},{9,11},{10,... | collective-permute-start | bytes 208904 | tf_op jit(solution)/shard_map/ppermute | solution.py:340
  43.0 2.9 %collective-permute-done.13.refs_2_ = s16[528,128]{1,0:T(8,128)(2,1)S(1)} collective-permute-done((s16[528,128]{1,0:T(8,128)(2,1)S(1)}, s16[528,128]{1,0:T(8,128)(2,1)S(1)}, u32[]{:S(2)}, u32[]{:S(2)}) %collective-permute-start.13) | collective-permute-done | bytes 135200 | tf_op jit(solution)/shard_map/ppermute | solution.py:340
  45.9 0.0 collective-permute-start.18
  45.9 0.5 %collective-permute-start.19 = (f32[2,128,128]{2,1,0:T(8,128)S(1)}, f32[2,128,128]{2,1,0:T(8,128)S(1)}, u32[]{:S(2)}, u32[]{:S(2)}) collective-permute-start(f32[2,128,128]{2,1,0:T(8,128)S(1)} %get-tuple-element.53.refs_3_), channel_id=1, source_target_pairs={{0,1},{1,0},{2,3},{3,2},{4,5},{5,4},{6,7},{7,6},{8,9},{9,8},{10,11... | collective-permute-start | bytes 393224 | tf_op jit(solution)/shard_map/ppermute | solution.py:337
  46.4 0.2 collective-permute-done.15.refs_4_
  46.7 0.0 collective-permute-start.20
  47.3 0.1 collective-permute-done.19.refs_8_
  47.5 0.5 collective-permute-done.20.refs_9_
  47.9 0.0 collective-permute-done.18.refs_7_
  47.9 0.0 collective-permute-done.16.refs_5_
  47.9 2.2 %shard_map.99 = f32[24,128,128]{2,1,0:T(8,128)} custom-call(s32[96]{0:T(128)S(1)} %get-tuple-element.30.pair_eval_ref, s32[96]{0:T(128)S(1)} %get-tuple-element.31.pair_corpus_ref, s32[1]{0:T(128)S(6)} %copy.10.pair_count_ref, f32[32,128,128]{2,1,0:T(8,128)S(1)} %get-tuple-element.32.scale_ref, f32[10,128,128]{2,1,0:T(8,128)S(1)} %shard_map.97.refs_0_, ...), custom_call_target="tpu_custom_call" | custom-call | tf_op jit(solution)/shard_map/pallas_call | solution.py:383
  (7 shorter events, 0.0 us)
Async XLA Ops:
  0.0 11.5 %copy-start.1 = (s32[8,3]{0,1:T(4,128)S(1)}, s32[8,3]{0,1:T(4,128)}, u32[]{:S(2)}) copy-start(s32[8,3]{0,1:T(4,128)} %param.10) | copy-start | bytes 292
  0.0 11.5 %copy-start = (s32[4,3]{1,0:T(4,128)S(1)}, s32[4,3]{1,0:T(4,128)}, u32[]{:S(2)}) copy-start(s32[4,3]{1,0:T(4,128)} %refs_3_.1) | copy-start | bytes 148
  0.0 12.9 %collective-permute-start.1 = (bf16[4,3,128,512]{3,2,1,0:T(8,128)(2,1)}, bf16[4,3,128,512]{3,2,1,0:T(8,128)(2,1)S(1)}, u32[]{:S(2)}, u32[]{:S(2)}) collective-permute-start(bf16[4,3,128,512]{3,2,1,0:T(8,128)(2,1)} %refs_0_.1), channel_id=1, source_target_pairs={{0,1},{1,0},{2,3},{3,2},{4,5},{5,4},{6,7},{7,6},{8,9},{9,8},{10,11... | collective-permute-start | bytes 4718600 | tf_op jit(solution)/shard_map/ppermute | solution.py:337
  0.5 3.8 %collective-permute-start = (bf16[1,3,128,512]{3,2,1,0:T(8,128)(2,1)}, bf16[1,3,128,512]{3,2,1,0:T(8,128)(2,1)S(1)}, u32[]{:S(2)}, u32[]{:S(2)}) collective-permute-start(bf16[1,3,128,512]{3,2,1,0:T(8,128)(2,1)} %refs_1_.1), channel_id=1, source_target_pairs={{0,1},{1,0},{2,3},{3,2},{4,5},{5,4},{6,7},{7,6},{8,9},{9,8},{10,11... | collective-permute-start | bytes 1179656 | tf_op jit(solution)/shard_map/ppermute | solution.py:337
  0.5 8.9 %collective-permute-start.4 = (bf16[1,3,128,512]{3,2,1,0:T(8,128)(2,1)}, bf16[1,3,128,512]{3,2,1,0:T(8,128)(2,1)S(1)}, u32[]{:S(2)}, u32[]{:S(2)}) collective-permute-start(bf16[1,3,128,512]{3,2,1,0:T(8,128)(2,1)} %refs_1_.1), channel_id=1, source_target_pairs={{0,8},{1,5},{2,10},{3,7},{8,16},{9,1},{10,18},{11,3},{16,24},{17,9... | collective-permute-start | bytes 1179656 | tf_op jit(solution)/shard_map/ppermute | solution.py:334
  4.3 9.9 %collective-permute-start.5 = (bf16[1,3,128,512]{3,2,1,0:T(8,128)(2,1)S(1)}, bf16[1,3,128,512]{3,2,1,0:T(8,128)(2,1)S(1)}, u32[]{:S(2)}, u32[]{:S(2)}) collective-permute-start(bf16[1,3,128,512]{3,2,1,0:T(8,128)(2,1)S(1)} %collective-permute-done.refs_4_), channel_id=1, source_target_pairs={{0,8},{1,5},{2,10},{3,7},{8,16},{9,1},{10,18},{11,3},{16,24},{17,9... | collective-permute-start | bytes 1179656 | tf_op jit(solution)/shard_map/ppermute | solution.py:334
  9.4 8.4 %collective-permute-start.7 = (bf16[1,3,128,512]{3,2,1,0:T(8,128)(2,1)S(1)}, bf16[1,3,128,512]{3,2,1,0:T(8,128)(2,1)S(1)}, u32[]{:S(2)}, u32[]{:S(2)}) collective-permute-start(bf16[1,3,128,512]{3,2,1,0:T(8,128)(2,1)S(1)} %collective-permute-done.4.refs_0_), channel_id=1, source_target_pairs={{0,8},{1,5},{2,10},{3,7},{8,16},{9,1},{10,18},{11,3},{16,24},{17,9... | collective-permute-start | bytes 1179656 | tf_op jit(solution)/shard_map/ppermute | solution.py:334
  11.5 1.3 %collective-permute-start.2 = (s32[3,8]{1,0:T(4,128)S(1)}, s32[3,8]{1,0:T(4,128)S(1)}, u32[]{:S(2)}, u32[]{:S(2)}) collective-permute-start(s32[3,8]{1,0:T(4,128)S(1)} %bitcast.6), channel_id=1, source_target_pairs={{0,1},{1,0},{2,3},{3,2},{4,5},{5,4},{6,7},{7,6},{8,9},{9,8},{10,11... | collective-permute-start | bytes 296 | tf_op jit(solution)/shard_map/ppermute | solution.py:337
  11.5 1.3 %collective-permute-start.3 = (s32[4,3]{1,0:T(4,128)S(1)}, s32[4,3]{1,0:T(4,128)S(1)}, u32[]{:S(2)}, u32[]{:S(2)}) collective-permute-start(s32[4,3]{1,0:T(4,128)S(1)} %copy-done), channel_id=1, source_target_pairs={{0,1},{1,0},{2,3},{3,2},{4,5},{5,4},{6,7},{7,6},{8,9},{9,8},{10,11... | collective-permute-start | bytes 152 | tf_op jit(solution)/shard_map/ppermute | solution.py:337
  14.2 11.6 %collective-permute-start.8 = (bf16[1,3,128,512]{3,2,1,0:T(8,128)(2,1)S(1)}, bf16[1,3,128,512]{3,2,1,0:T(8,128)(2,1)S(1)}, u32[]{:S(2)}, u32[]{:S(2)}) collective-permute-start(bf16[1,3,128,512]{3,2,1,0:T(8,128)(2,1)S(1)} %collective-permute-done.5.refs_4_), channel_id=1, source_target_pairs={{0,8},{1,5},{2,10},{3,7},{8,16},{9,1},{10,18},{11,3},{16,24},{17,9... | collective-permute-start | bytes 1179656 | tf_op jit(solution)/shard_map/ppermute | solution.py:334
  17.9 11.1 %collective-permute-start.10 = (bf16[1,3,128,512]{3,2,1,0:T(8,128)(2,1)S(1)}, bf16[1,3,128,512]{3,2,1,0:T(8,128)(2,1)S(1)}, u32[]{:S(2)}, u32[]{:S(2)}) collective-permute-start(bf16[1,3,128,512]{3,2,1,0:T(8,128)(2,1)S(1)} %collective-permute-done.7.refs_0_), channel_id=1, source_target_pairs={{0,8},{1,5},{2,10},{3,7},{8,16},{9,1},{10,18},{11,3},{16,24},{17,9... | collective-permute-start | bytes 1179656 | tf_op jit(solution)/shard_map/ppermute | solution.py:334
  20.0 5.8 %collective-permute-start.6 = (s16[784,128]{1,0:T(8,128)(2,1)S(1)}, s16[784,128]{1,0:T(8,128)(2,1)S(1)}, u32[]{:S(2)}, u32[]{:S(2)}) collective-permute-start(s16[784,128]{1,0:T(8,128)(2,1)S(1)} %get-tuple-element.40), channel_id=1, source_target_pairs={{0,2},{1,3},{2,0},{3,1},{4,6},{5,7},{6,4},{7,5},{8,10},{9,11},{10,... | collective-permute-start | bytes 602120 | tf_op jit(solution)/shard_map/ppermute | solution.py:340
  25.7 9.9 %collective-permute-start.12 = (bf16[1,3,128,512]{3,2,1,0:T(8,128)(2,1)S(1)}, bf16[1,3,128,512]{3,2,1,0:T(8,128)(2,1)S(1)}, u32[]{:S(2)}, u32[]{:S(2)}) collective-permute-start(bf16[1,3,128,512]{3,2,1,0:T(8,128)(2,1)S(1)} %collective-permute-done.8.refs_4_), channel_id=1, source_target_pairs={{0,8},{1,5},{2,10},{3,7},{8,16},{9,1},{10,18},{11,3},{16,24},{17,9... | collective-permute-start | bytes 1179656 | tf_op jit(solution)/shard_map/ppermute | solution.py:334
  29.0 8.7 %collective-permute-start.11 = (bf16[1,3,128,512]{3,2,1,0:T(8,128)(2,1)S(1)}, bf16[1,3,128,512]{3,2,1,0:T(8,128)(2,1)S(1)}, u32[]{:S(2)}, u32[]{:S(2)}) collective-permute-start(bf16[1,3,128,512]{3,2,1,0:T(8,128)(2,1)S(1)} %collective-permute-done.10.refs_0_), channel_id=1, source_target_pairs={{0,8},{1,5},{2,10},{3,7},{8,16},{9,1},{10,18},{11,3},{16,24},{17,9... | collective-permute-start | bytes 1179656 | tf_op jit(solution)/shard_map/ppermute | solution.py:334
  30.6 5.0 %collective-permute-start.9 = (s16[528,128]{1,0:T(8,128)(2,1)S(1)}, s16[528,128]{1,0:T(8,128)(2,1)S(1)}, u32[]{:S(2)}, u32[]{:S(2)}) collective-permute-start(s16[528,128]{1,0:T(8,128)(2,1)S(1)} %get-tuple-element.44), channel_id=1, source_target_pairs={{0,2},{1,3},{2,0},{3,1},{4,6},{5,7},{6,4},{7,5},{8,10},{9,11},{10,... | collective-permute-start | bytes 405512 | tf_op jit(solution)/shard_map/ppermute | solution.py:340
  39.0 8.9 %collective-permute-start.16 = (f32[10,128,128]{2,1,0:T(8,128)S(1)}, f32[10,128,128]{2,1,0:T(8,128)S(1)}, u32[]{:S(2)}, u32[]{:S(2)}) collective-permute-start(f32[10,128,128]{2,1,0:T(8,128)S(1)} %shard_map.97.refs_0_), channel_id=1, source_target_pairs={{0,1},{1,0},{2,3},{3,2},{4,5},{5,4},{6,7},{7,6},{8,9},{9,8},{10,11... | collective-permute-start | bytes 1966088 | tf_op jit(solution)/shard_map/ppermute | solution.py:337
  39.1 2.3 %collective-permute-start.14 = (f32[2,128,128]{2,1,0:T(8,128)S(1)}, f32[2,128,128]{2,1,0:T(8,128)S(1)}, u32[]{:S(2)}, u32[]{:S(2)}) collective-permute-start(f32[2,128,128]{2,1,0:T(8,128)S(1)} %get-tuple-element.52), channel_id=1, source_target_pairs={{0,1},{1,0},{2,3},{3,2},{4,5},{5,4},{6,7},{7,6},{8,9},{9,8},{10,11... | collective-permute-start | bytes 393224 | tf_op jit(solution)/shard_map/ppermute | solution.py:337
  39.6 6.3 %collective-permute-start.13 = (s16[528,128]{1,0:T(8,128)(2,1)S(1)}, s16[528,128]{1,0:T(8,128)(2,1)S(1)}, u32[]{:S(2)}, u32[]{:S(2)}) collective-permute-start(s16[528,128]{1,0:T(8,128)(2,1)S(1)} %get-tuple-element.51), channel_id=1, source_target_pairs={{0,2},{1,3},{2,0},{3,1},{4,6},{5,7},{6,4},{7,5},{8,10},{9,11},{10,... | collective-permute-start | bytes 405512 | tf_op jit(solution)/shard_map/ppermute | solution.py:340
  41.1 6.2 %collective-permute-start.17 = (f32[4,128,128]{2,1,0:T(8,128)S(1)}, f32[4,128,128]{2,1,0:T(8,128)S(1)}, u32[]{:S(2)}, u32[]{:S(2)}) collective-permute-start(f32[4,128,128]{2,1,0:T(8,128)S(1)} %get-tuple-element.47.refs_1_), channel_id=1, source_target_pairs={{0,1},{1,0},{2,3},{3,2},{4,5},{5,4},{6,7},{7,6},{8,9},{9,8},{10,11... | collective-permute-start | bytes 786440 | tf_op jit(solution)/shard_map/ppermute | solution.py:337
  41.5 5.2 %collective-permute-start.15 = (s16[272,128]{1,0:T(8,128)(2,1)S(1)}, s16[272,128]{1,0:T(8,128)(2,1)S(1)}, u32[]{:S(2)}, u32[]{:S(2)}) collective-permute-start(s16[272,128]{1,0:T(8,128)(2,1)S(1)} %get-tuple-element.54), channel_id=1, source_target_pairs={{0,2},{1,3},{2,0},{3,1},{4,6},{5,7},{6,4},{7,5},{8,10},{9,11},{10,... | collective-permute-start | bytes 208904 | tf_op jit(solution)/shard_map/ppermute | solution.py:340
  45.9 2.0 %collective-permute-start.18 = (s16[528,128]{1,0:T(8,128)(2,1)S(1)}, s16[528,128]{1,0:T(8,128)(2,1)S(1)}, u32[]{:S(2)}, u32[]{:S(2)}) collective-permute-start(s16[528,128]{1,0:T(8,128)(2,1)S(1)} %collective-permute-done.13.refs_2_), channel_id=1, source_target_pairs={{0,1},{1,0},{2,3},{3,2},{4,5},{5,4},{6,7},{7,6},{8,9},{9,8},{10,11... | collective-permute-start | bytes 405512 | tf_op jit(solution)/shard_map/ppermute | solution.py:337
  45.9 1.5 %collective-permute-start.19 = (f32[2,128,128]{2,1,0:T(8,128)S(1)}, f32[2,128,128]{2,1,0:T(8,128)S(1)}, u32[]{:S(2)}, u32[]{:S(2)}) collective-permute-start(f32[2,128,128]{2,1,0:T(8,128)S(1)} %get-tuple-element.53.refs_3_), channel_id=1, source_target_pairs={{0,1},{1,0},{2,3},{3,2},{4,5},{5,4},{6,7},{7,6},{8,9},{9,8},{10,11... | collective-permute-start | bytes 393224 | tf_op jit(solution)/shard_map/ppermute | solution.py:337
  46.7 1.3 %collective-permute-start.20 = (s16[272,128]{1,0:T(8,128)(2,1)S(1)}, s16[272,128]{1,0:T(8,128)(2,1)S(1)}, u32[]{:S(2)}, u32[]{:S(2)}) collective-permute-start(s16[272,128]{1,0:T(8,128)(2,1)S(1)} %collective-permute-done.15.refs_4_), channel_id=1, source_target_pairs={{0,1},{1,0},{2,3},{3,2},{4,5},{5,4},{6,7},{7,6},{8,9},{9,8},{10,11... | collective-permute-start | bytes 208904 | tf_op jit(solution)/shard_map/ppermute | solution.py:337

commit v3 on v2

--- a/solution.py
+++ b/solution.py
@@ -126,48 +126,46 @@
 
 
 def dots_kernel(tiles_slice, step, halved, carried, coded, *refs):
-    outs = len(halved) + coded
+    outs = 1 + coded
     sources = [refs[4 * n : 4 * n + 4] for n in range((len(refs) - outs - carried) // 4)]
     carried_refs = refs[4 * len(sources) : len(refs) - outs]
-    out_refs = refs[len(refs) - outs :]
+    out_ref, *code_ref = refs[len(refs) - outs :]
     slots, shards = sources[0][2].shape
     ring = ring_of(shards)
     place, way, core = ring_place(shards)
     e = look_up(ring, (place + way * step + shards) % shards)
     tiles = []
-    for out_ref, half in zip(out_refs, halved):
-        count = out_ref.shape[0]
-        first = 0 if half is None else (core ^ half) * count
-        for q in range(count):
-            d = first + q
-            total = None
-            for eval_ref, corpus_ref, eval_ids, corpus_ids in sources:
-                for i in range(slots):
-                    own = eval_ids[i, e]
-                    column, hit = 0, jnp.float32(0.0)
-                    for j in range(slots):
-                        same = (own == corpus_ids[d, j]) & (own < tiles_slice)
-                        column = jnp.where(same, j, column)
-                        hit = jnp.where(same, 1.0, hit)
-                    product = lax.dot_general(
-                        eval_ref[0, i] * hit.astype(jnp.bfloat16),
-                        corpus_ref[d, column],
-                        (((1,), (1,)), ((), ())),
-                        preferred_element_type=jnp.float32,
-                    )
-                    total = product if total is None else total + product
-            out_ref[q] = total
-            tiles.append(total)
+    count = out_ref.shape[0]
+    for q in range(count):
+        d = core * count + q if halved else q
+        total = None
+        for eval_ref, corpus_ref, eval_ids, corpus_ids in sources:
+            for i in range(slots):
+                own = eval_ids[i, e]
+                column, hit = 0, jnp.float32(0.0)
+                for j in range(slots):
+                    same = (own == corpus_ids[d, j]) & (own < tiles_slice)
+                    column = jnp.where(same, j, column)
+                    hit = jnp.where(same, 1.0, hit)
+                product = lax.dot_general(
+                    eval_ref[0, i] * hit.astype(jnp.bfloat16),
+                    corpus_ref[d, column],
+                    (((1,), (1,)), ((), ())),
+                    preferred_element_type=jnp.float32,
+                )
+                total = product if total is None else total + product
+        out_ref[q] = total
+        tiles.append(total)
     if coded:
-        encode([ref[q] for ref in carried_refs for q in range(ref.shape[0])] + tiles, out_refs[-1])
+        encode([ref[q] for ref in carried_refs for q in range(ref.shape[0])] + tiles, *code_ref)
 
 
 def dots(step, sources, halved, carried=(), coded=True):
     blocks, slots, rows, terms = sources[0][1].shape
-    counts = [blocks if half is None else blocks // 2 for half in halved]
-    outs = [jax.ShapeDtypeStruct((count, rows, rows), jnp.float32) for count in counts]
+    count = blocks // 2 if halved else blocks
+    outs = [jax.ShapeDtypeStruct((count, rows, rows), jnp.float32)]
     if coded:
-        outs.append(code_shape(sum(c.shape[0] for c in carried) + counts[0], rows))
+        outs.append(code_shape(sum(c.shape[0] for c in carried) + count, rows))
     tiles_slice = tiles_in_slice(sources[0][1])
     return pl.pallas_call(
         functools.partial(dots_kernel, tiles_slice, step, halved, len(carried), coded),
@@ -176,28 +174,11 @@
         out_specs=(VMEM,) * len(outs),
         compiler_params=pltpu.CompilerParams(vmem_limit_bytes=LIMIT),
         cost_estimate=pl.CostEstimate(
-            flops=2 * sum(counts) * len(sources) * slots * rows * rows * terms,
+            flops=2 * count * len(sources) * slots * rows * rows * terms,
             bytes_accessed=2 * len(sources) * (blocks + 1) * slots * rows * terms,
             transcendentals=0,
         ),
     )(*[array for source in sources for array in source], *carried)
-
-
-def add_kernel(near_ref, far_ref, out_ref, code_ref):
-    tiles = [near_ref[q] + far_ref[q] for q in range(out_ref.shape[0])]
-    for q, tile in enumerate(tiles):
-        out_ref[q] = tile
-    encode(tiles, code_ref)
-
-
-def add_and_code(near, far):
-    return pl.pallas_call(
-        add_kernel,
-        out_shape=(jax.ShapeDtypeStruct(near.shape, near.dtype), code_shape(*near.shape[:2])),
-        in_specs=[VMEM] * 2,
-        out_specs=(VMEM, VMEM),
-        compiler_params=pltpu.CompilerParams(vmem_limit_bytes=LIMIT),
-    )(near, far)
 
 
 def joined(parts):
@@ -352,32 +333,27 @@
     near[1] = after(near[1], scale)
 
     def work(step, halved, **more):
-        sources = [(near[step], corpus_tiles, *ids)]
-        if step < len(also):
-            sources.append((also[step], corpus_also, *ids_also))
+        sources = [(near[step], corpus_tiles, *ids), (also[step], corpus_also, *ids_also)]
         return dots(step, sources, halved, **more)
 
+    (own,) = work(0, True, coded=False)
+    also[1] = after(also[1], own)
     parts = []
-    for step in range(far):
-        if step > 0:
-            near.append(move(near[step]))
-            if step + 1 < far:
-                also.append(move(also[step]))
-        if step == 0:
-            (own,) = work(0, (0,), coded=False)
-            also[1] = after(also[1], own)
-            continue
-        chip, code = work(step, (None,), carried=(own,) if step == 1 else ())
-        code_there = cross(code)
-        parts.append([own, chip, code_there] if step == 1 else [chip, code_there])
-        near[step + 1] = after(near[step + 1], chip)
+    for step in range(1, far):
+        near.append(move(near[step]))
         if step + 1 < far:
-            also[step + 1] = after(also[step + 1], code_there)
-    keep, send = work(far, (0, 1), coded=False)
-    last, last_code = add_and_code(keep, swap(send))
+            also.append(move(also[step]))
+        carried = (own,) if step == 1 else ()
+        chip, code = work(step, False, carried=carried)
+        parts.append([*carried, chip, cross(code)])
+        near[step + 1] = after(near[step + 1], chip, *[part[-1] for part in parts[:-1]])
+    parts[-2][-1] = after(parts[-2][-1], parts[-1][0])
+    early = join(parts[:-1])
+    near[far] = after(near[far], early)
+    also.append(swap(near[far]))
+    last, last_code = work(far, True)
     parts.append([last, cross(last_code)])
-    parts[-3][-1] = after(parts[-3][-1], keep)
-    early, late = join(parts[:-2]), parts[-2:]
+    late = parts[-2:]
     mine = [early] + [array for part in late for array in part]
     sums = mine + [swap(array) for array in mine]
     return pl.pallas_call(

time: 50.3 us -> 46.4 us (0.922)
  waiting for transfers between devices: 14.4 us -> 9.11 us
  starting transfers between devices: 23 us -> 24.3 us
    ppermute x4, waiting for transfers between devices: 11 us -> 3.47 us  [cross(): return lax.ppermute(array, 'vocab', to_chip)]
    ppermute x7, waiting for transfers between devices: 1.04 us -> 3.5 us  [move(): return lax.ppermute(block, ('corpus', 'vocab'), onward)]
    ppermute x7, starting transfers between devices: 14.9 us -> 15.9 us  [move(): return lax.ppermute(block, ('corpus', 'vocab'), onward)]
  transfers between devices with their start and end apart: 21 -> 21, of which waited for: 12 -> 12; matrix products, arithmetic and copies ran while one was open for 0% -> 0% of each run, Pallas kernels for 17% -> 21%
where the time goes in v3:
time: 46.4 us; the launch traced here: 46.2 us
  starting transfers between devices  24.3 us (52%)
  Pallas kernels  12 us (26%)
  waiting for transfers between devices  9.11 us (20%)
  between operations  0.78 us (2%)
    ppermute x7, starting transfers between devices, move(): return lax.ppermute(block, ('corpus', 'vocab'), onward)  15.9 us
    pallas_call x5, Pallas kernels, dots(): pl.pallas_call(functools.partial(dots_kernel, tiles_slice, step, halved,...  7.88 us
    ppermute x4, starting transfers between devices, cross(): return lax.ppermute(array, 'vocab', to_chip)  6.53 us
    ppermute x7, waiting for transfers between devices, move(): return lax.ppermute(block, ('corpus', 'vocab'), onward)  3.5 us
    ppermute x4, waiting for transfers between devices, cross(): return lax.ppermute(array, 'vocab', to_chip)  3.47 us
    pallas_call x1, Pallas kernels, few_items(): pl.pallas_call(functools.partial(spread_kernel, shards, blocks, [len(part...  2.19 us
    ppermute x10, waiting for transfers between devices, swap(): return lax.ppermute(array, 'vocab', to_core)  2.14 us
    ppermute x10, starting transfers between devices, swap(): return lax.ppermute(array, 'vocab', to_core)  1.85 us
  transfers between devices with their start and end apart: 21, of which 12 were waited for; matrix products, arithmetic and copies ran while one was open for 0% of the time, Pallas kernels for 21%

profile of v3, /device:TPU:0, one launch (start us, length us, event | category | flops | bytes accessed | tf_op | source)
XLA Modules:
  0.0 46.2 jit_solution(14571268514796458854)
XLA Ops:
  0.0 0.5 collective-permute-start.1
  0.5 0.1 collective-permute-start
  0.5 3.0 %collective-permute-start.4 = (bf16[1,3,128,512]{3,2,1,0:T(8,128)(2,1)}, bf16[1,3,128,512]{3,2,1,0:T(8,128)(2,1)S(1)}, u32[]{:S(2)}, u32[]{:S(2)}) collective-permute-start(bf16[1,3,128,512]{3,2,1,0:T(8,128)(2,1)} %refs_1_.1), channel_id=1, source_target_pairs={{0,8},{1,5},{2,10},{3,7},{8,16},{9,1},{10,18},{11,3},{16,24},{17,9... | collective-permute-start | bytes 1179656 | tf_op jit(solution)/shard_map/ppermute | solution.py:315
  3.5 0.7 %collective-permute-done.refs_4_ = bf16[1,3,128,512]{3,2,1,0:T(8,128)(2,1)S(1)} collective-permute-done((bf16[1,3,128,512]{3,2,1,0:T(8,128)(2,1)}, bf16[1,3,128,512]{3,2,1,0:T(8,128)(2,1)S(1)}, u32[]{:S(2)}, u32[]{:S(2)}) %collective-permute-start) | collective-permute-done | bytes 393248 | tf_op jit(solution)/shard_map/ppermute | solution.py:318
  4.3 2.9 %collective-permute-start.5 = (bf16[1,3,128,512]{3,2,1,0:T(8,128)(2,1)S(1)}, bf16[1,3,128,512]{3,2,1,0:T(8,128)(2,1)S(1)}, u32[]{:S(2)}, u32[]{:S(2)}) collective-permute-start(bf16[1,3,128,512]{3,2,1,0:T(8,128)(2,1)S(1)} %collective-permute-done.refs_4_), channel_id=1, source_target_pairs={{0,8},{1,5},{2,10},{3,7},{8,16},{9,1},{10,18},{11,3},{16,24},{17,9... | collective-permute-start | bytes 1179656 | tf_op jit(solution)/shard_map/ppermute | solution.py:315
  7.2 1.8 %shard_map.91 = (bf16[4,3,128,512]{3,2,1,0:T(8,128)(2,1)S(1)}, bf16[1,3,128,512]{3,2,1,0:T(8,128)(2,1)S(1)}, s32[3,8]{1,0:T(4,128)S(1)}, s32[4,3]{1,0:T(4,128)S(...) custom-call(bf16[4,3,128,512]{3,2,1,0:T(8,128)(2,1)} %refs_0_.1, bf16[1,3,128,512]{3,2,1,0:T(8,128)(2,1)} %refs_1_.1, ...), custom_call_target="tpu_custom_call" | custom-call | tf_op jit(solution)/shard_map/pallas_call | solution.py:240
  9.1 0.4 collective-permute-done.4.refs_0_
  9.4 2.1 %collective-permute-start.7 = (bf16[1,3,128,512]{3,2,1,0:T(8,128)(2,1)S(1)}, bf16[1,3,128,512]{3,2,1,0:T(8,128)(2,1)S(1)}, u32[]{:S(2)}, u32[]{:S(2)}) collective-permute-start(bf16[1,3,128,512]{3,2,1,0:T(8,128)(2,1)S(1)} %collective-permute-done.4.refs_0_), channel_id=1, source_target_pairs={{0,8},{1,5},{2,10},{3,7},{8,16},{9,1},{10,18},{11,3},{16,24},{17,9... | collective-permute-start | bytes 1179656 | tf_op jit(solution)/shard_map/ppermute | solution.py:315
  11.5 0.0 collective-permute-start.2
  11.5 0.5 %collective-permute-start.3 = (s32[4,3]{1,0:T(4,128)S(1)}, s32[4,3]{1,0:T(4,128)S(1)}, u32[]{:S(2)}, u32[]{:S(2)}) collective-permute-start(s32[4,3]{1,0:T(4,128)S(1)} %copy-done), channel_id=1, source_target_pairs={{0,1},{1,0},{2,3},{3,2},{4,5},{5,4},{6,7},{7,6},{8,9},{9,8},{10,11... | collective-permute-start | bytes 152 | tf_op jit(solution)/shard_map/ppermute | solution.py:318
  12.0 0.8 %collective-permute-done.3.refs_7_ = s32[4,3]{1,0:T(4,128)S(1)} collective-permute-done((s32[4,3]{1,0:T(4,128)S(1)}, s32[4,3]{1,0:T(4,128)S(1)}, u32[]{:S(2)}, u32[]{:S(2)}) %collective-permute-start.3) | collective-permute-done | bytes 80 | tf_op jit(solution)/shard_map/ppermute | solution.py:318
  12.9 0.0 collective-permute-done.2.refs_6_
  12.9 0.0 collective-permute-done.1.refs_5_
  12.9 1.3 %shard_map.92.refs_8_.refs_0_ = f32[2,128,128]{2,1,0:T(8,128)S(1)} custom-call(bf16[1,3,128,512]{3,2,1,0:T(8,128)(2,1)S(1)} %get-tuple-element.30.refs_0_, bf16[4,3,128,512]{3,2,1,0:T(8,128)(2,1)S(1)} %get-tuple-element.31.refs_1_, s32[3,8]{1,0:T(4,128)S(1)} %get-tuple-element.32.refs_2_, s32[4,3]{1,0:T(4,128)S(1)} %get-tuple-element.33.refs_3_, ...), custom_call_target="tpu_custom_call" | custom-call | flops 201326592 | bytes 3932160 | tf_op jit(solution)/shard_map/pallas_call | solution.py:170
  14.1 0.0 collective-permute-done.5.refs_4_
  14.2 1.6 %collective-permute-start.8 = (bf16[1,3,128,512]{3,2,1,0:T(8,128)(2,1)S(1)}, bf16[1,3,128,512]{3,2,1,0:T(8,128)(2,1)S(1)}, u32[]{:S(2)}, u32[]{:S(2)}) collective-permute-start(bf16[1,3,128,512]{3,2,1,0:T(8,128)(2,1)S(1)} %collective-permute-done.5.refs_4_), channel_id=1, source_target_pairs={{0,8},{1,5},{2,10},{3,7},{8,16},{9,1},{10,18},{11,3},{16,24},{17,9... | collective-permute-start | bytes 1179656 | tf_op jit(solution)/shard_map/ppermute | solution.py:315
  15.8 1.8 %shard_map.93 = (f32[4,128,128]{2,1,0:T(8,128)S(1)}, s16[784,128]{1,0:T(8,128)(2,1)S(1)}) custom-call(bf16[1,3,128,512]{3,2,1,0:T(8,128)(2,1)S(1)} %collective-permute-done.4.refs_0_, bf16[4,3,128,512]{3,2,1,0:T(8,128)(2,1)S(1)} %get-tuple-element.31.refs_1_, s32[3,8]{1,0:T(4,128)S(1)} %get-tuple-element.32.refs_2_, s32[4,3]{1,0:T(4,128)S(1)} %get-tuple-element.33.refs_3_, ...), custom_call_target="tpu_custom_call" | custom-call | flops 402653184 | bytes 3932160 | tf_op jit(solution)/shard_map/pallas_call | solution.py:170
  17.6 0.3 collective-permute-done.7.refs_0_
  17.9 2.1 %collective-permute-start.10 = (bf16[1,3,128,512]{3,2,1,0:T(8,128)(2,1)S(1)}, bf16[1,3,128,512]{3,2,1,0:T(8,128)(2,1)S(1)}, u32[]{:S(2)}, u32[]{:S(2)}) collective-permute-start(bf16[1,3,128,512]{3,2,1,0:T(8,128)(2,1)S(1)} %collective-permute-done.7.refs_0_), channel_id=1, source_target_pairs={{0,8},{1,5},{2,10},{3,7},{8,16},{9,1},{10,18},{11,3},{16,24},{17,9... | collective-permute-start | bytes 1179656 | tf_op jit(solution)/shard_map/ppermute | solution.py:315
  20.0 1.5 %collective-permute-start.6 = (s16[784,128]{1,0:T(8,128)(2,1)S(1)}, s16[784,128]{1,0:T(8,128)(2,1)S(1)}, u32[]{:S(2)}, u32[]{:S(2)}) collective-permute-start(s16[784,128]{1,0:T(8,128)(2,1)S(1)} %get-tuple-element.37), channel_id=1, source_target_pairs={{0,2},{1,3},{2,0},{3,1},{4,6},{5,7},{6,4},{7,5},{8,10},{9,11},{10,... | collective-permute-start | bytes 602120 | tf_op jit(solution)/shard_map/ppermute | solution.py:321
  21.4 0.6 %collective-permute-done.8.refs_4_ = bf16[1,3,128,512]{3,2,1,0:T(8,128)(2,1)S(1)} collective-permute-done((bf16[1,3,128,512]{3,2,1,0:T(8,128)(2,1)S(1)}, bf16[1,3,128,512]{3,2,1,0:T(8,128)(2,1)S(1)}, u32[]{:S(2)}, u32[]{:S(2)}) %collective-permute-start.8) | collective-permute-done | bytes 393248 | tf_op jit(solution)/shard_map/ppermute | solution.py:315
  22.1 2.1 %collective-permute-start.11 = (bf16[1,3,128,512]{3,2,1,0:T(8,128)(2,1)S(1)}, bf16[1,3,128,512]{3,2,1,0:T(8,128)(2,1)S(1)}, u32[]{:S(2)}, u32[]{:S(2)}) collective-permute-start(bf16[1,3,128,512]{3,2,1,0:T(8,128)(2,1)S(1)} %collective-permute-done.8.refs_4_), channel_id=1, source_target_pairs={{0,8},{1,5},{2,10},{3,7},{8,16},{9,1},{10,18},{11,3},{16,24},{17,9... | collective-permute-start | bytes 1179656 | tf_op jit(solution)/shard_map/ppermute | solution.py:315
  24.2 1.7 %shard_map.94 = (f32[4,128,128]{2,1,0:T(8,128)S(1)}, s16[528,128]{1,0:T(8,128)(2,1)S(1)}) custom-call(bf16[1,3,128,512]{3,2,1,0:T(8,128)(2,1)S(1)} %collective-permute-done.7.refs_0_, bf16[4,3,128,512]{3,2,1,0:T(8,128)(2,1)S(1)} %get-tuple-element.31.refs_1_, s32[3,8]{1,0:T(4,128)S(1)} %get-tuple-element.32.refs_2_, s32[4,3]{1,0:T(4,128)S(1)} %get-tuple-element.33.refs_3_, ...), custom_call_target="tpu_custom_call" | custom-call | flops 402653184 | bytes 3932160 | tf_op jit(solution)/shard_map/pallas_call | solution.py:170
  25.9 0.0 collective-permute-done.6.refs_2_
  25.9 0.4 collective-permute-done.10.refs_0_
  26.3 2.1 %collective-permute-start.13 = (bf16[1,3,128,512]{3,2,1,0:T(8,128)(2,1)S(1)}, bf16[1,3,128,512]{3,2,1,0:T(8,128)(2,1)S(1)}, u32[]{:S(2)}, u32[]{:S(2)}) collective-permute-start(bf16[1,3,128,512]{3,2,1,0:T(8,128)(2,1)S(1)} %collective-permute-done.10.refs_0_), channel_id=1, source_target_pairs={{0,8},{1,5},{2,10},{3,7},{8,16},{9,1},{10,18},{11,3},{16,24},{17,9... | collective-permute-start | bytes 1179656 | tf_op jit(solution)/shard_map/ppermute | solution.py:315
  28.4 1.5 %collective-permute-start.9 = (s16[528,128]{1,0:T(8,128)(2,1)S(1)}, s16[528,128]{1,0:T(8,128)(2,1)S(1)}, u32[]{:S(2)}, u32[]{:S(2)}) collective-permute-start(s16[528,128]{1,0:T(8,128)(2,1)S(1)} %get-tuple-element.40), channel_id=1, source_target_pairs={{0,2},{1,3},{2,0},{3,1},{4,6},{5,7},{6,4},{7,5},{8,10},{9,11},{10,... | collective-permute-start | bytes 405512 | tf_op jit(solution)/shard_map/ppermute | solution.py:321
  29.9 0.6 %collective-permute-done.11.refs_4_ = bf16[1,3,128,512]{3,2,1,0:T(8,128)(2,1)S(1)} collective-permute-done((bf16[1,3,128,512]{3,2,1,0:T(8,128)(2,1)S(1)}, bf16[1,3,128,512]{3,2,1,0:T(8,128)(2,1)S(1)}, u32[]{:S(2)}, u32[]{:S(2)}) %collective-permute-start.11) | collective-permute-done | bytes 393248 | tf_op jit(solution)/shard_map/ppermute | solution.py:315
  30.5 1.8 %shard_map.95 = (f32[4,128,128]{2,1,0:T(8,128)S(1)}, s16[528,128]{1,0:T(8,128)(2,1)S(1)}) custom-call(bf16[1,3,128,512]{3,2,1,0:T(8,128)(2,1)S(1)} %collective-permute-done.10.refs_0_, bf16[4,3,128,512]{3,2,1,0:T(8,128)(2,1)S(1)} %get-tuple-element.31.refs_1_, s32[3,8]{1,0:T(4,128)S(1)} %get-tuple-element.32.refs_2_, s32[4,3]{1,0:T(4,128)S(1)} %get-tuple-element.33.refs_3_, ...), custom_call_target="tpu_custom_call" | custom-call | flops 402653184 | bytes 3932160 | tf_op jit(solution)/shard_map/pallas_call | solution.py:170
  32.3 1.1 %collective-permute-done.9.refs_4_ = s16[528,128]{1,0:T(8,128)(2,1)S(1)} collective-permute-done((s16[528,128]{1,0:T(8,128)(2,1)S(1)}, s16[528,128]{1,0:T(8,128)(2,1)S(1)}, u32[]{:S(2)}, u32[]{:S(2)}) %collective-permute-start.9) | collective-permute-done | bytes 135200 | tf_op jit(solution)/shard_map/ppermute | solution.py:321
  33.4 0.1 shard_map.96.refs_0_
  33.5 0.1 collective-permute-start.16
  33.6 1.2 %collective-permute-done.13.refs_0_ = bf16[1,3,128,512]{3,2,1,0:T(8,128)(2,1)S(1)} collective-permute-done((bf16[1,3,128,512]{3,2,1,0:T(8,128)(2,1)S(1)}, bf16[1,3,128,512]{3,2,1,0:T(8,128)(2,1)S(1)}, u32[]{:S(2)}, u32[]{:S(2)}) %collective-permute-start.13) | collective-permute-done | bytes 393248 | tf_op jit(solution)/shard_map/ppermute | solution.py:315
  34.7 0.0 collective-permute-start.14
  34.7 2.0 %collective-permute-start.12 = (s16[528,128]{1,0:T(8,128)(2,1)S(1)}, s16[528,128]{1,0:T(8,128)(2,1)S(1)}, u32[]{:S(2)}, u32[]{:S(2)}) collective-permute-start(s16[528,128]{1,0:T(8,128)(2,1)S(1)} %get-tuple-element.44), channel_id=1, source_target_pairs={{0,2},{1,3},{2,0},{3,1},{4,6},{5,7},{6,4},{7,5},{8,10},{9,11},{10,... | collective-permute-start | bytes 405512 | tf_op jit(solution)/shard_map/ppermute | solution.py:321
  36.7 0.2 collective-permute-start.17
  37.0 0.0 collective-permute-done.14.refs_4_
  37.0 1.3 %shard_map.97 = (f32[2,128,128]{2,1,0:T(8,128)S(1)}, s16[272,128]{1,0:T(8,128)(2,1)S(1)}) custom-call(bf16[1,3,128,512]{3,2,1,0:T(8,128)(2,1)S(1)} %collective-permute-done.13.refs_0_, bf16[4,3,128,512]{3,2,1,0:T(8,128)(2,1)S(1)} %get-tuple-element.31.refs_1_, s32[3,8]{1,0:T(4,128)S(1)} %get-tuple-element.32.refs_2_, s32[4,3]{1,0:T(4,128)S(1)} %get-tuple-element.33.refs_3_, ...), custom_call_target="tpu_custom_call" | custom-call | flops 201326592 | bytes 3932160 | tf_op jit(solution)/shard_map/pallas_call | solution.py:170
  38.3 1.6 %collective-permute-start.15 = (s16[272,128]{1,0:T(8,128)(2,1)S(1)}, s16[272,128]{1,0:T(8,128)(2,1)S(1)}, u32[]{:S(2)}, u32[]{:S(2)}) collective-permute-start(s16[272,128]{1,0:T(8,128)(2,1)S(1)} %get-tuple-element.48), channel_id=1, source_target_pairs={{0,2},{1,3},{2,0},{3,1},{4,6},{5,7},{6,4},{7,5},{8,10},{9,11},{10,... | collective-permute-start | bytes 208904 | tf_op jit(solution)/shard_map/ppermute | solution.py:321
  39.8 1.1 %collective-permute-done.12.refs_2_ = s16[528,128]{1,0:T(8,128)(2,1)S(1)} collective-permute-done((s16[528,128]{1,0:T(8,128)(2,1)S(1)}, s16[528,128]{1,0:T(8,128)(2,1)S(1)}, u32[]{:S(2)}, u32[]{:S(2)}) %collective-permute-start.12) | collective-permute-done | bytes 135200 | tf_op jit(solution)/shard_map/ppermute | solution.py:321
  41.0 0.0 collective-permute-start.18
  41.0 0.5 %collective-permute-start.19 = (f32[2,128,128]{2,1,0:T(8,128)S(1)}, f32[2,128,128]{2,1,0:T(8,128)S(1)}, u32[]{:S(2)}, u32[]{:S(2)}) collective-permute-start(f32[2,128,128]{2,1,0:T(8,128)S(1)} %get-tuple-element.47.refs_3_), channel_id=1, source_target_pairs={{0,1},{1,0},{2,3},{3,2},{4,5},{5,4},{6,7},{7,6},{8,9},{9,8},{10,11... | collective-permute-start | bytes 393224 | tf_op jit(solution)/shard_map/ppermute | solution.py:318
  41.5 1.2 %collective-permute-done.15.refs_4_ = s16[272,128]{1,0:T(8,128)(2,1)S(1)} collective-permute-done((s16[272,128]{1,0:T(8,128)(2,1)S(1)}, s16[272,128]{1,0:T(8,128)(2,1)S(1)}, u32[]{:S(2)}, u32[]{:S(2)}) %collective-permute-start.15) | collective-permute-done | bytes 69664 | tf_op jit(solution)/shard_map/ppermute | solution.py:321
  42.7 0.0 collective-permute-start.20
  43.4 0.0 collective-permute-done.17.refs_6_
  43.4 0.0 collective-permute-done.19.refs_8_
  43.4 0.6 %collective-permute-done.20.refs_9_ = s16[272,128]{1,0:T(8,128)(2,1)S(1)} collective-permute-done((s16[272,128]{1,0:T(8,128)(2,1)S(1)}, s16[272,128]{1,0:T(8,128)(2,1)S(1)}, u32[]{:S(2)}, u32[]{:S(2)}) %collective-permute-start.20) | collective-permute-done | bytes 69664 | tf_op jit(solution)/shard_map/ppermute | solution.py:318
  44.0 2.2 %shard_map.98 = f32[24,128,128]{2,1,0:T(8,128)} custom-call(s32[96]{0:T(128)S(1)} %get-tuple-element.27.pair_eval_ref, s32[96]{0:T(128)S(1)} %get-tuple-element.28.pair_corpus_ref, s32[1]{0:T(128)S(6)} %copy.10.pair_count_ref, f32[32,128,128]{2,1,0:T(8,128)S(1)} %get-tuple-element.29.scale_ref, f32[10,128,128]{2,1,0:T(8,128)S(1)} %shard_map.96.refs_0_, ...), custom_call_target="tpu_custom_call" | custom-call | tf_op jit(solution)/shard_map/pallas_call | solution.py:359
  (6 shorter events, 0.0 us)
Async XLA Ops:
  0.0 11.5 %copy-start.1 = (s32[8,3]{0,1:T(4,128)S(1)}, s32[8,3]{0,1:T(4,128)}, u32[]{:S(2)}) copy-start(s32[8,3]{0,1:T(4,128)} %param.10) | copy-start | bytes 292
  0.0 11.5 %copy-start = (s32[4,3]{1,0:T(4,128)S(1)}, s32[4,3]{1,0:T(4,128)}, u32[]{:S(2)}) copy-start(s32[4,3]{1,0:T(4,128)} %refs_3_.1) | copy-start | bytes 148
  0.0 12.9 %collective-permute-start.1 = (bf16[4,3,128,512]{3,2,1,0:T(8,128)(2,1)}, bf16[4,3,128,512]{3,2,1,0:T(8,128)(2,1)S(1)}, u32[]{:S(2)}, u32[]{:S(2)}) collective-permute-start(bf16[4,3,128,512]{3,2,1,0:T(8,128)(2,1)} %refs_0_.1), channel_id=1, source_target_pairs={{0,1},{1,0},{2,3},{3,2},{4,5},{5,4},{6,7},{7,6},{8,9},{9,8},{10,11... | collective-permute-start | bytes 4718600 | tf_op jit(solution)/shard_map/ppermute | solution.py:318
  0.5 3.8 %collective-permute-start = (bf16[1,3,128,512]{3,2,1,0:T(8,128)(2,1)}, bf16[1,3,128,512]{3,2,1,0:T(8,128)(2,1)S(1)}, u32[]{:S(2)}, u32[]{:S(2)}) collective-permute-start(bf16[1,3,128,512]{3,2,1,0:T(8,128)(2,1)} %refs_1_.1), channel_id=1, source_target_pairs={{0,1},{1,0},{2,3},{3,2},{4,5},{5,4},{6,7},{7,6},{8,9},{9,8},{10,11... | collective-permute-start | bytes 1179656 | tf_op jit(solution)/shard_map/ppermute | solution.py:318
  0.5 8.9 %collective-permute-start.4 = (bf16[1,3,128,512]{3,2,1,0:T(8,128)(2,1)}, bf16[1,3,128,512]{3,2,1,0:T(8,128)(2,1)S(1)}, u32[]{:S(2)}, u32[]{:S(2)}) collective-permute-start(bf16[1,3,128,512]{3,2,1,0:T(8,128)(2,1)} %refs_1_.1), channel_id=1, source_target_pairs={{0,8},{1,5},{2,10},{3,7},{8,16},{9,1},{10,18},{11,3},{16,24},{17,9... | collective-permute-start | bytes 1179656 | tf_op jit(solution)/shard_map/ppermute | solution.py:315
  4.3 9.9 %collective-permute-start.5 = (bf16[1,3,128,512]{3,2,1,0:T(8,128)(2,1)S(1)}, bf16[1,3,128,512]{3,2,1,0:T(8,128)(2,1)S(1)}, u32[]{:S(2)}, u32[]{:S(2)}) collective-permute-start(bf16[1,3,128,512]{3,2,1,0:T(8,128)(2,1)S(1)} %collective-permute-done.refs_4_), channel_id=1, source_target_pairs={{0,8},{1,5},{2,10},{3,7},{8,16},{9,1},{10,18},{11,3},{16,24},{17,9... | collective-permute-start | bytes 1179656 | tf_op jit(solution)/shard_map/ppermute | solution.py:315
  9.4 8.4 %collective-permute-start.7 = (bf16[1,3,128,512]{3,2,1,0:T(8,128)(2,1)S(1)}, bf16[1,3,128,512]{3,2,1,0:T(8,128)(2,1)S(1)}, u32[]{:S(2)}, u32[]{:S(2)}) collective-permute-start(bf16[1,3,128,512]{3,2,1,0:T(8,128)(2,1)S(1)} %collective-permute-done.4.refs_0_), channel_id=1, source_target_pairs={{0,8},{1,5},{2,10},{3,7},{8,16},{9,1},{10,18},{11,3},{16,24},{17,9... | collective-permute-start | bytes 1179656 | tf_op jit(solution)/shard_map/ppermute | solution.py:315
  11.5 1.3 %collective-permute-start.2 = (s32[3,8]{1,0:T(4,128)S(1)}, s32[3,8]{1,0:T(4,128)S(1)}, u32[]{:S(2)}, u32[]{:S(2)}) collective-permute-start(s32[3,8]{1,0:T(4,128)S(1)} %bitcast.6), channel_id=1, source_target_pairs={{0,1},{1,0},{2,3},{3,2},{4,5},{5,4},{6,7},{7,6},{8,9},{9,8},{10,11... | collective-permute-start | bytes 296 | tf_op jit(solution)/shard_map/ppermute | solution.py:318
  11.5 1.3 %collective-permute-start.3 = (s32[4,3]{1,0:T(4,128)S(1)}, s32[4,3]{1,0:T(4,128)S(1)}, u32[]{:S(2)}, u32[]{:S(2)}) collective-permute-start(s32[4,3]{1,0:T(4,128)S(1)} %copy-done), channel_id=1, source_target_pairs={{0,1},{1,0},{2,3},{3,2},{4,5},{5,4},{6,7},{7,6},{8,9},{9,8},{10,11... | collective-permute-start | bytes 152 | tf_op jit(solution)/shard_map/ppermute | solution.py:318
  14.2 7.9 %collective-permute-start.8 = (bf16[1,3,128,512]{3,2,1,0:T(8,128)(2,1)S(1)}, bf16[1,3,128,512]{3,2,1,0:T(8,128)(2,1)S(1)}, u32[]{:S(2)}, u32[]{:S(2)}) collective-permute-start(bf16[1,3,128,512]{3,2,1,0:T(8,128)(2,1)S(1)} %collective-permute-done.5.refs_4_), channel_id=1, source_target_pairs={{0,8},{1,5},{2,10},{3,7},{8,16},{9,1},{10,18},{11,3},{16,24},{17,9... | collective-permute-start | bytes 1179656 | tf_op jit(solution)/shard_map/ppermute | solution.py:315
  17.9 8.4 %collective-permute-start.10 = (bf16[1,3,128,512]{3,2,1,0:T(8,128)(2,1)S(1)}, bf16[1,3,128,512]{3,2,1,0:T(8,128)(2,1)S(1)}, u32[]{:S(2)}, u32[]{:S(2)}) collective-permute-start(bf16[1,3,128,512]{3,2,1,0:T(8,128)(2,1)S(1)} %collective-permute-done.7.refs_0_), channel_id=1, source_target_pairs={{0,8},{1,5},{2,10},{3,7},{8,16},{9,1},{10,18},{11,3},{16,24},{17,9... | collective-permute-start | bytes 1179656 | tf_op jit(solution)/shard_map/ppermute | solution.py:315
  20.0 6.0 %collective-permute-start.6 = (s16[784,128]{1,0:T(8,128)(2,1)S(1)}, s16[784,128]{1,0:T(8,128)(2,1)S(1)}, u32[]{:S(2)}, u32[]{:S(2)}) collective-permute-start(s16[784,128]{1,0:T(8,128)(2,1)S(1)} %get-tuple-element.37), channel_id=1, source_target_pairs={{0,2},{1,3},{2,0},{3,1},{4,6},{5,7},{6,4},{7,5},{8,10},{9,11},{10,... | collective-permute-start | bytes 602120 | tf_op jit(solution)/shard_map/ppermute | solution.py:321
  22.1 8.4 %collective-permute-start.11 = (bf16[1,3,128,512]{3,2,1,0:T(8,128)(2,1)S(1)}, bf16[1,3,128,512]{3,2,1,0:T(8,128)(2,1)S(1)}, u32[]{:S(2)}, u32[]{:S(2)}) collective-permute-start(bf16[1,3,128,512]{3,2,1,0:T(8,128)(2,1)S(1)} %collective-permute-done.8.refs_4_), channel_id=1, source_target_pairs={{0,8},{1,5},{2,10},{3,7},{8,16},{9,1},{10,18},{11,3},{16,24},{17,9... | collective-permute-start | bytes 1179656 | tf_op jit(solution)/shard_map/ppermute | solution.py:315
  26.3 8.4 %collective-permute-start.13 = (bf16[1,3,128,512]{3,2,1,0:T(8,128)(2,1)S(1)}, bf16[1,3,128,512]{3,2,1,0:T(8,128)(2,1)S(1)}, u32[]{:S(2)}, u32[]{:S(2)}) collective-permute-start(bf16[1,3,128,512]{3,2,1,0:T(8,128)(2,1)S(1)} %collective-permute-done.10.refs_0_), channel_id=1, source_target_pairs={{0,8},{1,5},{2,10},{3,7},{8,16},{9,1},{10,18},{11,3},{16,24},{17,9... | collective-permute-start | bytes 1179656 | tf_op jit(solution)/shard_map/ppermute | solution.py:315
  28.4 5.0 %collective-permute-start.9 = (s16[528,128]{1,0:T(8,128)(2,1)S(1)}, s16[528,128]{1,0:T(8,128)(2,1)S(1)}, u32[]{:S(2)}, u32[]{:S(2)}) collective-permute-start(s16[528,128]{1,0:T(8,128)(2,1)S(1)} %get-tuple-element.40), channel_id=1, source_target_pairs={{0,2},{1,3},{2,0},{3,1},{4,6},{5,7},{6,4},{7,5},{8,10},{9,11},{10,... | collective-permute-start | bytes 405512 | tf_op jit(solution)/shard_map/ppermute | solution.py:321
  33.5 10.5 %collective-permute-start.16 = (f32[10,128,128]{2,1,0:T(8,128)S(1)}, f32[10,128,128]{2,1,0:T(8,128)S(1)}, u32[]{:S(2)}, u32[]{:S(2)}) collective-permute-start(f32[10,128,128]{2,1,0:T(8,128)S(1)} %shard_map.96.refs_0_), channel_id=1, source_target_pairs={{0,1},{1,0},{2,3},{3,2},{4,5},{5,4},{6,7},{7,6},{8,9},{9,8},{10,11... | collective-permute-start | bytes 1966088 | tf_op jit(solution)/shard_map/ppermute | solution.py:318
  34.7 2.2 %collective-permute-start.14 = (bf16[1,3,128,512]{3,2,1,0:T(8,128)(2,1)S(1)}, bf16[1,3,128,512]{3,2,1,0:T(8,128)(2,1)S(1)}, u32[]{:S(2)}, u32[]{:S(2)}) collective-permute-start(bf16[1,3,128,512]{3,2,1,0:T(8,128)(2,1)S(1)} %collective-permute-done.13.refs_0_), channel_id=1, source_target_pairs={{0,1},{1,0},{2,3},{3,2},{4,5},{5,4},{6,7},{7,6},{8,9},{9,8},{10,11... | collective-permute-start | bytes 1179656 | tf_op jit(solution)/shard_map/ppermute | solution.py:318
  34.7 6.2 %collective-permute-start.12 = (s16[528,128]{1,0:T(8,128)(2,1)S(1)}, s16[528,128]{1,0:T(8,128)(2,1)S(1)}, u32[]{:S(2)}, u32[]{:S(2)}) collective-permute-start(s16[528,128]{1,0:T(8,128)(2,1)S(1)} %get-tuple-element.44), channel_id=1, source_target_pairs={{0,2},{1,3},{2,0},{3,1},{4,6},{5,7},{6,4},{7,5},{8,10},{9,11},{10,... | collective-permute-start | bytes 405512 | tf_op jit(solution)/shard_map/ppermute | solution.py:321
  36.7 6.7 %collective-permute-start.17 = (f32[4,128,128]{2,1,0:T(8,128)S(1)}, f32[4,128,128]{2,1,0:T(8,128)S(1)}, u32[]{:S(2)}, u32[]{:S(2)}) collective-permute-start(f32[4,128,128]{2,1,0:T(8,128)S(1)} %get-tuple-element.42.refs_1_), channel_id=1, source_target_pairs={{0,1},{1,0},{2,3},{3,2},{4,5},{5,4},{6,7},{7,6},{8,9},{9,8},{10,11... | collective-permute-start | bytes 786440 | tf_op jit(solution)/shard_map/ppermute | solution.py:318
  38.3 4.4 %collective-permute-start.15 = (s16[272,128]{1,0:T(8,128)(2,1)S(1)}, s16[272,128]{1,0:T(8,128)(2,1)S(1)}, u32[]{:S(2)}, u32[]{:S(2)}) collective-permute-start(s16[272,128]{1,0:T(8,128)(2,1)S(1)} %get-tuple-element.48), channel_id=1, source_target_pairs={{0,2},{1,3},{2,0},{3,1},{4,6},{5,7},{6,4},{7,5},{8,10},{9,11},{10,... | collective-permute-start | bytes 208904 | tf_op jit(solution)/shard_map/ppermute | solution.py:321
  41.0 2.4 %collective-permute-start.18 = (s16[528,128]{1,0:T(8,128)(2,1)S(1)}, s16[528,128]{1,0:T(8,128)(2,1)S(1)}, u32[]{:S(2)}, u32[]{:S(2)}) collective-permute-start(s16[528,128]{1,0:T(8,128)(2,1)S(1)} %collective-permute-done.12.refs_2_), channel_id=1, source_target_pairs={{0,1},{1,0},{2,3},{3,2},{4,5},{5,4},{6,7},{7,6},{8,9},{9,8},{10,11... | collective-permute-start | bytes 405512 | tf_op jit(solution)/shard_map/ppermute | solution.py:318
  41.0 2.4 %collective-permute-start.19 = (f32[2,128,128]{2,1,0:T(8,128)S(1)}, f32[2,128,128]{2,1,0:T(8,128)S(1)}, u32[]{:S(2)}, u32[]{:S(2)}) collective-permute-start(f32[2,128,128]{2,1,0:T(8,128)S(1)} %get-tuple-element.47.refs_3_), channel_id=1, source_target_pairs={{0,1},{1,0},{2,3},{3,2},{4,5},{5,4},{6,7},{7,6},{8,9},{9,8},{10,11... | collective-permute-start | bytes 393224 | tf_op jit(solution)/shard_map/ppermute | solution.py:318
  42.7 1.3 %collective-permute-start.20 = (s16[272,128]{1,0:T(8,128)(2,1)S(1)}, s16[272,128]{1,0:T(8,128)(2,1)S(1)}, u32[]{:S(2)}, u32[]{:S(2)}) collective-permute-start(s16[272,128]{1,0:T(8,128)(2,1)S(1)} %collective-permute-done.15.refs_4_), channel_id=1, source_target_pairs={{0,1},{1,0},{2,3},{3,2},{4,5},{5,4},{6,7},{7,6},{8,9},{9,8},{10,11... | collective-permute-start | bytes 208904 | tf_op jit(solution)/shard_map/ppermute | solution.py:318

commit v4 on v3

--- a/solution.py
+++ b/solution.py
@@ -252,34 +252,56 @@
     )(*given)
 
 
-def spread_kernel(shards, blocks, counts, pair_eval_ref, pair_corpus_ref, pair_count_ref, scale_ref, *refs):
-    sums, (out_ref, table, staged, sem) = list(refs[:-4]), refs[-4:]
-    quarter = out_ref.shape[0]
+def steps_of(shards, blocks, side, steps):
     ring, far, half = ring_of(shards), shards // 2, blocks // 2
     place, way, core = ring_place(shards)
-    for side in range(2):
-        early, *late = sums[side * (len(sums) // 2) : (side + 1) * (len(sums) // 2)]
-        tiles = [early[q] for q in range(early.shape[0])] + list(joined(grouped(late, counts)))
-        at = 0
-        for step in range(far + 1):
-            e = look_up(ring, (place + (1 - 2 * side) * way * step + shards) % shards)
-            shared = step in (0, far)
-            for q in range(half if shared else blocks):
-                table[e * blocks + ((core ^ side) * half + q if shared else q)] = tiles[at]
-                at += 1
-    copies = []
-    group = 6 if quarter % 6 == 0 else quarter
+    for step in steps:
+        e = look_up(ring, (place + (1 - 2 * side) * way * step + shards) % shards)
+        shared = step in (0, far)
+        for q in range(half if shared else blocks):
+            yield e, (core ^ side) * half + q if shared else q
+
+
+def rows_of(blocks, pair_eval_ref, pair_corpus_ref, quarter):
     for p in range(quarter):
         slot = lax.axis_index("vocab") * quarter + p
-        row = pair_eval_ref[slot] * blocks + pair_corpus_ref[slot]
-        staged[p] = jnp.where(slot < pair_count_ref[0], table[row] * scale_ref[row], 0.0)
-        if (p + 1) % group == 0:
-            part = pl.ds(p + 1 - group, group)
-            copy = pltpu.make_async_copy(staged.at[part], out_ref.at[part], sem.at[p // group])
-            copy.start()
-            copies.append(copy)
-    for copy in copies:
-        copy.wait()
+        yield p, slot, pair_eval_ref[slot], pair_eval_ref[slot] * blocks + pair_corpus_ref[slot]
+
+
+def comes_late(shards, e):
+    ring, far = ring_of(shards), shards // 2
+    place, _, _ = ring_place(shards)
+    at = look_up([ring.index(c) for c in range(shards)], e)
+    distance = (at - place + shards) % shards
+    return (distance >= far - 1) & (distance <= far + 1)
+
+
+def table_kernel(shards, blocks, scale_ref, mine_ref, other_ref, table_ref):
+    for side, sums_ref in enumerate((mine_ref, other_ref)):
+        for at, (e, d) in enumerate(steps_of(shards, blocks, side, range(shards // 2 - 1))):
+            row = e * blocks + d
+            table_ref[row] = sums_ref[at] * scale_ref[row]
+
+
+def spread_kernel(shards, blocks, counts, pair_eval_ref, pair_corpus_ref, pair_count_ref, scale_ref, early_ref, *refs):
+    *sums, out_ref, table, zeros, sem = refs
+    quarter = out_ref.shape[0]
+    half = len(sums) // 2
+    zeros[...] = jnp.zeros_like(zeros)
+    slots = []
+    for p, slot, e, row in rows_of(blocks, pair_eval_ref, pair_corpus_ref, quarter):
+        live, late = slot < pair_count_ref[0], comes_late(shards, e)
+        slots.append((p, row, live & late))
+        pl.when(live & jnp.logical_not(late))(pltpu.make_async_copy(early_ref.at[row], out_ref.at[p], sem.at[p]).start)
+        pl.when(jnp.logical_not(live))(pltpu.make_async_copy(zeros, out_ref.at[p], sem.at[p]).start)
+    for side in range(2):
+        tiles = joined(grouped(sums[side * half : (side + 1) * half], counts))
+        for tile, (e, d) in zip(tiles, steps_of(shards, blocks, side, (shards // 2 - 1, shards // 2))):
+            table[e * blocks + d] = tile * scale_ref[e * blocks + d]
+    for p, row, late in slots:
+        pl.when(late)(pltpu.make_async_copy(table.at[row], out_ref.at[p], sem.at[p]).start)
+    for p in range(quarter):
+        pltpu.make_async_copy(zeros, out_ref.at[p], sem.at[p]).wait()
 
 
 def after(array, *others):
@@ -354,20 +376,29 @@
     last, last_code = work(far, True)
     parts.append([last, cross(last_code)])
     late = parts[-2:]
-    mine = [early] + [array for part in late for array in part]
+    early_other = swap(early)
+    table = jax.ShapeDtypeStruct((shards * blocks, rows, rows), jnp.float32)
+    cosines = pl.pallas_call(
+        functools.partial(table_kernel, shards, blocks),
+        out_shape=table,
+        in_specs=[VMEM] * 3,
+        out_specs=VMEM,
+        compiler_params=pltpu.CompilerParams(vmem_limit_bytes=LIMIT),
+    )(scale, early, early_other)
+    mine = [array for part in late for array in part]
     sums = mine + [swap(array) for array in mine]
     return pl.pallas_call(
         functools.partial(spread_kernel, shards, blocks, [len(part) for part in late]),
         out_shape=jax.ShapeDtypeStruct((quarter, rows, rows), jnp.float32),
-        in_specs=[SMEM] * 3 + [VMEM] * (1 + len(sums)),
+        in_specs=[SMEM] * 3 + [VMEM] * (2 + len(sums)),
         out_specs=pl.BlockSpec(memory_space=pl.ANY),
         scratch_shapes=[
-            pltpu.VMEM((shards * blocks, rows, rows), jnp.float32),
-            pltpu.VMEM((quarter, rows, rows), jnp.float32),
+            pltpu.VMEM(table.shape, jnp.float32),
+            pltpu.VMEM((rows, rows), jnp.float32),
             pltpu.SemaphoreType.DMA((quarter,)),
         ],
         compiler_params=pltpu.CompilerParams(vmem_limit_bytes=LIMIT),
-    )(pair_eval_block, pair_corpus_block, pair_count, scale, *sums)
+    )(pair_eval_block, pair_corpus_block, pair_count, scale, cosines, *sums)
 
 
 def solution(mesh):

time: 46.4 us -> 46.2 us (level)
  transfers between devices with their start and end apart: 21 -> 21, of which waited for: 12 -> 12; matrix products, arithmetic and copies ran while one was open for 0% -> 0% of each run, Pallas kernels for 21% -> 22%
where the time goes in v4:
time: 46.2 us; the launch traced here: 46 us
  starting transfers between devices  24.3 us (53%)
  Pallas kernels  12 us (26%)
  waiting for transfers between devices  8.9 us (19%)
  between operations  0.79 us (2%)
    ppermute x7, starting transfers between devices, move(): return lax.ppermute(block, ('corpus', 'vocab'), onward)  15.9 us
    pallas_call x5, Pallas kernels, dots(): pl.pallas_call(functools.partial(dots_kernel, tiles_slice, step, halved,...  7.91 us
    ppermute x4, starting transfers between devices, cross(): return lax.ppermute(array, 'vocab', to_chip)  6.53 us
    ppermute x4, waiting for transfers between devices, cross(): return lax.ppermute(array, 'vocab', to_chip)  3.47 us
    ppermute x7, waiting for transfers between devices, move(): return lax.ppermute(block, ('corpus', 'vocab'), onward)  3.47 us
    pallas_call x1, Pallas kernels, few_items(): pl.pallas_call(functools.partial(spread_kernel, shards, blocks, [len(part...  2.04 us
    ppermute x10, waiting for transfers between devices, swap(): return lax.ppermute(array, 'vocab', to_core)  1.96 us
    ppermute x10, starting transfers between devices, swap(): return lax.ppermute(array, 'vocab', to_core)  1.85 us
  transfers between devices with their start and end apart: 21, of which 12 were waited for; matrix products, arithmetic and copies ran while one was open for 0% of the time, Pallas kernels for 22%

profile of v4, /device:TPU:0, one launch (start us, length us, event | category | flops | bytes accessed | tf_op | source)
XLA Modules:
  0.0 46.0 jit_solution(16280429332806369334)
XLA Ops:
  0.0 0.5 collective-permute-start.1
  0.5 0.1 collective-permute-start
  0.5 3.0 %collective-permute-start.4 = (bf16[1,3,128,512]{3,2,1,0:T(8,128)(2,1)}, bf16[1,3,128,512]{3,2,1,0:T(8,128)(2,1)S(1)}, u32[]{:S(2)}, u32[]{:S(2)}) collective-permute-start(bf16[1,3,128,512]{3,2,1,0:T(8,128)(2,1)} %refs_1_.1), channel_id=1, source_target_pairs={{0,8},{1,5},{2,10},{3,7},{8,16},{9,1},{10,18},{11,3},{16,24},{17,9... | collective-permute-start | bytes 1179656 | tf_op jit(solution)/shard_map/ppermute | solution.py:337
  3.5 0.7 %collective-permute-done.refs_4_ = bf16[1,3,128,512]{3,2,1,0:T(8,128)(2,1)S(1)} collective-permute-done((bf16[1,3,128,512]{3,2,1,0:T(8,128)(2,1)}, bf16[1,3,128,512]{3,2,1,0:T(8,128)(2,1)S(1)}, u32[]{:S(2)}, u32[]{:S(2)}) %collective-permute-start) | collective-permute-done | bytes 393248 | tf_op jit(solution)/shard_map/ppermute | solution.py:340
  4.3 2.9 %collective-permute-start.5 = (bf16[1,3,128,512]{3,2,1,0:T(8,128)(2,1)S(1)}, bf16[1,3,128,512]{3,2,1,0:T(8,128)(2,1)S(1)}, u32[]{:S(2)}, u32[]{:S(2)}) collective-permute-start(bf16[1,3,128,512]{3,2,1,0:T(8,128)(2,1)S(1)} %collective-permute-done.refs_4_), channel_id=1, source_target_pairs={{0,8},{1,5},{2,10},{3,7},{8,16},{9,1},{10,18},{11,3},{16,24},{17,9... | collective-permute-start | bytes 1179656 | tf_op jit(solution)/shard_map/ppermute | solution.py:337
  7.2 1.8 %shard_map.91 = (bf16[4,3,128,512]{3,2,1,0:T(8,128)(2,1)S(1)}, bf16[1,3,128,512]{3,2,1,0:T(8,128)(2,1)S(1)}, s32[3,8]{1,0:T(4,128)S(1)}, s32[4,3]{1,0:T(4,128)S(...) custom-call(bf16[4,3,128,512]{3,2,1,0:T(8,128)(2,1)} %refs_0_.1, bf16[1,3,128,512]{3,2,1,0:T(8,128)(2,1)} %refs_1_.1, ...), custom_call_target="tpu_custom_call" | custom-call | tf_op jit(solution)/shard_map/pallas_call | solution.py:240
  9.1 0.4 collective-permute-done.4.refs_0_
  9.4 2.1 %collective-permute-start.7 = (bf16[1,3,128,512]{3,2,1,0:T(8,128)(2,1)S(1)}, bf16[1,3,128,512]{3,2,1,0:T(8,128)(2,1)S(1)}, u32[]{:S(2)}, u32[]{:S(2)}) collective-permute-start(bf16[1,3,128,512]{3,2,1,0:T(8,128)(2,1)S(1)} %collective-permute-done.4.refs_0_), channel_id=1, source_target_pairs={{0,8},{1,5},{2,10},{3,7},{8,16},{9,1},{10,18},{11,3},{16,24},{17,9... | collective-permute-start | bytes 1179656 | tf_op jit(solution)/shard_map/ppermute | solution.py:337
  11.5 0.0 collective-permute-start.2
  11.5 0.5 %collective-permute-start.3 = (s32[4,3]{1,0:T(4,128)S(1)}, s32[4,3]{1,0:T(4,128)S(1)}, u32[]{:S(2)}, u32[]{:S(2)}) collective-permute-start(s32[4,3]{1,0:T(4,128)S(1)} %copy-done), channel_id=1, source_target_pairs={{0,1},{1,0},{2,3},{3,2},{4,5},{5,4},{6,7},{7,6},{8,9},{9,8},{10,11... | collective-permute-start | bytes 152 | tf_op jit(solution)/shard_map/ppermute | solution.py:340
  12.0 0.8 %collective-permute-done.3.refs_7_ = s32[4,3]{1,0:T(4,128)S(1)} collective-permute-done((s32[4,3]{1,0:T(4,128)S(1)}, s32[4,3]{1,0:T(4,128)S(1)}, u32[]{:S(2)}, u32[]{:S(2)}) %collective-permute-start.3) | collective-permute-done | bytes 80 | tf_op jit(solution)/shard_map/ppermute | solution.py:340
  12.9 0.0 collective-permute-done.2.refs_6_
  12.9 0.0 collective-permute-done.1.refs_5_
  12.9 1.3 %shard_map.92.refs_8_.refs_0_ = f32[2,128,128]{2,1,0:T(8,128)S(1)} custom-call(bf16[1,3,128,512]{3,2,1,0:T(8,128)(2,1)S(1)} %get-tuple-element.30.refs_0_, bf16[4,3,128,512]{3,2,1,0:T(8,128)(2,1)S(1)} %get-tuple-element.31.refs_1_, s32[3,8]{1,0:T(4,128)S(1)} %get-tuple-element.32.refs_2_, s32[4,3]{1,0:T(4,128)S(1)} %get-tuple-element.33.refs_3_, ...), custom_call_target="tpu_custom_call" | custom-call | flops 201326592 | bytes 3932160 | tf_op jit(solution)/shard_map/pallas_call | solution.py:170
  14.2 1.6 %collective-permute-start.8 = (bf16[1,3,128,512]{3,2,1,0:T(8,128)(2,1)S(1)}, bf16[1,3,128,512]{3,2,1,0:T(8,128)(2,1)S(1)}, u32[]{:S(2)}, u32[]{:S(2)}) collective-permute-start(bf16[1,3,128,512]{3,2,1,0:T(8,128)(2,1)S(1)} %collective-permute-done.5.refs_4_), channel_id=1, source_target_pairs={{0,8},{1,5},{2,10},{3,7},{8,16},{9,1},{10,18},{11,3},{16,24},{17,9... | collective-permute-start | bytes 1179656 | tf_op jit(solution)/shard_map/ppermute | solution.py:337
  15.8 1.8 %shard_map.93 = (f32[4,128,128]{2,1,0:T(8,128)S(1)}, s16[784,128]{1,0:T(8,128)(2,1)S(1)}) custom-call(bf16[1,3,128,512]{3,2,1,0:T(8,128)(2,1)S(1)} %collective-permute-done.4.refs_0_, bf16[4,3,128,512]{3,2,1,0:T(8,128)(2,1)S(1)} %get-tuple-element.31.refs_1_, s32[3,8]{1,0:T(4,128)S(1)} %get-tuple-element.32.refs_2_, s32[4,3]{1,0:T(4,128)S(1)} %get-tuple-element.33.refs_3_, ...), custom_call_target="tpu_custom_call" | custom-call | flops 402653184 | bytes 3932160 | tf_op jit(solution)/shard_map/pallas_call | solution.py:170
  17.6 0.3 collective-permute-done.7.refs_0_
  17.9 2.1 %collective-permute-start.10 = (bf16[1,3,128,512]{3,2,1,0:T(8,128)(2,1)S(1)}, bf16[1,3,128,512]{3,2,1,0:T(8,128)(2,1)S(1)}, u32[]{:S(2)}, u32[]{:S(2)}) collective-permute-start(bf16[1,3,128,512]{3,2,1,0:T(8,128)(2,1)S(1)} %collective-permute-done.7.refs_0_), channel_id=1, source_target_pairs={{0,8},{1,5},{2,10},{3,7},{8,16},{9,1},{10,18},{11,3},{16,24},{17,9... | collective-permute-start | bytes 1179656 | tf_op jit(solution)/shard_map/ppermute | solution.py:337
  20.0 1.5 %collective-permute-start.6 = (s16[784,128]{1,0:T(8,128)(2,1)S(1)}, s16[784,128]{1,0:T(8,128)(2,1)S(1)}, u32[]{:S(2)}, u32[]{:S(2)}) collective-permute-start(s16[784,128]{1,0:T(8,128)(2,1)S(1)} %get-tuple-element.37), channel_id=1, source_target_pairs={{0,2},{1,3},{2,0},{3,1},{4,6},{5,7},{6,4},{7,5},{8,10},{9,11},{10,... | collective-permute-start | bytes 602120 | tf_op jit(solution)/shard_map/ppermute | solution.py:343
  21.4 0.6 %collective-permute-done.8.refs_4_ = bf16[1,3,128,512]{3,2,1,0:T(8,128)(2,1)S(1)} collective-permute-done((bf16[1,3,128,512]{3,2,1,0:T(8,128)(2,1)S(1)}, bf16[1,3,128,512]{3,2,1,0:T(8,128)(2,1)S(1)}, u32[]{:S(2)}, u32[]{:S(2)}) %collective-permute-start.8) | collective-permute-done | bytes 393248 | tf_op jit(solution)/shard_map/ppermute | solution.py:337
  22.1 2.1 %collective-permute-start.11 = (bf16[1,3,128,512]{3,2,1,0:T(8,128)(2,1)S(1)}, bf16[1,3,128,512]{3,2,1,0:T(8,128)(2,1)S(1)}, u32[]{:S(2)}, u32[]{:S(2)}) collective-permute-start(bf16[1,3,128,512]{3,2,1,0:T(8,128)(2,1)S(1)} %collective-permute-done.8.refs_4_), channel_id=1, source_target_pairs={{0,8},{1,5},{2,10},{3,7},{8,16},{9,1},{10,18},{11,3},{16,24},{17,9... | collective-permute-start | bytes 1179656 | tf_op jit(solution)/shard_map/ppermute | solution.py:337
  24.2 1.8 %shard_map.94 = (f32[4,128,128]{2,1,0:T(8,128)S(1)}, s16[528,128]{1,0:T(8,128)(2,1)S(1)}) custom-call(bf16[1,3,128,512]{3,2,1,0:T(8,128)(2,1)S(1)} %collective-permute-done.7.refs_0_, bf16[4,3,128,512]{3,2,1,0:T(8,128)(2,1)S(1)} %get-tuple-element.31.refs_1_, s32[3,8]{1,0:T(4,128)S(1)} %get-tuple-element.32.refs_2_, s32[4,3]{1,0:T(4,128)S(1)} %get-tuple-element.33.refs_3_, ...), custom_call_target="tpu_custom_call" | custom-call | flops 402653184 | bytes 3932160 | tf_op jit(solution)/shard_map/pallas_call | solution.py:170
  25.9 0.0 collective-permute-done.6.refs_2_
  26.0 0.3 collective-permute-done.10.refs_0_
  26.3 2.1 %collective-permute-start.14 = (bf16[1,3,128,512]{3,2,1,0:T(8,128)(2,1)S(1)}, bf16[1,3,128,512]{3,2,1,0:T(8,128)(2,1)S(1)}, u32[]{:S(2)}, u32[]{:S(2)}) collective-permute-start(bf16[1,3,128,512]{3,2,1,0:T(8,128)(2,1)S(1)} %collective-permute-done.10.refs_0_), channel_id=1, source_target_pairs={{0,8},{1,5},{2,10},{3,7},{8,16},{9,1},{10,18},{11,3},{16,24},{17,9... | collective-permute-start | bytes 1179656 | tf_op jit(solution)/shard_map/ppermute | solution.py:337
  28.4 1.5 %collective-permute-start.9 = (s16[528,128]{1,0:T(8,128)(2,1)S(1)}, s16[528,128]{1,0:T(8,128)(2,1)S(1)}, u32[]{:S(2)}, u32[]{:S(2)}) collective-permute-start(s16[528,128]{1,0:T(8,128)(2,1)S(1)} %get-tuple-element.40), channel_id=1, source_target_pairs={{0,2},{1,3},{2,0},{3,1},{4,6},{5,7},{6,4},{7,5},{8,10},{9,11},{10,... | collective-permute-start | bytes 405512 | tf_op jit(solution)/shard_map/ppermute | solution.py:343
  29.9 0.6 %collective-permute-done.11.refs_4_ = bf16[1,3,128,512]{3,2,1,0:T(8,128)(2,1)S(1)} collective-permute-done((bf16[1,3,128,512]{3,2,1,0:T(8,128)(2,1)S(1)}, bf16[1,3,128,512]{3,2,1,0:T(8,128)(2,1)S(1)}, u32[]{:S(2)}, u32[]{:S(2)}) %collective-permute-start.11) | collective-permute-done | bytes 393248 | tf_op jit(solution)/shard_map/ppermute | solution.py:337
  30.5 1.8 %shard_map.95 = (f32[4,128,128]{2,1,0:T(8,128)S(1)}, s16[528,128]{1,0:T(8,128)(2,1)S(1)}) custom-call(bf16[1,3,128,512]{3,2,1,0:T(8,128)(2,1)S(1)} %collective-permute-done.10.refs_0_, bf16[4,3,128,512]{3,2,1,0:T(8,128)(2,1)S(1)} %get-tuple-element.31.refs_1_, s32[3,8]{1,0:T(4,128)S(1)} %get-tuple-element.32.refs_2_, s32[4,3]{1,0:T(4,128)S(1)} %get-tuple-element.33.refs_3_, ...), custom_call_target="tpu_custom_call" | custom-call | flops 402653184 | bytes 3932160 | tf_op jit(solution)/shard_map/pallas_call | solution.py:170
  32.3 1.1 %collective-permute-done.9.refs_4_ = s16[528,128]{1,0:T(8,128)(2,1)S(1)} collective-permute-done((s16[528,128]{1,0:T(8,128)(2,1)S(1)}, s16[528,128]{1,0:T(8,128)(2,1)S(1)}, u32[]{:S(2)}, u32[]{:S(2)}) %collective-permute-start.9) | collective-permute-done | bytes 135200 | tf_op jit(solution)/shard_map/ppermute | solution.py:343
  33.4 0.1 shard_map.96.mine_ref
  33.5 0.1 collective-permute-start.12
  33.6 1.2 %collective-permute-done.14.refs_0_ = bf16[1,3,128,512]{3,2,1,0:T(8,128)(2,1)S(1)} collective-permute-done((bf16[1,3,128,512]{3,2,1,0:T(8,128)(2,1)S(1)}, bf16[1,3,128,512]{3,2,1,0:T(8,128)(2,1)S(1)}, u32[]{:S(2)}, u32[]{:S(2)}) %collective-permute-start.14) | collective-permute-done | bytes 393248 | tf_op jit(solution)/shard_map/ppermute | solution.py:337
  34.7 0.0 collective-permute-start.15
  34.7 2.0 %collective-permute-start.13 = (s16[528,128]{1,0:T(8,128)(2,1)S(1)}, s16[528,128]{1,0:T(8,128)(2,1)S(1)}, u32[]{:S(2)}, u32[]{:S(2)}) collective-permute-start(s16[528,128]{1,0:T(8,128)(2,1)S(1)} %get-tuple-element.44), channel_id=1, source_target_pairs={{0,2},{1,3},{2,0},{3,1},{4,6},{5,7},{6,4},{7,5},{8,10},{9,11},{10,... | collective-permute-start | bytes 405512 | tf_op jit(solution)/shard_map/ppermute | solution.py:343
  36.7 0.2 collective-permute-start.17
  37.0 0.0 collective-permute-done.15.refs_4_
  37.0 1.3 %shard_map.98 = (f32[2,128,128]{2,1,0:T(8,128)S(1)}, s16[272,128]{1,0:T(8,128)(2,1)S(1)}) custom-call(bf16[1,3,128,512]{3,2,1,0:T(8,128)(2,1)S(1)} %collective-permute-done.14.refs_0_, bf16[4,3,128,512]{3,2,1,0:T(8,128)(2,1)S(1)} %get-tuple-element.31.refs_1_, s32[3,8]{1,0:T(4,128)S(1)} %get-tuple-element.32.refs_2_, s32[4,3]{1,0:T(4,128)S(1)} %get-tuple-element.33.refs_3_, ...), custom_call_target="tpu_custom_call" | custom-call | flops 201326592 | bytes 3932160 | tf_op jit(solution)/shard_map/pallas_call | solution.py:170
  38.3 1.6 %collective-permute-start.16 = (s16[272,128]{1,0:T(8,128)(2,1)S(1)}, s16[272,128]{1,0:T(8,128)(2,1)S(1)}, u32[]{:S(2)}, u32[]{:S(2)}) collective-permute-start(s16[272,128]{1,0:T(8,128)(2,1)S(1)} %get-tuple-element.48), channel_id=1, source_target_pairs={{0,2},{1,3},{2,0},{3,1},{4,6},{5,7},{6,4},{7,5},{8,10},{9,11},{10,... | collective-permute-start | bytes 208904 | tf_op jit(solution)/shard_map/ppermute | solution.py:343
  39.8 1.1 %collective-permute-done.13.refs_1_ = s16[528,128]{1,0:T(8,128)(2,1)S(1)} collective-permute-done((s16[528,128]{1,0:T(8,128)(2,1)S(1)}, s16[528,128]{1,0:T(8,128)(2,1)S(1)}, u32[]{:S(2)}, u32[]{:S(2)}) %collective-permute-start.13) | collective-permute-done | bytes 135200 | tf_op jit(solution)/shard_map/ppermute | solution.py:343
  41.0 0.0 collective-permute-start.18
  41.0 0.5 %collective-permute-start.19 = (f32[2,128,128]{2,1,0:T(8,128)S(1)}, f32[2,128,128]{2,1,0:T(8,128)S(1)}, u32[]{:S(2)}, u32[]{:S(2)}) collective-permute-start(f32[2,128,128]{2,1,0:T(8,128)S(1)} %get-tuple-element.47.refs_2_), channel_id=1, source_target_pairs={{0,1},{1,0},{2,3},{3,2},{4,5},{5,4},{6,7},{7,6},{8,9},{9,8},{10,11... | collective-permute-start | bytes 393224 | tf_op jit(solution)/shard_map/ppermute | solution.py:340
  41.5 1.2 %collective-permute-done.16.refs_3_ = s16[272,128]{1,0:T(8,128)(2,1)S(1)} collective-permute-done((s16[272,128]{1,0:T(8,128)(2,1)S(1)}, s16[272,128]{1,0:T(8,128)(2,1)S(1)}, u32[]{:S(2)}, u32[]{:S(2)}) %collective-permute-start.16) | collective-permute-done | bytes 69664 | tf_op jit(solution)/shard_map/ppermute | solution.py:343
  42.7 0.0 collective-permute-start.20
  43.4 0.2 shard_map.97.early_ref
  43.6 0.0 collective-permute-done.17.refs_4_
  43.6 0.0 collective-permute-done.18.refs_5_
  43.6 0.4 collective-permute-done.20.refs_7_
  44.0 2.0 %shard_map.99 = f32[24,128,128]{2,1,0:T(8,128)} custom-call(s32[96]{0:T(128)S(1)} %get-tuple-element.27.pair_eval_ref, s32[96]{0:T(128)S(1)} %get-tuple-element.28.pair_corpus_ref, s32[1]{0:T(128)S(6)} %copy.10.pair_count_ref, f32[32,128,128]{2,1,0:T(8,128)S(1)} %get-tuple-element.29.scale_ref, f32[32,128,128]{2,1,0:T(8,128)S(1)} %shard_map.97.early_ref, ...), custom_call_target="tpu_custom_call" | custom-call | tf_op jit(solution)/shard_map/pallas_call | solution.py:390
  (7 shorter events, 0.0 us)
Async XLA Ops:
  0.0 11.5 %copy-start.1 = (s32[8,3]{0,1:T(4,128)S(1)}, s32[8,3]{0,1:T(4,128)}, u32[]{:S(2)}) copy-start(s32[8,3]{0,1:T(4,128)} %param.10) | copy-start | bytes 292
  0.0 11.5 %copy-start = (s32[4,3]{1,0:T(4,128)S(1)}, s32[4,3]{1,0:T(4,128)}, u32[]{:S(2)}) copy-start(s32[4,3]{1,0:T(4,128)} %refs_3_.1) | copy-start | bytes 148
  0.0 12.9 %collective-permute-start.1 = (bf16[4,3,128,512]{3,2,1,0:T(8,128)(2,1)}, bf16[4,3,128,512]{3,2,1,0:T(8,128)(2,1)S(1)}, u32[]{:S(2)}, u32[]{:S(2)}) collective-permute-start(bf16[4,3,128,512]{3,2,1,0:T(8,128)(2,1)} %refs_0_.1), channel_id=1, source_target_pairs={{0,1},{1,0},{2,3},{3,2},{4,5},{5,4},{6,7},{7,6},{8,9},{9,8},{10,11... | collective-permute-start | bytes 4718600 | tf_op jit(solution)/shard_map/ppermute | solution.py:340
  0.5 3.8 %collective-permute-start = (bf16[1,3,128,512]{3,2,1,0:T(8,128)(2,1)}, bf16[1,3,128,512]{3,2,1,0:T(8,128)(2,1)S(1)}, u32[]{:S(2)}, u32[]{:S(2)}) collective-permute-start(bf16[1,3,128,512]{3,2,1,0:T(8,128)(2,1)} %refs_1_.1), channel_id=1, source_target_pairs={{0,1},{1,0},{2,3},{3,2},{4,5},{5,4},{6,7},{7,6},{8,9},{9,8},{10,11... | collective-permute-start | bytes 1179656 | tf_op jit(solution)/shard_map/ppermute | solution.py:340
  0.5 8.9 %collective-permute-start.4 = (bf16[1,3,128,512]{3,2,1,0:T(8,128)(2,1)}, bf16[1,3,128,512]{3,2,1,0:T(8,128)(2,1)S(1)}, u32[]{:S(2)}, u32[]{:S(2)}) collective-permute-start(bf16[1,3,128,512]{3,2,1,0:T(8,128)(2,1)} %refs_1_.1), channel_id=1, source_target_pairs={{0,8},{1,5},{2,10},{3,7},{8,16},{9,1},{10,18},{11,3},{16,24},{17,9... | collective-permute-start | bytes 1179656 | tf_op jit(solution)/shard_map/ppermute | solution.py:337
  4.3 9.9 %collective-permute-start.5 = (bf16[1,3,128,512]{3,2,1,0:T(8,128)(2,1)S(1)}, bf16[1,3,128,512]{3,2,1,0:T(8,128)(2,1)S(1)}, u32[]{:S(2)}, u32[]{:S(2)}) collective-permute-start(bf16[1,3,128,512]{3,2,1,0:T(8,128)(2,1)S(1)} %collective-permute-done.refs_4_), channel_id=1, source_target_pairs={{0,8},{1,5},{2,10},{3,7},{8,16},{9,1},{10,18},{11,3},{16,24},{17,9... | collective-permute-start | bytes 1179656 | tf_op jit(solution)/shard_map/ppermute | solution.py:337
  9.4 8.4 %collective-permute-start.7 = (bf16[1,3,128,512]{3,2,1,0:T(8,128)(2,1)S(1)}, bf16[1,3,128,512]{3,2,1,0:T(8,128)(2,1)S(1)}, u32[]{:S(2)}, u32[]{:S(2)}) collective-permute-start(bf16[1,3,128,512]{3,2,1,0:T(8,128)(2,1)S(1)} %collective-permute-done.4.refs_0_), channel_id=1, source_target_pairs={{0,8},{1,5},{2,10},{3,7},{8,16},{9,1},{10,18},{11,3},{16,24},{17,9... | collective-permute-start | bytes 1179656 | tf_op jit(solution)/shard_map/ppermute | solution.py:337
  11.5 1.3 %collective-permute-start.2 = (s32[3,8]{1,0:T(4,128)S(1)}, s32[3,8]{1,0:T(4,128)S(1)}, u32[]{:S(2)}, u32[]{:S(2)}) collective-permute-start(s32[3,8]{1,0:T(4,128)S(1)} %bitcast.6), channel_id=1, source_target_pairs={{0,1},{1,0},{2,3},{3,2},{4,5},{5,4},{6,7},{7,6},{8,9},{9,8},{10,11... | collective-permute-start | bytes 296 | tf_op jit(solution)/shard_map/ppermute | solution.py:340
  11.5 1.3 %collective-permute-start.3 = (s32[4,3]{1,0:T(4,128)S(1)}, s32[4,3]{1,0:T(4,128)S(1)}, u32[]{:S(2)}, u32[]{:S(2)}) collective-permute-start(s32[4,3]{1,0:T(4,128)S(1)} %copy-done), channel_id=1, source_target_pairs={{0,1},{1,0},{2,3},{3,2},{4,5},{5,4},{6,7},{7,6},{8,9},{9,8},{10,11... | collective-permute-start | bytes 152 | tf_op jit(solution)/shard_map/ppermute | solution.py:340
  14.2 7.9 %collective-permute-start.8 = (bf16[1,3,128,512]{3,2,1,0:T(8,128)(2,1)S(1)}, bf16[1,3,128,512]{3,2,1,0:T(8,128)(2,1)S(1)}, u32[]{:S(2)}, u32[]{:S(2)}) collective-permute-start(bf16[1,3,128,512]{3,2,1,0:T(8,128)(2,1)S(1)} %collective-permute-done.5.refs_4_), channel_id=1, source_target_pairs={{0,8},{1,5},{2,10},{3,7},{8,16},{9,1},{10,18},{11,3},{16,24},{17,9... | collective-permute-start | bytes 1179656 | tf_op jit(solution)/shard_map/ppermute | solution.py:337
  17.9 8.4 %collective-permute-start.10 = (bf16[1,3,128,512]{3,2,1,0:T(8,128)(2,1)S(1)}, bf16[1,3,128,512]{3,2,1,0:T(8,128)(2,1)S(1)}, u32[]{:S(2)}, u32[]{:S(2)}) collective-permute-start(bf16[1,3,128,512]{3,2,1,0:T(8,128)(2,1)S(1)} %collective-permute-done.7.refs_0_), channel_id=1, source_target_pairs={{0,8},{1,5},{2,10},{3,7},{8,16},{9,1},{10,18},{11,3},{16,24},{17,9... | collective-permute-start | bytes 1179656 | tf_op jit(solution)/shard_map/ppermute | solution.py:337
  20.0 6.0 %collective-permute-start.6 = (s16[784,128]{1,0:T(8,128)(2,1)S(1)}, s16[784,128]{1,0:T(8,128)(2,1)S(1)}, u32[]{:S(2)}, u32[]{:S(2)}) collective-permute-start(s16[784,128]{1,0:T(8,128)(2,1)S(1)} %get-tuple-element.37), channel_id=1, source_target_pairs={{0,2},{1,3},{2,0},{3,1},{4,6},{5,7},{6,4},{7,5},{8,10},{9,11},{10,... | collective-permute-start | bytes 602120 | tf_op jit(solution)/shard_map/ppermute | solution.py:343
  22.1 8.4 %collective-permute-start.11 = (bf16[1,3,128,512]{3,2,1,0:T(8,128)(2,1)S(1)}, bf16[1,3,128,512]{3,2,1,0:T(8,128)(2,1)S(1)}, u32[]{:S(2)}, u32[]{:S(2)}) collective-permute-start(bf16[1,3,128,512]{3,2,1,0:T(8,128)(2,1)S(1)} %collective-permute-done.8.refs_4_), channel_id=1, source_target_pairs={{0,8},{1,5},{2,10},{3,7},{8,16},{9,1},{10,18},{11,3},{16,24},{17,9... | collective-permute-start | bytes 1179656 | tf_op jit(solution)/shard_map/ppermute | solution.py:337
  26.3 8.4 %collective-permute-start.14 = (bf16[1,3,128,512]{3,2,1,0:T(8,128)(2,1)S(1)}, bf16[1,3,128,512]{3,2,1,0:T(8,128)(2,1)S(1)}, u32[]{:S(2)}, u32[]{:S(2)}) collective-permute-start(bf16[1,3,128,512]{3,2,1,0:T(8,128)(2,1)S(1)} %collective-permute-done.10.refs_0_), channel_id=1, source_target_pairs={{0,8},{1,5},{2,10},{3,7},{8,16},{9,1},{10,18},{11,3},{16,24},{17,9... | collective-permute-start | bytes 1179656 | tf_op jit(solution)/shard_map/ppermute | solution.py:337
  28.4 5.0 %collective-permute-start.9 = (s16[528,128]{1,0:T(8,128)(2,1)S(1)}, s16[528,128]{1,0:T(8,128)(2,1)S(1)}, u32[]{:S(2)}, u32[]{:S(2)}) collective-permute-start(s16[528,128]{1,0:T(8,128)(2,1)S(1)} %get-tuple-element.40), channel_id=1, source_target_pairs={{0,2},{1,3},{2,0},{3,1},{4,6},{5,7},{6,4},{7,5},{8,10},{9,11},{10,... | collective-permute-start | bytes 405512 | tf_op jit(solution)/shard_map/ppermute | solution.py:343
  33.5 9.9 %collective-permute-start.12 = (f32[10,128,128]{2,1,0:T(8,128)S(1)}, f32[10,128,128]{2,1,0:T(8,128)S(1)}, u32[]{:S(2)}, u32[]{:S(2)}) collective-permute-start(f32[10,128,128]{2,1,0:T(8,128)S(1)} %shard_map.96.mine_ref), channel_id=1, source_target_pairs={{0,1},{1,0},{2,3},{3,2},{4,5},{5,4},{6,7},{7,6},{8,9},{9,8},{10,11... | collective-permute-start | bytes 1966088 | tf_op jit(solution)/shard_map/ppermute | solution.py:340
  34.7 2.2 %collective-permute-start.15 = (bf16[1,3,128,512]{3,2,1,0:T(8,128)(2,1)S(1)}, bf16[1,3,128,512]{3,2,1,0:T(8,128)(2,1)S(1)}, u32[]{:S(2)}, u32[]{:S(2)}) collective-permute-start(bf16[1,3,128,512]{3,2,1,0:T(8,128)(2,1)S(1)} %collective-permute-done.14.refs_0_), channel_id=1, source_target_pairs={{0,1},{1,0},{2,3},{3,2},{4,5},{5,4},{6,7},{7,6},{8,9},{9,8},{10,11... | collective-permute-start | bytes 1179656 | tf_op jit(solution)/shard_map/ppermute | solution.py:340
  34.7 6.2 %collective-permute-start.13 = (s16[528,128]{1,0:T(8,128)(2,1)S(1)}, s16[528,128]{1,0:T(8,128)(2,1)S(1)}, u32[]{:S(2)}, u32[]{:S(2)}) collective-permute-start(s16[528,128]{1,0:T(8,128)(2,1)S(1)} %get-tuple-element.44), channel_id=1, source_target_pairs={{0,2},{1,3},{2,0},{3,1},{4,6},{5,7},{6,4},{7,5},{8,10},{9,11},{10,... | collective-permute-start | bytes 405512 | tf_op jit(solution)/shard_map/ppermute | solution.py:343
  36.7 6.8 %collective-permute-start.17 = (f32[4,128,128]{2,1,0:T(8,128)S(1)}, f32[4,128,128]{2,1,0:T(8,128)S(1)}, u32[]{:S(2)}, u32[]{:S(2)}) collective-permute-start(f32[4,128,128]{2,1,0:T(8,128)S(1)} %get-tuple-element.42.refs_0_), channel_id=1, source_target_pairs={{0,1},{1,0},{2,3},{3,2},{4,5},{5,4},{6,7},{7,6},{8,9},{9,8},{10,11... | collective-permute-start | bytes 786440 | tf_op jit(solution)/shard_map/ppermute | solution.py:340
  38.3 4.4 %collective-permute-start.16 = (s16[272,128]{1,0:T(8,128)(2,1)S(1)}, s16[272,128]{1,0:T(8,128)(2,1)S(1)}, u32[]{:S(2)}, u32[]{:S(2)}) collective-permute-start(s16[272,128]{1,0:T(8,128)(2,1)S(1)} %get-tuple-element.48), channel_id=1, source_target_pairs={{0,2},{1,3},{2,0},{3,1},{4,6},{5,7},{6,4},{7,5},{8,10},{9,11},{10,... | collective-permute-start | bytes 208904 | tf_op jit(solution)/shard_map/ppermute | solution.py:343
  41.0 2.6 %collective-permute-start.18 = (s16[528,128]{1,0:T(8,128)(2,1)S(1)}, s16[528,128]{1,0:T(8,128)(2,1)S(1)}, u32[]{:S(2)}, u32[]{:S(2)}) collective-permute-start(s16[528,128]{1,0:T(8,128)(2,1)S(1)} %collective-permute-done.13.refs_1_), channel_id=1, source_target_pairs={{0,1},{1,0},{2,3},{3,2},{4,5},{5,4},{6,7},{7,6},{8,9},{9,8},{10,11... | collective-permute-start | bytes 405512 | tf_op jit(solution)/shard_map/ppermute | solution.py:340
  41.0 2.6 %collective-permute-start.19 = (f32[2,128,128]{2,1,0:T(8,128)S(1)}, f32[2,128,128]{2,1,0:T(8,128)S(1)}, u32[]{:S(2)}, u32[]{:S(2)}) collective-permute-start(f32[2,128,128]{2,1,0:T(8,128)S(1)} %get-tuple-element.47.refs_2_), channel_id=1, source_target_pairs={{0,1},{1,0},{2,3},{3,2},{4,5},{5,4},{6,7},{7,6},{8,9},{9,8},{10,11... | collective-permute-start | bytes 393224 | tf_op jit(solution)/shard_map/ppermute | solution.py:340
  42.7 1.3 %collective-permute-start.20 = (s16[272,128]{1,0:T(8,128)(2,1)S(1)}, s16[272,128]{1,0:T(8,128)(2,1)S(1)}, u32[]{:S(2)}, u32[]{:S(2)}) collective-permute-start(s16[272,128]{1,0:T(8,128)(2,1)S(1)} %collective-permute-done.16.refs_3_), channel_id=1, source_target_pairs={{0,1},{1,0},{2,3},{3,2},{4,5},{5,4},{6,7},{7,6},{8,9},{9,8},{10,11... | collective-permute-start | bytes 208904 | tf_op jit(solution)/shard_map/ppermute | solution.py:340

commit v5 on v4

--- a/solution.py
+++ b/solution.py
@@ -193,23 +193,31 @@
     return [[refs.pop(0) for _ in range(count)] for count in counts]
 
 
-def join_kernel(counts, *refs):
-    *refs, out_ref = refs
+def join_kernel(shards, blocks, counts, pair_eval_ref, pair_corpus_ref, pair_count_ref, *refs):
+    *refs, out_ref, slot_ref = refs
     for q, tile in enumerate(joined(grouped(refs, counts))):
         out_ref[q] = tile
-
-
-def join(parts):
+    quarter = slot_ref.shape[0]
+    for p in range(quarter):
+        slot = lax.axis_index("vocab") * quarter + p
+        row = pair_eval_ref[slot] * blocks + pair_corpus_ref[slot]
+        slot_ref[p] = jnp.where(slot < pair_count_ref[0], row, shards * blocks)
+
+
+def join(shards, blocks, quarter, pairs, parts):
     arrays = [array for part in parts for array in part]
     tiles = [array for part in parts for array in part[:-1]]
     count = sum(array.shape[0] for array in tiles)
     return pl.pallas_call(
-        functools.partial(join_kernel, [len(part) for part in parts]),
-        out_shape=jax.ShapeDtypeStruct((count, *tiles[0].shape[1:]), jnp.float32),
-        in_specs=[VMEM] * len(arrays),
-        out_specs=VMEM,
+        functools.partial(join_kernel, shards, blocks, [len(part) for part in parts]),
+        out_shape=(
+            jax.ShapeDtypeStruct((count, *tiles[0].shape[1:]), jnp.float32),
+            jax.ShapeDtypeStruct((quarter,), jnp.int32),
+        ),
+        in_specs=[SMEM] * 3 + [VMEM] * len(arrays),
+        out_specs=(VMEM, SMEM),
         compiler_params=pltpu.CompilerParams(vmem_limit_bytes=LIMIT),
-    )(*arrays)
+    )(*pairs, *arrays)
 
 
 def load_kernel(count, *refs):
@@ -262,46 +270,26 @@
             yield e, (core ^ side) * half + q if shared else q
 
 
-def rows_of(blocks, pair_eval_ref, pair_corpus_ref, quarter):
-    for p in range(quarter):
-        slot = lax.axis_index("vocab") * quarter + p
-        yield p, slot, pair_eval_ref[slot], pair_eval_ref[slot] * blocks + pair_corpus_ref[slot]
-
-
-def comes_late(shards, e):
-    ring, far = ring_of(shards), shards // 2
-    place, _, _ = ring_place(shards)
-    at = look_up([ring.index(c) for c in range(shards)], e)
-    distance = (at - place + shards) % shards
-    return (distance >= far - 1) & (distance <= far + 1)
-
-
 def table_kernel(shards, blocks, scale_ref, mine_ref, other_ref, table_ref):
     for side, sums_ref in enumerate((mine_ref, other_ref)):
         for at, (e, d) in enumerate(steps_of(shards, blocks, side, range(shards // 2 - 1))):
-            row = e * blocks + d
-            table_ref[row] = sums_ref[at] * scale_ref[row]
-
-
-def spread_kernel(shards, blocks, counts, pair_eval_ref, pair_corpus_ref, pair_count_ref, scale_ref, early_ref, *refs):
-    *sums, out_ref, table, zeros, sem = refs
-    quarter = out_ref.shape[0]
+            table_ref[e * blocks + d] = sums_ref[at] * scale_ref[e * blocks + d]
+    table_ref[shards * blocks] = jnp.zeros(table_ref.shape[1:], jnp.float32)
+
+
+def spread_kernel(shards, blocks, counts, slot_ref, scale_ref, *refs):
+    *sums, _, table_ref, out_ref, row_ref, row_sem, sem = refs
     half = len(sums) // 2
-    zeros[...] = jnp.zeros_like(zeros)
-    slots = []
-    for p, slot, e, row in rows_of(blocks, pair_eval_ref, pair_corpus_ref, quarter):
-        live, late = slot < pair_count_ref[0], comes_late(shards, e)
-        slots.append((p, row, live & late))
-        pl.when(live & jnp.logical_not(late))(pltpu.make_async_copy(early_ref.at[row], out_ref.at[p], sem.at[p]).start)
-        pl.when(jnp.logical_not(live))(pltpu.make_async_copy(zeros, out_ref.at[p], sem.at[p]).start)
+    rows_copy = pltpu.make_async_copy(slot_ref, row_ref, row_sem)
+    rows_copy.start()
     for side in range(2):
         tiles = joined(grouped(sums[side * half : (side + 1) * half], counts))
         for tile, (e, d) in zip(tiles, steps_of(shards, blocks, side, (shards // 2 - 1, shards // 2))):
-            table[e * blocks + d] = tile * scale_ref[e * blocks + d]
-    for p, row, late in slots:
-        pl.when(late)(pltpu.make_async_copy(table.at[row], out_ref.at[p], sem.at[p]).start)
-    for p in range(quarter):
-        pltpu.make_async_copy(zeros, out_ref.at[p], sem.at[p]).wait()
+            table_ref[e * blocks + d] = tile * scale_ref[e * blocks + d]
+    rows_copy.wait()
+    for p in range(out_ref.shape[0]):
+        pltpu.make_async_copy(table_ref.at[row_ref[p]], out_ref.at[p], sem).start()
+    pltpu.make_async_copy(out_ref, out_ref, sem).wait()
 
 
 def after(array, *others):
@@ -370,14 +358,15 @@
         parts.append([*carried, chip, cross(code)])
         near[step + 1] = after(near[step + 1], chip, *[part[-1] for part in parts[:-1]])
     parts[-2][-1] = after(parts[-2][-1], parts[-1][0])
-    early = join(parts[:-1])
+    pairs = (pair_eval_block, pair_corpus_block, pair_count)
+    early, slot_rows = join(shards, blocks, quarter, pairs, parts[:-1])
     near[far] = after(near[far], early)
     also.append(swap(near[far]))
     last, last_code = work(far, True)
     parts.append([last, cross(last_code)])
     late = parts[-2:]
     early_other = swap(early)
-    table = jax.ShapeDtypeStruct((shards * blocks, rows, rows), jnp.float32)
+    table = jax.ShapeDtypeStruct((shards * blocks + 1, rows, rows), jnp.float32)
     cosines = pl.pallas_call(
         functools.partial(table_kernel, shards, blocks),
         out_shape=table,
@@ -389,16 +378,13 @@
     sums = mine + [swap(array) for array in mine]
     return pl.pallas_call(
         functools.partial(spread_kernel, shards, blocks, [len(part) for part in late]),
-        out_shape=jax.ShapeDtypeStruct((quarter, rows, rows), jnp.float32),
-        in_specs=[SMEM] * 3 + [VMEM] * (2 + len(sums)),
-        out_specs=pl.BlockSpec(memory_space=pl.ANY),
-        scratch_shapes=[
-            pltpu.VMEM(table.shape, jnp.float32),
-            pltpu.VMEM((rows, rows), jnp.float32),
-            pltpu.SemaphoreType.DMA((quarter,)),
-        ],
+        out_shape=(table, jax.ShapeDtypeStruct((quarter, rows, rows), jnp.float32)),
+        in_specs=[VMEM] * (3 + len(sums)),
+        out_specs=(VMEM, pl.BlockSpec(memory_space=pl.ANY)),
+        input_output_aliases={2 + len(sums): 0},
+        scratch_shapes=[pltpu.SMEM((quarter,), jnp.int32), pltpu.SemaphoreType.DMA, pltpu.SemaphoreType.DMA],
         compiler_params=pltpu.CompilerParams(vmem_limit_bytes=LIMIT),
-    )(pair_eval_block, pair_corpus_block, pair_count, scale, cosines, *sums)
+    )(slot_rows, scale, *sums, cosines)[1]
 
 
 def solution(mesh):

time: 46.2 us -> 46.2 us (level)
  Pallas kernels: 12 us -> 12.8 us
  waiting for transfers between devices: 8.9 us -> 8.11 us
    ppermute x7, waiting for transfers between devices: 3.47 us -> 1.72 us  [move(): return lax.ppermute(block, ('corpus', 'vocab'), onward)]
    pallas_call x1, Pallas kernels: 0.1 us -> 1.2 us  [join(): pl.pallas_call(functools.partial(join_kernel, shards, blocks, [len(part)...]
    ppermute x10, waiting for transfers between devices: 1.96 us -> 3 us  [swap(): return lax.ppermute(array, 'vocab', to_core)]
  transfers between devices with their start and end apart: 21 -> 21, of which waited for: 12 -> 11; matrix products, arithmetic and copies ran while one was open for 0% -> 0% of each run, Pallas kernels for 22% -> 24%
where the time goes in v5:
time: 46.2 us; the launch traced here: 46 us
  starting transfers between devices  24.3 us (53%)
  Pallas kernels  12.8 us (28%)
  waiting for transfers between devices  8.11 us (18%)
  between operations  0.79 us (2%)
    ppermute x7, starting transfers between devices, move(): return lax.ppermute(block, ('corpus', 'vocab'), onward)  15.9 us
    pallas_call x5, Pallas kernels, dots(): pl.pallas_call(functools.partial(dots_kernel, tiles_slice, step, halved,...  7.91 us
    ppermute x4, starting transfers between devices, cross(): return lax.ppermute(array, 'vocab', to_chip)  6.08 us
    ppermute x4, waiting for transfers between devices, cross(): return lax.ppermute(array, 'vocab', to_chip)  3.39 us
    ppermute x10, waiting for transfers between devices, swap(): return lax.ppermute(array, 'vocab', to_core)  3 us
    ppermute x10, starting transfers between devices, swap(): return lax.ppermute(array, 'vocab', to_core)  2.3 us
    pallas_call x1, Pallas kernels, load(): pl.pallas_call(functools.partial(load_kernel, len(arrays)), out_shape=[ja...  1.84 us
    ppermute x7, waiting for transfers between devices, move(): return lax.ppermute(block, ('corpus', 'vocab'), onward)  1.72 us
  transfers between devices with their start and end apart: 21, of which 11 were waited for; matrix products, arithmetic and copies ran while one was open for 0% of the time, Pallas kernels for 24%

profile of v5, /device:TPU:0, one launch (start us, length us, event | category | flops | bytes accessed | tf_op | source)
XLA Modules:
  0.0 46.0 jit_solution(17984836116763168832)
XLA Ops:
  0.0 0.5 collective-permute-start.1
  0.5 0.1 collective-permute-start
  0.5 3.0 %collective-permute-start.4 = (bf16[1,3,128,512]{3,2,1,0:T(8,128)(2,1)}, bf16[1,3,128,512]{3,2,1,0:T(8,128)(2,1)S(1)}, u32[]{:S(2)}, u32[]{:S(2)}) collective-permute-start(bf16[1,3,128,512]{3,2,1,0:T(8,128)(2,1)} %refs_1_.1), channel_id=1, source_target_pairs={{0,8},{1,5},{2,10},{3,7},{8,16},{9,1},{10,18},{11,3},{16,24},{17,9... | collective-permute-start | bytes 1179656 | tf_op jit(solution)/shard_map/ppermute | solution.py:325
  3.5 0.7 %collective-permute-done.refs_4_ = bf16[1,3,128,512]{3,2,1,0:T(8,128)(2,1)S(1)} collective-permute-done((bf16[1,3,128,512]{3,2,1,0:T(8,128)(2,1)}, bf16[1,3,128,512]{3,2,1,0:T(8,128)(2,1)S(1)}, u32[]{:S(2)}, u32[]{:S(2)}) %collective-permute-start) | collective-permute-done | bytes 393248 | tf_op jit(solution)/shard_map/ppermute | solution.py:328
  4.3 2.9 %collective-permute-start.5 = (bf16[1,3,128,512]{3,2,1,0:T(8,128)(2,1)S(1)}, bf16[1,3,128,512]{3,2,1,0:T(8,128)(2,1)S(1)}, u32[]{:S(2)}, u32[]{:S(2)}) collective-permute-start(bf16[1,3,128,512]{3,2,1,0:T(8,128)(2,1)S(1)} %collective-permute-done.refs_4_), channel_id=1, source_target_pairs={{0,8},{1,5},{2,10},{3,7},{8,16},{9,1},{10,18},{11,3},{16,24},{17,9... | collective-permute-start | bytes 1179656 | tf_op jit(solution)/shard_map/ppermute | solution.py:325
  7.2 1.8 %shard_map.91 = (bf16[4,3,128,512]{3,2,1,0:T(8,128)(2,1)S(1)}, bf16[1,3,128,512]{3,2,1,0:T(8,128)(2,1)S(1)}, s32[3,8]{1,0:T(4,128)S(1)}, s32[4,3]{1,0:T(4,128)S(...) custom-call(bf16[4,3,128,512]{3,2,1,0:T(8,128)(2,1)} %refs_0_.1, bf16[1,3,128,512]{3,2,1,0:T(8,128)(2,1)} %refs_1_.1, ...), custom_call_target="tpu_custom_call" | custom-call | tf_op jit(solution)/shard_map/pallas_call | solution.py:248
  9.1 0.4 collective-permute-done.4.refs_0_
  9.4 2.1 %collective-permute-start.7 = (bf16[1,3,128,512]{3,2,1,0:T(8,128)(2,1)S(1)}, bf16[1,3,128,512]{3,2,1,0:T(8,128)(2,1)S(1)}, u32[]{:S(2)}, u32[]{:S(2)}) collective-permute-start(bf16[1,3,128,512]{3,2,1,0:T(8,128)(2,1)S(1)} %collective-permute-done.4.refs_0_), channel_id=1, source_target_pairs={{0,8},{1,5},{2,10},{3,7},{8,16},{9,1},{10,18},{11,3},{16,24},{17,9... | collective-permute-start | bytes 1179656 | tf_op jit(solution)/shard_map/ppermute | solution.py:325
  11.5 0.0 collective-permute-start.2
  11.5 0.5 %collective-permute-start.3 = (s32[4,3]{1,0:T(4,128)S(1)}, s32[4,3]{1,0:T(4,128)S(1)}, u32[]{:S(2)}, u32[]{:S(2)}) collective-permute-start(s32[4,3]{1,0:T(4,128)S(1)} %copy-done), channel_id=1, source_target_pairs={{0,1},{1,0},{2,3},{3,2},{4,5},{5,4},{6,7},{7,6},{8,9},{9,8},{10,11... | collective-permute-start | bytes 152 | tf_op jit(solution)/shard_map/ppermute | solution.py:328
  12.0 0.8 %collective-permute-done.3.refs_7_ = s32[4,3]{1,0:T(4,128)S(1)} collective-permute-done((s32[4,3]{1,0:T(4,128)S(1)}, s32[4,3]{1,0:T(4,128)S(1)}, u32[]{:S(2)}, u32[]{:S(2)}) %collective-permute-start.3) | collective-permute-done | bytes 80 | tf_op jit(solution)/shard_map/ppermute | solution.py:328
  12.9 0.0 collective-permute-done.2.refs_6_
  12.9 0.0 collective-permute-done.1.refs_5_
  12.9 1.3 %shard_map.92.refs_8_.refs_0_ = f32[2,128,128]{2,1,0:T(8,128)S(1)} custom-call(bf16[1,3,128,512]{3,2,1,0:T(8,128)(2,1)S(1)} %get-tuple-element.32.refs_0_, bf16[4,3,128,512]{3,2,1,0:T(8,128)(2,1)S(1)} %get-tuple-element.33.refs_1_, s32[3,8]{1,0:T(4,128)S(1)} %get-tuple-element.34.refs_2_, s32[4,3]{1,0:T(4,128)S(1)} %get-tuple-element.35.refs_3_, ...), custom_call_target="tpu_custom_call" | custom-call | flops 201326592 | bytes 3932160 | tf_op jit(solution)/shard_map/pallas_call | solution.py:170
  14.2 1.6 %collective-permute-start.8 = (bf16[1,3,128,512]{3,2,1,0:T(8,128)(2,1)S(1)}, bf16[1,3,128,512]{3,2,1,0:T(8,128)(2,1)S(1)}, u32[]{:S(2)}, u32[]{:S(2)}) collective-permute-start(bf16[1,3,128,512]{3,2,1,0:T(8,128)(2,1)S(1)} %collective-permute-done.5.refs_4_), channel_id=1, source_target_pairs={{0,8},{1,5},{2,10},{3,7},{8,16},{9,1},{10,18},{11,3},{16,24},{17,9... | collective-permute-start | bytes 1179656 | tf_op jit(solution)/shard_map/ppermute | solution.py:325
  15.8 1.8 %shard_map.93 = (f32[4,128,128]{2,1,0:T(8,128)S(1)}, s16[784,128]{1,0:T(8,128)(2,1)S(1)}) custom-call(bf16[1,3,128,512]{3,2,1,0:T(8,128)(2,1)S(1)} %collective-permute-done.4.refs_0_, bf16[4,3,128,512]{3,2,1,0:T(8,128)(2,1)S(1)} %get-tuple-element.33.refs_1_, s32[3,8]{1,0:T(4,128)S(1)} %get-tuple-element.34.refs_2_, s32[4,3]{1,0:T(4,128)S(1)} %get-tuple-element.35.refs_3_, ...), custom_call_target="tpu_custom_call" | custom-call | flops 402653184 | bytes 3932160 | tf_op jit(solution)/shard_map/pallas_call | solution.py:170
  17.6 0.3 collective-permute-done.7.refs_0_
  17.9 2.1 %collective-permute-start.10 = (bf16[1,3,128,512]{3,2,1,0:T(8,128)(2,1)S(1)}, bf16[1,3,128,512]{3,2,1,0:T(8,128)(2,1)S(1)}, u32[]{:S(2)}, u32[]{:S(2)}) collective-permute-start(bf16[1,3,128,512]{3,2,1,0:T(8,128)(2,1)S(1)} %collective-permute-done.7.refs_0_), channel_id=1, source_target_pairs={{0,8},{1,5},{2,10},{3,7},{8,16},{9,1},{10,18},{11,3},{16,24},{17,9... | collective-permute-start | bytes 1179656 | tf_op jit(solution)/shard_map/ppermute | solution.py:325
  20.0 1.5 %collective-permute-start.6 = (s16[784,128]{1,0:T(8,128)(2,1)S(1)}, s16[784,128]{1,0:T(8,128)(2,1)S(1)}, u32[]{:S(2)}, u32[]{:S(2)}) collective-permute-start(s16[784,128]{1,0:T(8,128)(2,1)S(1)} %get-tuple-element.40), channel_id=1, source_target_pairs={{0,2},{1,3},{2,0},{3,1},{4,6},{5,7},{6,4},{7,5},{8,10},{9,11},{10,... | collective-permute-start | bytes 602120 | tf_op jit(solution)/shard_map/ppermute | solution.py:331
  21.4 0.6 %collective-permute-done.8.refs_4_ = bf16[1,3,128,512]{3,2,1,0:T(8,128)(2,1)S(1)} collective-permute-done((bf16[1,3,128,512]{3,2,1,0:T(8,128)(2,1)S(1)}, bf16[1,3,128,512]{3,2,1,0:T(8,128)(2,1)S(1)}, u32[]{:S(2)}, u32[]{:S(2)}) %collective-permute-start.8) | collective-permute-done | bytes 393248 | tf_op jit(solution)/shard_map/ppermute | solution.py:325
  22.1 2.1 %collective-permute-start.11 = (bf16[1,3,128,512]{3,2,1,0:T(8,128)(2,1)S(1)}, bf16[1,3,128,512]{3,2,1,0:T(8,128)(2,1)S(1)}, u32[]{:S(2)}, u32[]{:S(2)}) collective-permute-start(bf16[1,3,128,512]{3,2,1,0:T(8,128)(2,1)S(1)} %collective-permute-done.8.refs_4_), channel_id=1, source_target_pairs={{0,8},{1,5},{2,10},{3,7},{8,16},{9,1},{10,18},{11,3},{16,24},{17,9... | collective-permute-start | bytes 1179656 | tf_op jit(solution)/shard_map/ppermute | solution.py:325
  24.2 1.8 %shard_map.94 = (f32[4,128,128]{2,1,0:T(8,128)S(1)}, s16[528,128]{1,0:T(8,128)(2,1)S(1)}) custom-call(bf16[1,3,128,512]{3,2,1,0:T(8,128)(2,1)S(1)} %collective-permute-done.7.refs_0_, bf16[4,3,128,512]{3,2,1,0:T(8,128)(2,1)S(1)} %get-tuple-element.33.refs_1_, s32[3,8]{1,0:T(4,128)S(1)} %get-tuple-element.34.refs_2_, s32[4,3]{1,0:T(4,128)S(1)} %get-tuple-element.35.refs_3_, ...), custom_call_target="tpu_custom_call" | custom-call | flops 402653184 | bytes 3932160 | tf_op jit(solution)/shard_map/pallas_call | solution.py:170
  25.9 0.0 collective-permute-done.6.refs_2_
  26.0 0.3 collective-permute-done.10.refs_0_
  26.3 2.1 %collective-permute-start.13 = (bf16[1,3,128,512]{3,2,1,0:T(8,128)(2,1)S(1)}, bf16[1,3,128,512]{3,2,1,0:T(8,128)(2,1)S(1)}, u32[]{:S(2)}, u32[]{:S(2)}) collective-permute-start(bf16[1,3,128,512]{3,2,1,0:T(8,128)(2,1)S(1)} %collective-permute-done.10.refs_0_), channel_id=1, source_target_pairs={{0,8},{1,5},{2,10},{3,7},{8,16},{9,1},{10,18},{11,3},{16,24},{17,9... | collective-permute-start | bytes 1179656 | tf_op jit(solution)/shard_map/ppermute | solution.py:325
  28.4 1.5 %collective-permute-start.9 = (s16[528,128]{1,0:T(8,128)(2,1)S(1)}, s16[528,128]{1,0:T(8,128)(2,1)S(1)}, u32[]{:S(2)}, u32[]{:S(2)}) collective-permute-start(s16[528,128]{1,0:T(8,128)(2,1)S(1)} %get-tuple-element.43), channel_id=1, source_target_pairs={{0,2},{1,3},{2,0},{3,1},{4,6},{5,7},{6,4},{7,5},{8,10},{9,11},{10,... | collective-permute-start | bytes 405512 | tf_op jit(solution)/shard_map/ppermute | solution.py:331
  30.5 1.8 %shard_map.95 = (f32[4,128,128]{2,1,0:T(8,128)S(1)}, s16[528,128]{1,0:T(8,128)(2,1)S(1)}) custom-call(bf16[1,3,128,512]{3,2,1,0:T(8,128)(2,1)S(1)} %collective-permute-done.10.refs_0_, bf16[4,3,128,512]{3,2,1,0:T(8,128)(2,1)S(1)} %get-tuple-element.33.refs_1_, s32[3,8]{1,0:T(4,128)S(1)} %get-tuple-element.34.refs_2_, s32[4,3]{1,0:T(4,128)S(1)} %get-tuple-element.35.refs_3_, ...), custom_call_target="tpu_custom_call" | custom-call | flops 402653184 | bytes 3932160 | tf_op jit(solution)/shard_map/pallas_call | solution.py:170
  32.3 1.1 %collective-permute-done.9.refs_4_ = s16[528,128]{1,0:T(8,128)(2,1)S(1)} collective-permute-done((s16[528,128]{1,0:T(8,128)(2,1)S(1)}, s16[528,128]{1,0:T(8,128)(2,1)S(1)}, u32[]{:S(2)}, u32[]{:S(2)}) %collective-permute-start.9) | collective-permute-done | bytes 135200 | tf_op jit(solution)/shard_map/ppermute | solution.py:331
  33.4 1.2 %shard_map.96 = (f32[10,128,128]{2,1,0:T(8,128)S(1)}, s32[24]{0:T(128)S(1)}) custom-call(s32[96]{0:T(128)S(1)} %get-tuple-element.30.pair_eval_ref, s32[96]{0:T(128)S(1)} %get-tuple-element.31.pair_corpus_ref, s32[1]{0:T(128)S(6)} %copy.12.pair_count_ref, f32[2,128,128]{2,1,0:T(8,128)S(1)} %shard_map.92.refs_8_.refs_0_, ...), custom_call_target="tpu_custom_call" | custom-call | tf_op jit(solution)/shard_map/pallas_call | solution.py:211
  34.6 0.1 collective-permute-start.20
  34.7 0.0 collective-permute-done.13.refs_0_
  34.7 0.5 collective-permute-start.14
  35.2 1.5 %collective-permute-start.12 = (s16[528,128]{1,0:T(8,128)(2,1)S(1)}, s16[528,128]{1,0:T(8,128)(2,1)S(1)}, u32[]{:S(2)}, u32[]{:S(2)}) collective-permute-start(s16[528,128]{1,0:T(8,128)(2,1)S(1)} %get-tuple-element.48), channel_id=1, source_target_pairs={{0,2},{1,3},{2,0},{3,1},{4,6},{5,7},{6,4},{7,5},{8,10},{9,11},{10,... | collective-permute-start | bytes 405512 | tf_op jit(solution)/shard_map/ppermute | solution.py:331
  36.7 0.2 collective-permute-start.16
  37.0 0.4 collective-permute-done.14.refs_4_
  37.3 1.3 %shard_map.97 = (f32[2,128,128]{2,1,0:T(8,128)S(1)}, s16[272,128]{1,0:T(8,128)(2,1)S(1)}) custom-call(bf16[1,3,128,512]{3,2,1,0:T(8,128)(2,1)S(1)} %collective-permute-done.13.refs_0_, bf16[4,3,128,512]{3,2,1,0:T(8,128)(2,1)S(1)} %get-tuple-element.33.refs_1_, s32[3,8]{1,0:T(4,128)S(1)} %get-tuple-element.34.refs_2_, s32[4,3]{1,0:T(4,128)S(1)} %get-tuple-element.35.refs_3_, ...), custom_call_target="tpu_custom_call" | custom-call | flops 201326592 | bytes 3932160 | tf_op jit(solution)/shard_map/pallas_call | solution.py:170
  38.7 1.6 %collective-permute-start.15 = (s16[272,128]{1,0:T(8,128)(2,1)S(1)}, s16[272,128]{1,0:T(8,128)(2,1)S(1)}, u32[]{:S(2)}, u32[]{:S(2)}) collective-permute-start(s16[272,128]{1,0:T(8,128)(2,1)S(1)} %get-tuple-element.53), channel_id=1, source_target_pairs={{0,2},{1,3},{2,0},{3,1},{4,6},{5,7},{6,4},{7,5},{8,10},{9,11},{10,... | collective-permute-start | bytes 208904 | tf_op jit(solution)/shard_map/ppermute | solution.py:331
  40.2 0.8 %collective-permute-done.12.refs_1_ = s16[528,128]{1,0:T(8,128)(2,1)S(1)} collective-permute-done((s16[528,128]{1,0:T(8,128)(2,1)S(1)}, s16[528,128]{1,0:T(8,128)(2,1)S(1)}, u32[]{:S(2)}, u32[]{:S(2)}) %collective-permute-start.12) | collective-permute-done | bytes 135200 | tf_op jit(solution)/shard_map/ppermute | solution.py:331
  41.0 0.0 collective-permute-start.17
  41.0 0.5 %collective-permute-start.18 = (f32[2,128,128]{2,1,0:T(8,128)S(1)}, f32[2,128,128]{2,1,0:T(8,128)S(1)}, u32[]{:S(2)}, u32[]{:S(2)}) collective-permute-start(f32[2,128,128]{2,1,0:T(8,128)S(1)} %get-tuple-element.52.refs_2_), channel_id=1, source_target_pairs={{0,1},{1,0},{2,3},{3,2},{4,5},{5,4},{6,7},{7,6},{8,9},{9,8},{10,11... | collective-permute-start | bytes 393224 | tf_op jit(solution)/shard_map/ppermute | solution.py:328
  41.5 1.5 %collective-permute-done.15.refs_3_ = s16[272,128]{1,0:T(8,128)(2,1)S(1)} collective-permute-done((s16[272,128]{1,0:T(8,128)(2,1)S(1)}, s16[272,128]{1,0:T(8,128)(2,1)S(1)}, u32[]{:S(2)}, u32[]{:S(2)}) %collective-permute-start.15) | collective-permute-done | bytes 69664 | tf_op jit(solution)/shard_map/ppermute | solution.py:331
  43.0 0.0 collective-permute-start.19
  43.0 0.0 collective-permute-done.20.other_ref
  43.0 0.2 shard_map.98.refs_8_
  43.2 0.0 collective-permute-done.16.refs_4_
  43.2 0.0 collective-permute-done.17.refs_5_
  43.2 1.1 %collective-permute-done.19.refs_7_ = s16[272,128]{1,0:T(8,128)(2,1)S(1)} collective-permute-done((s16[272,128]{1,0:T(8,128)(2,1)S(1)}, s16[272,128]{1,0:T(8,128)(2,1)S(1)}, u32[]{:S(2)}, u32[]{:S(2)}) %collective-permute-start.19) | collective-permute-done | bytes 69664 | tf_op jit(solution)/shard_map/ppermute | solution.py:328
  44.3 1.7 %shard_map.99 = (f32[33,128,128]{2,1,0:T(8,128)S(1)}, f32[24,128,128]{2,1,0:T(8,128)}) custom-call(s32[24]{0:T(128)S(1)} %get-tuple-element.47.slot_ref, f32[32,128,128]{2,1,0:T(8,128)S(1)} %get-tuple-element.36.scale_ref, f32[4,128,128]{2,1,0:T(8,128)S(1)} %get-tuple-element.45.refs_0_, ...), custom_call_target="tpu_custom_call", output_to_operand_aliasing={{0}: (10, {})} | custom-call | tf_op jit(solution)/shard_map/pallas_call | solution.py:379
  (7 shorter events, 0.0 us)
Async XLA Ops:
  0.0 11.5 %copy-start = (s32[4,3]{1,0:T(4,128)S(1)}, s32[4,3]{1,0:T(4,128)}, u32[]{:S(2)}) copy-start(s32[4,3]{1,0:T(4,128)} %refs_3_.1) | copy-start | bytes 148
  0.0 11.5 %copy-start.1 = (s32[8,3]{0,1:T(4,128)S(1)}, s32[8,3]{0,1:T(4,128)}, u32[]{:S(2)}) copy-start(s32[8,3]{0,1:T(4,128)} %param.10) | copy-start | bytes 292
  0.0 12.9 %collective-permute-start.1 = (bf16[4,3,128,512]{3,2,1,0:T(8,128)(2,1)}, bf16[4,3,128,512]{3,2,1,0:T(8,128)(2,1)S(1)}, u32[]{:S(2)}, u32[]{:S(2)}) collective-permute-start(bf16[4,3,128,512]{3,2,1,0:T(8,128)(2,1)} %refs_0_.1), channel_id=1, source_target_pairs={{0,1},{1,0},{2,3},{3,2},{4,5},{5,4},{6,7},{7,6},{8,9},{9,8},{10,11... | collective-permute-start | bytes 4718600 | tf_op jit(solution)/shard_map/ppermute | solution.py:328
  0.5 3.8 %collective-permute-start = (bf16[1,3,128,512]{3,2,1,0:T(8,128)(2,1)}, bf16[1,3,128,512]{3,2,1,0:T(8,128)(2,1)S(1)}, u32[]{:S(2)}, u32[]{:S(2)}) collective-permute-start(bf16[1,3,128,512]{3,2,1,0:T(8,128)(2,1)} %refs_1_.1), channel_id=1, source_target_pairs={{0,1},{1,0},{2,3},{3,2},{4,5},{5,4},{6,7},{7,6},{8,9},{9,8},{10,11... | collective-permute-start | bytes 1179656 | tf_op jit(solution)/shard_map/ppermute | solution.py:328
  0.5 8.9 %collective-permute-start.4 = (bf16[1,3,128,512]{3,2,1,0:T(8,128)(2,1)}, bf16[1,3,128,512]{3,2,1,0:T(8,128)(2,1)S(1)}, u32[]{:S(2)}, u32[]{:S(2)}) collective-permute-start(bf16[1,3,128,512]{3,2,1,0:T(8,128)(2,1)} %refs_1_.1), channel_id=1, source_target_pairs={{0,8},{1,5},{2,10},{3,7},{8,16},{9,1},{10,18},{11,3},{16,24},{17,9... | collective-permute-start | bytes 1179656 | tf_op jit(solution)/shard_map/ppermute | solution.py:325
  4.3 9.9 %collective-permute-start.5 = (bf16[1,3,128,512]{3,2,1,0:T(8,128)(2,1)S(1)}, bf16[1,3,128,512]{3,2,1,0:T(8,128)(2,1)S(1)}, u32[]{:S(2)}, u32[]{:S(2)}) collective-permute-start(bf16[1,3,128,512]{3,2,1,0:T(8,128)(2,1)S(1)} %collective-permute-done.refs_4_), channel_id=1, source_target_pairs={{0,8},{1,5},{2,10},{3,7},{8,16},{9,1},{10,18},{11,3},{16,24},{17,9... | collective-permute-start | bytes 1179656 | tf_op jit(solution)/shard_map/ppermute | solution.py:325
  9.4 8.4 %collective-permute-start.7 = (bf16[1,3,128,512]{3,2,1,0:T(8,128)(2,1)S(1)}, bf16[1,3,128,512]{3,2,1,0:T(8,128)(2,1)S(1)}, u32[]{:S(2)}, u32[]{:S(2)}) collective-permute-start(bf16[1,3,128,512]{3,2,1,0:T(8,128)(2,1)S(1)} %collective-permute-done.4.refs_0_), channel_id=1, source_target_pairs={{0,8},{1,5},{2,10},{3,7},{8,16},{9,1},{10,18},{11,3},{16,24},{17,9... | collective-permute-start | bytes 1179656 | tf_op jit(solution)/shard_map/ppermute | solution.py:325
  11.5 1.3 %collective-permute-start.2 = (s32[3,8]{1,0:T(4,128)S(1)}, s32[3,8]{1,0:T(4,128)S(1)}, u32[]{:S(2)}, u32[]{:S(2)}) collective-permute-start(s32[3,8]{1,0:T(4,128)S(1)} %bitcast.6), channel_id=1, source_target_pairs={{0,1},{1,0},{2,3},{3,2},{4,5},{5,4},{6,7},{7,6},{8,9},{9,8},{10,11... | collective-permute-start | bytes 296 | tf_op jit(solution)/shard_map/ppermute | solution.py:328
  11.5 1.3 %collective-permute-start.3 = (s32[4,3]{1,0:T(4,128)S(1)}, s32[4,3]{1,0:T(4,128)S(1)}, u32[]{:S(2)}, u32[]{:S(2)}) collective-permute-start(s32[4,3]{1,0:T(4,128)S(1)} %copy-done), channel_id=1, source_target_pairs={{0,1},{1,0},{2,3},{3,2},{4,5},{5,4},{6,7},{7,6},{8,9},{9,8},{10,11... | collective-permute-start | bytes 152 | tf_op jit(solution)/shard_map/ppermute | solution.py:328
  14.2 7.9 %collective-permute-start.8 = (bf16[1,3,128,512]{3,2,1,0:T(8,128)(2,1)S(1)}, bf16[1,3,128,512]{3,2,1,0:T(8,128)(2,1)S(1)}, u32[]{:S(2)}, u32[]{:S(2)}) collective-permute-start(bf16[1,3,128,512]{3,2,1,0:T(8,128)(2,1)S(1)} %collective-permute-done.5.refs_4_), channel_id=1, source_target_pairs={{0,8},{1,5},{2,10},{3,7},{8,16},{9,1},{10,18},{11,3},{16,24},{17,9... | collective-permute-start | bytes 1179656 | tf_op jit(solution)/shard_map/ppermute | solution.py:325
  17.9 8.4 %collective-permute-start.10 = (bf16[1,3,128,512]{3,2,1,0:T(8,128)(2,1)S(1)}, bf16[1,3,128,512]{3,2,1,0:T(8,128)(2,1)S(1)}, u32[]{:S(2)}, u32[]{:S(2)}) collective-permute-start(bf16[1,3,128,512]{3,2,1,0:T(8,128)(2,1)S(1)} %collective-permute-done.7.refs_0_), channel_id=1, source_target_pairs={{0,8},{1,5},{2,10},{3,7},{8,16},{9,1},{10,18},{11,3},{16,24},{17,9... | collective-permute-start | bytes 1179656 | tf_op jit(solution)/shard_map/ppermute | solution.py:325
  20.0 6.0 %collective-permute-start.6 = (s16[784,128]{1,0:T(8,128)(2,1)S(1)}, s16[784,128]{1,0:T(8,128)(2,1)S(1)}, u32[]{:S(2)}, u32[]{:S(2)}) collective-permute-start(s16[784,128]{1,0:T(8,128)(2,1)S(1)} %get-tuple-element.40), channel_id=1, source_target_pairs={{0,2},{1,3},{2,0},{3,1},{4,6},{5,7},{6,4},{7,5},{8,10},{9,11},{10,... | collective-permute-start | bytes 602120 | tf_op jit(solution)/shard_map/ppermute | solution.py:331
  22.1 8.4 %collective-permute-start.11 = (bf16[1,3,128,512]{3,2,1,0:T(8,128)(2,1)S(1)}, bf16[1,3,128,512]{3,2,1,0:T(8,128)(2,1)S(1)}, u32[]{:S(2)}, u32[]{:S(2)}) collective-permute-start(bf16[1,3,128,512]{3,2,1,0:T(8,128)(2,1)S(1)} %collective-permute-done.8.refs_4_), channel_id=1, source_target_pairs={{0,8},{1,5},{2,10},{3,7},{8,16},{9,1},{10,18},{11,3},{16,24},{17,9... | collective-permute-start | bytes 1179656 | tf_op jit(solution)/shard_map/ppermute | solution.py:325
  26.3 8.4 %collective-permute-start.13 = (bf16[1,3,128,512]{3,2,1,0:T(8,128)(2,1)S(1)}, bf16[1,3,128,512]{3,2,1,0:T(8,128)(2,1)S(1)}, u32[]{:S(2)}, u32[]{:S(2)}) collective-permute-start(bf16[1,3,128,512]{3,2,1,0:T(8,128)(2,1)S(1)} %collective-permute-done.10.refs_0_), channel_id=1, source_target_pairs={{0,8},{1,5},{2,10},{3,7},{8,16},{9,1},{10,18},{11,3},{16,24},{17,9... | collective-permute-start | bytes 1179656 | tf_op jit(solution)/shard_map/ppermute | solution.py:325
  28.4 5.0 %collective-permute-start.9 = (s16[528,128]{1,0:T(8,128)(2,1)S(1)}, s16[528,128]{1,0:T(8,128)(2,1)S(1)}, u32[]{:S(2)}, u32[]{:S(2)}) collective-permute-start(s16[528,128]{1,0:T(8,128)(2,1)S(1)} %get-tuple-element.43), channel_id=1, source_target_pairs={{0,2},{1,3},{2,0},{3,1},{4,6},{5,7},{6,4},{7,5},{8,10},{9,11},{10,... | collective-permute-start | bytes 405512 | tf_op jit(solution)/shard_map/ppermute | solution.py:331
  34.6 8.4 %collective-permute-start.20 = (f32[10,128,128]{2,1,0:T(8,128)S(1)}, f32[10,128,128]{2,1,0:T(8,128)S(1)}, u32[]{:S(2)}, u32[]{:S(2)}) collective-permute-start(f32[10,128,128]{2,1,0:T(8,128)S(1)} %get-tuple-element.50.mine_ref), channel_id=1, source_target_pairs={{0,1},{1,0},{2,3},{3,2},{4,5},{5,4},{6,7},{7,6},{8,9},{9,8},{10,11... | collective-permute-start | bytes 1966088 | tf_op jit(solution)/shard_map/ppermute | solution.py:328
  34.7 2.6 %collective-permute-start.14 = (bf16[1,3,128,512]{3,2,1,0:T(8,128)(2,1)S(1)}, bf16[1,3,128,512]{3,2,1,0:T(8,128)(2,1)S(1)}, u32[]{:S(2)}, u32[]{:S(2)}) collective-permute-start(bf16[1,3,128,512]{3,2,1,0:T(8,128)(2,1)S(1)} %collective-permute-done.13.refs_0_), channel_id=1, source_target_pairs={{0,1},{1,0},{2,3},{3,2},{4,5},{5,4},{6,7},{7,6},{8,9},{9,8},{10,11... | collective-permute-start | bytes 1179656 | tf_op jit(solution)/shard_map/ppermute | solution.py:328
  35.2 5.8 %collective-permute-start.12 = (s16[528,128]{1,0:T(8,128)(2,1)S(1)}, s16[528,128]{1,0:T(8,128)(2,1)S(1)}, u32[]{:S(2)}, u32[]{:S(2)}) collective-permute-start(s16[528,128]{1,0:T(8,128)(2,1)S(1)} %get-tuple-element.48), channel_id=1, source_target_pairs={{0,2},{1,3},{2,0},{3,1},{4,6},{5,7},{6,4},{7,5},{8,10},{9,11},{10,... | collective-permute-start | bytes 405512 | tf_op jit(solution)/shard_map/ppermute | solution.py:331
  36.7 6.5 %collective-permute-start.16 = (f32[4,128,128]{2,1,0:T(8,128)S(1)}, f32[4,128,128]{2,1,0:T(8,128)S(1)}, u32[]{:S(2)}, u32[]{:S(2)}) collective-permute-start(f32[4,128,128]{2,1,0:T(8,128)S(1)} %get-tuple-element.45.refs_0_), channel_id=1, source_target_pairs={{0,1},{1,0},{2,3},{3,2},{4,5},{5,4},{6,7},{7,6},{8,9},{9,8},{10,11... | collective-permute-start | bytes 786440 | tf_op jit(solution)/shard_map/ppermute | solution.py:328
  38.7 4.4 %collective-permute-start.15 = (s16[272,128]{1,0:T(8,128)(2,1)S(1)}, s16[272,128]{1,0:T(8,128)(2,1)S(1)}, u32[]{:S(2)}, u32[]{:S(2)}) collective-permute-start(s16[272,128]{1,0:T(8,128)(2,1)S(1)} %get-tuple-element.53), channel_id=1, source_target_pairs={{0,2},{1,3},{2,0},{3,1},{4,6},{5,7},{6,4},{7,5},{8,10},{9,11},{10,... | collective-permute-start | bytes 208904 | tf_op jit(solution)/shard_map/ppermute | solution.py:331
  41.0 2.2 %collective-permute-start.17 = (s16[528,128]{1,0:T(8,128)(2,1)S(1)}, s16[528,128]{1,0:T(8,128)(2,1)S(1)}, u32[]{:S(2)}, u32[]{:S(2)}) collective-permute-start(s16[528,128]{1,0:T(8,128)(2,1)S(1)} %collective-permute-done.12.refs_1_), channel_id=1, source_target_pairs={{0,1},{1,0},{2,3},{3,2},{4,5},{5,4},{6,7},{7,6},{8,9},{9,8},{10,11... | collective-permute-start | bytes 405512 | tf_op jit(solution)/shard_map/ppermute | solution.py:328
  41.0 2.2 %collective-permute-start.18 = (f32[2,128,128]{2,1,0:T(8,128)S(1)}, f32[2,128,128]{2,1,0:T(8,128)S(1)}, u32[]{:S(2)}, u32[]{:S(2)}) collective-permute-start(f32[2,128,128]{2,1,0:T(8,128)S(1)} %get-tuple-element.52.refs_2_), channel_id=1, source_target_pairs={{0,1},{1,0},{2,3},{3,2},{4,5},{5,4},{6,7},{7,6},{8,9},{9,8},{10,11... | collective-permute-start | bytes 393224 | tf_op jit(solution)/shard_map/ppermute | solution.py:328
  43.0 1.3 %collective-permute-start.19 = (s16[272,128]{1,0:T(8,128)(2,1)S(1)}, s16[272,128]{1,0:T(8,128)(2,1)S(1)}, u32[]{:S(2)}, u32[]{:S(2)}) collective-permute-start(s16[272,128]{1,0:T(8,128)(2,1)S(1)} %collective-permute-done.15.refs_3_), channel_id=1, source_target_pairs={{0,1},{1,0},{2,3},{3,2},{4,5},{5,4},{6,7},{7,6},{8,9},{9,8},{10,11... | collective-permute-start | bytes 208904 | tf_op jit(solution)/shard_map/ppermute | solution.py:328

commit v6 on v5

--- a/solution.py
+++ b/solution.py
@@ -193,71 +193,64 @@
     return [[refs.pop(0) for _ in range(count)] for count in counts]
 
 
-def join_kernel(shards, blocks, counts, pair_eval_ref, pair_corpus_ref, pair_count_ref, *refs):
-    *refs, out_ref, slot_ref = refs
+def join_kernel(counts, *refs):
+    *refs, out_ref = refs
     for q, tile in enumerate(joined(grouped(refs, counts))):
         out_ref[q] = tile
+
+
+def join(parts):
+    arrays = [array for part in parts for array in part]
+    tiles = [array for part in parts for array in part[:-1]]
+    count = sum(array.shape[0] for array in tiles)
+    return pl.pallas_call(
+        functools.partial(join_kernel, [len(part) for part in parts]),
+        out_shape=jax.ShapeDtypeStruct((count, *tiles[0].shape[1:]), jnp.float32),
+        in_specs=[VMEM] * len(arrays),
+        out_specs=VMEM,
+        compiler_params=pltpu.CompilerParams(vmem_limit_bytes=LIMIT),
+    )(*arrays)
+
+
+def load_kernel(count, *refs):
+    given, pair_count_ref = refs[: count + 4], refs[count + 4]
+    copied, rest = refs[count + 5 : 2 * count + 5], refs[2 * count + 5 :]
+    scale_ref, slot_ref, eval_norm_ref, corpus_norm_ref, pair_eval_ref, pair_corpus_ref, sem = rest
+    targets = [*copied, eval_norm_ref, corpus_norm_ref, pair_eval_ref, pair_corpus_ref]
+    copies = [pltpu.make_async_copy(src, dst, sem.at[n]) for n, (src, dst) in enumerate(zip(given, targets))]
+    for copy in copies:
+        copy.start()
+    for copy in copies[count:]:
+        copy.wait()
+    shards, blocks = eval_norm_ref.shape[0], corpus_norm_ref.shape[0]
+    eval_norm = eval_norm_ref[...].T
+    for e in range(shards):
+        for d in range(blocks):
+            scale_ref[e * blocks + d] = 1.0 / (eval_norm[:, e : e + 1] * corpus_norm_ref[d : d + 1, :])
     quarter = slot_ref.shape[0]
     for p in range(quarter):
         slot = lax.axis_index("vocab") * quarter + p
         row = pair_eval_ref[slot] * blocks + pair_corpus_ref[slot]
         slot_ref[p] = jnp.where(slot < pair_count_ref[0], row, shards * blocks)
-
-
-def join(shards, blocks, quarter, pairs, parts):
-    arrays = [array for part in parts for array in part]
-    tiles = [array for part in parts for array in part[:-1]]
-    count = sum(array.shape[0] for array in tiles)
-    return pl.pallas_call(
-        functools.partial(join_kernel, shards, blocks, [len(part) for part in parts]),
-        out_shape=(
-            jax.ShapeDtypeStruct((count, *tiles[0].shape[1:]), jnp.float32),
-            jax.ShapeDtypeStruct((quarter,), jnp.int32),
-        ),
-        in_specs=[SMEM] * 3 + [VMEM] * len(arrays),
-        out_specs=(VMEM, SMEM),
-        compiler_params=pltpu.CompilerParams(vmem_limit_bytes=LIMIT),
-    )(*pairs, *arrays)
-
-
-def load_kernel(count, *refs):
-    norms = 2
-    arrays = refs[: count + norms]
-    copied = refs[count + norms : 2 * count + norms]
-    scale_ref, *norm_refs, sem = refs[2 * count + norms :]
-    targets = [*copied, *norm_refs]
-    copies = [pltpu.make_async_copy(src, dst, sem.at[n]) for n, (src, dst) in enumerate(zip(arrays, targets))]
-    for copy in copies:
-        copy.start()
-    for copy in copies[-norms:]:
+    for copy in copies[:count]:
         copy.wait()
-    eval_norm_ref, corpus_norm_ref = norm_refs
-    shards, blocks = eval_norm_ref.shape[0], corpus_norm_ref.shape[0]
-    eval_norm = eval_norm_ref[...].T
-    for e in range(shards):
-        for d in range(blocks):
-            scale_ref[e * blocks + d] = 1.0 / (eval_norm[:, e : e + 1] * corpus_norm_ref[d : d + 1, :])
-    for copy in copies[:-norms]:
-        copy.wait()
-
-
-def load(arrays, eval_norm, corpus_norm):
-    items = eval_norm.shape[0] * corpus_norm.shape[0]
-    rows = eval_norm.shape[1]
-    given = [pltpu.with_memory_space_constraint(array, pltpu.HBM) for array in (*arrays, eval_norm, corpus_norm)]
+
+
+def load(arrays, norms, pairs, pair_count, quarter):
+    items = norms[0].shape[0] * norms[1].shape[0]
+    rows = norms[0].shape[1]
+    given = [pltpu.with_memory_space_constraint(array, pltpu.HBM) for array in (*arrays, *norms, *pairs)]
     return pl.pallas_call(
         functools.partial(load_kernel, len(arrays)),
         out_shape=[jax.ShapeDtypeStruct(array.shape, array.dtype) for array in arrays]
-        + [jax.ShapeDtypeStruct((items, rows, rows), jnp.float32)],
-        in_specs=[pl.BlockSpec(memory_space=pltpu.HBM)] * len(given),
-        out_specs=[VMEM] * (len(arrays) + 1),
-        scratch_shapes=[
-            pltpu.VMEM(eval_norm.shape, jnp.float32),
-            pltpu.VMEM(corpus_norm.shape, jnp.float32),
-            pltpu.SemaphoreType.DMA((len(given),)),
-        ],
+        + [jax.ShapeDtypeStruct((items, rows, rows), jnp.float32), jax.ShapeDtypeStruct((quarter,), jnp.int32)],
+        in_specs=[pl.BlockSpec(memory_space=pltpu.HBM)] * len(given) + [SMEM],
+        out_specs=[VMEM] * (len(arrays) + 1) + [SMEM],
+        scratch_shapes=[pltpu.VMEM(norm.shape, norm.dtype) for norm in norms]
+        + [pltpu.SMEM(array.shape, array.dtype) for array in pairs]
+        + [pltpu.SemaphoreType.DMA((len(given),))],
         compiler_params=pltpu.CompilerParams(vmem_limit_bytes=LIMIT),
-    )(*given)
+    )(*given, pair_count)
 
 
 def steps_of(shards, blocks, side, steps):
@@ -336,9 +329,12 @@
     corpus_also = swap(corpus_tiles)
     ids = (eval_tile_list.T, corpus_tile_list)
     ids_also = tuple(swap(array) for array in ids)
-    given = (corpus_tiles, eval_tiles, *ids, pair_eval_block, pair_corpus_block)
-    corpus_tiles, near[0], *ids, pair_eval_block, pair_corpus_block, scale = load(
-        given, eval_norm.reshape(shards, rows), corpus_norm.reshape(blocks, rows)
+    corpus_tiles, near[0], *ids, scale, slot_rows = load(
+        (corpus_tiles, eval_tiles, *ids),
+        (eval_norm.reshape(shards, rows), corpus_norm.reshape(blocks, rows)),
+        (pair_eval_block, pair_corpus_block),
+        pair_count,
+        quarter,
     )
     near[1] = after(near[1], scale)
 
@@ -358,8 +354,7 @@
         parts.append([*carried, chip, cross(code)])
         near[step + 1] = after(near[step + 1], chip, *[part[-1] for part in parts[:-1]])
     parts[-2][-1] = after(parts[-2][-1], parts[-1][0])
-    pairs = (pair_eval_block, pair_corpus_block, pair_count)
-    early, slot_rows = join(shards, blocks, quarter, pairs, parts[:-1])
+    early = join(parts[:-1])
     near[far] = after(near[far], early)
     also.append(swap(near[far]))
     last, last_code = work(far, True)

time: 46.2 us -> 45.9 us (level)
  waiting for transfers between devices: 8.11 us -> 9.93 us
  starting transfers between devices: 24.3 us -> 22.7 us
  Pallas kernels: 12.8 us -> 12.3 us
    ppermute x7, waiting for transfers between devices: 1.72 us -> 4.14 us  [move(): return lax.ppermute(block, ('corpus', 'vocab'), onward)]
    ppermute x7, starting transfers between devices: 15.9 us -> 14.6 us  [move(): return lax.ppermute(block, ('corpus', 'vocab'), onward)]
    pallas_call x1, Pallas kernels: 1.2 us -> 0.09 us  [join(): pl.pallas_call(functools.partial(join_kernel, [len(part) for part in part...]
    pallas_call x1, Pallas kernels: 1.84 us -> 2.42 us  [load(): pl.pallas_call(functools.partial(load_kernel, len(arrays)), out_shape=[ja...]
  transfers between devices with their start and end apart: 21 -> 21, of which waited for: 11 -> 11; matrix products, arithmetic and copies ran while one was open for 0% -> 0% of each run, Pallas kernels for 24% -> 23%
where the time goes in v6:
time: 45.9 us; the launch traced here: 45.7 us
  starting transfers between devices  22.7 us (49%)
  Pallas kernels  12.3 us (27%)
  waiting for transfers between devices  9.93 us (22%)
  between operations  0.78 us (2%)
    ppermute x7, starting transfers between devices, move(): return lax.ppermute(block, ('corpus', 'vocab'), onward)  14.6 us
    pallas_call x5, Pallas kernels, dots(): pl.pallas_call(functools.partial(dots_kernel, tiles_slice, step, halved,...  7.91 us
    ppermute x4, starting transfers between devices, cross(): return lax.ppermute(array, 'vocab', to_chip)  6.23 us
    ppermute x7, waiting for transfers between devices, move(): return lax.ppermute(block, ('corpus', 'vocab'), onward)  4.14 us
    ppermute x4, waiting for transfers between devices, cross(): return lax.ppermute(array, 'vocab', to_chip)  3.17 us
    ppermute x10, waiting for transfers between devices, swap(): return lax.ppermute(array, 'vocab', to_core)  2.63 us
    pallas_call x1, Pallas kernels, load(): pl.pallas_call(functools.partial(load_kernel, len(arrays)), out_shape=[ja...  2.42 us
    ppermute x10, starting transfers between devices, swap(): return lax.ppermute(array, 'vocab', to_core)  1.85 us
  transfers between devices with their start and end apart: 21, of which 11 were waited for; matrix products, arithmetic and copies ran while one was open for 0% of the time, Pallas kernels for 23%

profile of v6, /device:TPU:0, one launch (start us, length us, event | category | flops | bytes accessed | tf_op | source)
XLA Modules:
  0.0 45.7 jit_solution(13923592864552870872)
XLA Ops:
  0.0 0.5 collective-permute-start.4
  0.5 0.1 collective-permute-start.2
  0.5 3.0 %collective-permute-start = (bf16[1,3,128,512]{3,2,1,0:T(8,128)(2,1)}, bf16[1,3,128,512]{3,2,1,0:T(8,128)(2,1)S(1)}, u32[]{:S(2)}, u32[]{:S(2)}) collective-permute-start(bf16[1,3,128,512]{3,2,1,0:T(8,128)(2,1)} %refs_1_.1), channel_id=1, source_target_pairs={{0,8},{1,5},{2,10},{3,7},{8,16},{9,1},{10,18},{11,3},{16,24},{17,9... | collective-permute-start | bytes 1179656 | tf_op jit(solution)/shard_map/ppermute | solution.py:318
  3.5 0.7 %collective-permute-done.2.refs_4_ = bf16[1,3,128,512]{3,2,1,0:T(8,128)(2,1)S(1)} collective-permute-done((bf16[1,3,128,512]{3,2,1,0:T(8,128)(2,1)}, bf16[1,3,128,512]{3,2,1,0:T(8,128)(2,1)S(1)}, u32[]{:S(2)}, u32[]{:S(2)}) %collective-permute-start.2) | collective-permute-done | bytes 393248 | tf_op jit(solution)/shard_map/ppermute | solution.py:321
  4.3 2.9 %collective-permute-start.3 = (bf16[1,3,128,512]{3,2,1,0:T(8,128)(2,1)S(1)}, bf16[1,3,128,512]{3,2,1,0:T(8,128)(2,1)S(1)}, u32[]{:S(2)}, u32[]{:S(2)}) collective-permute-start(bf16[1,3,128,512]{3,2,1,0:T(8,128)(2,1)S(1)} %collective-permute-done.2.refs_4_), channel_id=1, source_target_pairs={{0,8},{1,5},{2,10},{3,7},{8,16},{9,1},{10,18},{11,3},{16,24},{17,9... | collective-permute-start | bytes 1179656 | tf_op jit(solution)/shard_map/ppermute | solution.py:318
  7.9 2.4 %shard_map.91 = (bf16[4,3,128,512]{3,2,1,0:T(8,128)(2,1)S(1)}, bf16[1,3,128,512]{3,2,1,0:T(8,128)(2,1)S(1)}, s32[3,8]{1,0:T(4,128)S(1)}, s32[4,3]{1,0:T(4,128)S(...) custom-call(bf16[4,3,128,512]{3,2,1,0:T(8,128)(2,1)} %refs_0_.1, bf16[1,3,128,512]{3,2,1,0:T(8,128)(2,1)} %refs_1_.1, ...), custom_call_target="tpu_custom_call" | custom-call | tf_op jit(solution)/shard_map/pallas_call | solution.py:243
  10.3 0.0 collective-permute-done.refs_0_
  10.3 1.6 %collective-permute-start.1 = (bf16[1,3,128,512]{3,2,1,0:T(8,128)(2,1)S(1)}, bf16[1,3,128,512]{3,2,1,0:T(8,128)(2,1)S(1)}, u32[]{:S(2)}, u32[]{:S(2)}) collective-permute-start(bf16[1,3,128,512]{3,2,1,0:T(8,128)(2,1)S(1)} %collective-permute-done.refs_0_), channel_id=1, source_target_pairs={{0,8},{1,5},{2,10},{3,7},{8,16},{9,1},{10,18},{11,3},{16,24},{17,9... | collective-permute-start | bytes 1179656 | tf_op jit(solution)/shard_map/ppermute | solution.py:318
  11.9 0.0 collective-permute-start.5
  11.9 0.5 %collective-permute-start.6 = (s32[4,3]{1,0:T(4,128)S(1)}, s32[4,3]{1,0:T(4,128)S(1)}, u32[]{:S(2)}, u32[]{:S(2)}) collective-permute-start(s32[4,3]{1,0:T(4,128)S(1)} %copy-done), channel_id=1, source_target_pairs={{0,1},{1,0},{2,3},{3,2},{4,5},{5,4},{6,7},{7,6},{8,9},{9,8},{10,11... | collective-permute-start | bytes 152 | tf_op jit(solution)/shard_map/ppermute | solution.py:321
  12.4 0.8 %collective-permute-done.6.refs_7_ = s32[4,3]{1,0:T(4,128)S(1)} collective-permute-done((s32[4,3]{1,0:T(4,128)S(1)}, s32[4,3]{1,0:T(4,128)S(1)}, u32[]{:S(2)}, u32[]{:S(2)}) %collective-permute-start.6) | collective-permute-done | bytes 80 | tf_op jit(solution)/shard_map/ppermute | solution.py:321
  13.3 0.0 collective-permute-done.5.refs_6_
  13.3 1.3 %shard_map.92.refs_8_.refs_0_ = f32[2,128,128]{2,1,0:T(8,128)S(1)} custom-call(bf16[1,3,128,512]{3,2,1,0:T(8,128)(2,1)S(1)} %get-tuple-element.33.refs_0_, bf16[4,3,128,512]{3,2,1,0:T(8,128)(2,1)S(1)} %get-tuple-element.30.refs_1_, s32[3,8]{1,0:T(4,128)S(1)} %get-tuple-element.31.refs_2_, s32[4,3]{1,0:T(4,128)S(1)} %get-tuple-element.32.refs_3_, ...), custom_call_target="tpu_custom_call" | custom-call | flops 201326592 | bytes 3932160 | tf_op jit(solution)/shard_map/pallas_call | solution.py:170
  14.5 0.0 collective-permute-done.3.refs_4_
  14.6 1.6 %collective-permute-start.8 = (bf16[1,3,128,512]{3,2,1,0:T(8,128)(2,1)S(1)}, bf16[1,3,128,512]{3,2,1,0:T(8,128)(2,1)S(1)}, u32[]{:S(2)}, u32[]{:S(2)}) collective-permute-start(bf16[1,3,128,512]{3,2,1,0:T(8,128)(2,1)S(1)} %collective-permute-done.3.refs_4_), channel_id=1, source_target_pairs={{0,8},{1,5},{2,10},{3,7},{8,16},{9,1},{10,18},{11,3},{16,24},{17,9... | collective-permute-start | bytes 1179656 | tf_op jit(solution)/shard_map/ppermute | solution.py:318
  16.2 1.8 %shard_map.93 = (f32[4,128,128]{2,1,0:T(8,128)S(1)}, s16[784,128]{1,0:T(8,128)(2,1)S(1)}) custom-call(bf16[1,3,128,512]{3,2,1,0:T(8,128)(2,1)S(1)} %collective-permute-done.refs_0_, bf16[4,3,128,512]{3,2,1,0:T(8,128)(2,1)S(1)} %get-tuple-element.30.refs_1_, s32[3,8]{1,0:T(4,128)S(1)} %get-tuple-element.31.refs_2_, s32[4,3]{1,0:T(4,128)S(1)} %get-tuple-element.32.refs_3_, ...), custom_call_target="tpu_custom_call" | custom-call | flops 402653184 | bytes 3932160 | tf_op jit(solution)/shard_map/pallas_call | solution.py:170
  18.0 0.2 collective-permute-done.1.refs_0_
  18.1 1.8 %collective-permute-start.7 = (bf16[1,3,128,512]{3,2,1,0:T(8,128)(2,1)S(1)}, bf16[1,3,128,512]{3,2,1,0:T(8,128)(2,1)S(1)}, u32[]{:S(2)}, u32[]{:S(2)}) collective-permute-start(bf16[1,3,128,512]{3,2,1,0:T(8,128)(2,1)S(1)} %collective-permute-done.1.refs_0_), channel_id=1, source_target_pairs={{0,8},{1,5},{2,10},{3,7},{8,16},{9,1},{10,18},{11,3},{16,24},{17,9... | collective-permute-start | bytes 1179656 | tf_op jit(solution)/shard_map/ppermute | solution.py:318
  20.0 1.5 %collective-permute-start.9 = (s16[784,128]{1,0:T(8,128)(2,1)S(1)}, s16[784,128]{1,0:T(8,128)(2,1)S(1)}, u32[]{:S(2)}, u32[]{:S(2)}) collective-permute-start(s16[784,128]{1,0:T(8,128)(2,1)S(1)} %get-tuple-element.38), channel_id=1, source_target_pairs={{0,2},{1,3},{2,0},{3,1},{4,6},{5,7},{6,4},{7,5},{8,10},{9,11},{10,... | collective-permute-start | bytes 602120 | tf_op jit(solution)/shard_map/ppermute | solution.py:324
  21.4 0.9 %collective-permute-done.8.refs_4_ = bf16[1,3,128,512]{3,2,1,0:T(8,128)(2,1)S(1)} collective-permute-done((bf16[1,3,128,512]{3,2,1,0:T(8,128)(2,1)S(1)}, bf16[1,3,128,512]{3,2,1,0:T(8,128)(2,1)S(1)}, u32[]{:S(2)}, u32[]{:S(2)}) %collective-permute-start.8) | collective-permute-done | bytes 393248 | tf_op jit(solution)/shard_map/ppermute | solution.py:318
  22.4 1.8 %collective-permute-start.10 = (bf16[1,3,128,512]{3,2,1,0:T(8,128)(2,1)S(1)}, bf16[1,3,128,512]{3,2,1,0:T(8,128)(2,1)S(1)}, u32[]{:S(2)}, u32[]{:S(2)}) collective-permute-start(bf16[1,3,128,512]{3,2,1,0:T(8,128)(2,1)S(1)} %collective-permute-done.8.refs_4_), channel_id=1, source_target_pairs={{0,8},{1,5},{2,10},{3,7},{8,16},{9,1},{10,18},{11,3},{16,24},{17,9... | collective-permute-start | bytes 1179656 | tf_op jit(solution)/shard_map/ppermute | solution.py:318
  24.2 1.8 %shard_map.94 = (f32[4,128,128]{2,1,0:T(8,128)S(1)}, s16[528,128]{1,0:T(8,128)(2,1)S(1)}) custom-call(bf16[1,3,128,512]{3,2,1,0:T(8,128)(2,1)S(1)} %collective-permute-done.1.refs_0_, bf16[4,3,128,512]{3,2,1,0:T(8,128)(2,1)S(1)} %get-tuple-element.30.refs_1_, s32[3,8]{1,0:T(4,128)S(1)} %get-tuple-element.31.refs_2_, s32[4,3]{1,0:T(4,128)S(1)} %get-tuple-element.32.refs_3_, ...), custom_call_target="tpu_custom_call" | custom-call | flops 402653184 | bytes 3932160 | tf_op jit(solution)/shard_map/pallas_call | solution.py:170
  25.9 0.0 collective-permute-done.9.refs_2_
  26.0 0.6 %collective-permute-done.7.refs_0_ = bf16[1,3,128,512]{3,2,1,0:T(8,128)(2,1)S(1)} collective-permute-done((bf16[1,3,128,512]{3,2,1,0:T(8,128)(2,1)S(1)}, bf16[1,3,128,512]{3,2,1,0:T(8,128)(2,1)S(1)}, u32[]{:S(2)}, u32[]{:S(2)}) %collective-permute-start.7) | collective-permute-done | bytes 393248 | tf_op jit(solution)/shard_map/ppermute | solution.py:318
  26.6 1.8 %collective-permute-start.12 = (bf16[1,3,128,512]{3,2,1,0:T(8,128)(2,1)S(1)}, bf16[1,3,128,512]{3,2,1,0:T(8,128)(2,1)S(1)}, u32[]{:S(2)}, u32[]{:S(2)}) collective-permute-start(bf16[1,3,128,512]{3,2,1,0:T(8,128)(2,1)S(1)} %collective-permute-done.7.refs_0_), channel_id=1, source_target_pairs={{0,8},{1,5},{2,10},{3,7},{8,16},{9,1},{10,18},{11,3},{16,24},{17,9... | collective-permute-start | bytes 1179656 | tf_op jit(solution)/shard_map/ppermute | solution.py:318
  28.4 1.5 %collective-permute-start.13 = (s16[528,128]{1,0:T(8,128)(2,1)S(1)}, s16[528,128]{1,0:T(8,128)(2,1)S(1)}, u32[]{:S(2)}, u32[]{:S(2)}) collective-permute-start(s16[528,128]{1,0:T(8,128)(2,1)S(1)} %get-tuple-element.42), channel_id=1, source_target_pairs={{0,2},{1,3},{2,0},{3,1},{4,6},{5,7},{6,4},{7,5},{8,10},{9,11},{10,... | collective-permute-start | bytes 405512 | tf_op jit(solution)/shard_map/ppermute | solution.py:324
  29.9 0.9 %collective-permute-done.10.refs_4_ = bf16[1,3,128,512]{3,2,1,0:T(8,128)(2,1)S(1)} collective-permute-done((bf16[1,3,128,512]{3,2,1,0:T(8,128)(2,1)S(1)}, bf16[1,3,128,512]{3,2,1,0:T(8,128)(2,1)S(1)}, u32[]{:S(2)}, u32[]{:S(2)}) %collective-permute-start.10) | collective-permute-done | bytes 393248 | tf_op jit(solution)/shard_map/ppermute | solution.py:318
  30.8 1.8 %shard_map.95 = (f32[4,128,128]{2,1,0:T(8,128)S(1)}, s16[528,128]{1,0:T(8,128)(2,1)S(1)}) custom-call(bf16[1,3,128,512]{3,2,1,0:T(8,128)(2,1)S(1)} %collective-permute-done.7.refs_0_, bf16[4,3,128,512]{3,2,1,0:T(8,128)(2,1)S(1)} %get-tuple-element.30.refs_1_, s32[3,8]{1,0:T(4,128)S(1)} %get-tuple-element.31.refs_2_, s32[4,3]{1,0:T(4,128)S(1)} %get-tuple-element.32.refs_3_, ...), custom_call_target="tpu_custom_call" | custom-call | flops 402653184 | bytes 3932160 | tf_op jit(solution)/shard_map/pallas_call | solution.py:170
  32.6 0.8 %collective-permute-done.13.refs_4_ = s16[528,128]{1,0:T(8,128)(2,1)S(1)} collective-permute-done((s16[528,128]{1,0:T(8,128)(2,1)S(1)}, s16[528,128]{1,0:T(8,128)(2,1)S(1)}, u32[]{:S(2)}, u32[]{:S(2)}) %collective-permute-start.13) | collective-permute-done | bytes 135200 | tf_op jit(solution)/shard_map/ppermute | solution.py:324
  33.4 0.1 shard_map.96.mine_ref
  33.5 0.1 collective-permute-start.20
  33.6 1.5 %collective-permute-done.12.refs_0_ = bf16[1,3,128,512]{3,2,1,0:T(8,128)(2,1)S(1)} collective-permute-done((bf16[1,3,128,512]{3,2,1,0:T(8,128)(2,1)S(1)}, bf16[1,3,128,512]{3,2,1,0:T(8,128)(2,1)S(1)}, u32[]{:S(2)}, u32[]{:S(2)}) %collective-permute-start.12) | collective-permute-done | bytes 393248 | tf_op jit(solution)/shard_map/ppermute | solution.py:318
  35.0 1.7 %collective-permute-start.11 = (s16[528,128]{1,0:T(8,128)(2,1)S(1)}, s16[528,128]{1,0:T(8,128)(2,1)S(1)}, u32[]{:S(2)}, u32[]{:S(2)}) collective-permute-start(s16[528,128]{1,0:T(8,128)(2,1)S(1)} %get-tuple-element.41), channel_id=1, source_target_pairs={{0,2},{1,3},{2,0},{3,1},{4,6},{5,7},{6,4},{7,5},{8,10},{9,11},{10,... | collective-permute-start | bytes 405512 | tf_op jit(solution)/shard_map/ppermute | solution.py:324
  36.7 0.2 collective-permute-start.16
  37.0 0.0 collective-permute-done.14.refs_4_
  37.0 1.3 %shard_map.97 = (f32[2,128,128]{2,1,0:T(8,128)S(1)}, s16[272,128]{1,0:T(8,128)(2,1)S(1)}) custom-call(bf16[1,3,128,512]{3,2,1,0:T(8,128)(2,1)S(1)} %collective-permute-done.12.refs_0_, bf16[4,3,128,512]{3,2,1,0:T(8,128)(2,1)S(1)} %get-tuple-element.30.refs_1_, s32[3,8]{1,0:T(4,128)S(1)} %get-tuple-element.31.refs_2_, s32[4,3]{1,0:T(4,128)S(1)} %get-tuple-element.32.refs_3_, ...), custom_call_target="tpu_custom_call" | custom-call | flops 201326592 | bytes 3932160 | tf_op jit(solution)/shard_map/pallas_call | solution.py:170
  38.3 1.6 %collective-permute-start.15 = (s16[272,128]{1,0:T(8,128)(2,1)S(1)}, s16[272,128]{1,0:T(8,128)(2,1)S(1)}, u32[]{:S(2)}, u32[]{:S(2)}) collective-permute-start(s16[272,128]{1,0:T(8,128)(2,1)S(1)} %get-tuple-element.47), channel_id=1, source_target_pairs={{0,2},{1,3},{2,0},{3,1},{4,6},{5,7},{6,4},{7,5},{8,10},{9,11},{10,... | collective-permute-start | bytes 208904 | tf_op jit(solution)/shard_map/ppermute | solution.py:324
  39.8 1.2 %collective-permute-done.11.refs_1_ = s16[528,128]{1,0:T(8,128)(2,1)S(1)} collective-permute-done((s16[528,128]{1,0:T(8,128)(2,1)S(1)}, s16[528,128]{1,0:T(8,128)(2,1)S(1)}, u32[]{:S(2)}, u32[]{:S(2)}) %collective-permute-start.11) | collective-permute-done | bytes 135200 | tf_op jit(solution)/shard_map/ppermute | solution.py:324
  41.0 0.0 collective-permute-start.17
  41.0 0.5 %collective-permute-start.18 = (f32[2,128,128]{2,1,0:T(8,128)S(1)}, f32[2,128,128]{2,1,0:T(8,128)S(1)}, u32[]{:S(2)}, u32[]{:S(2)}) collective-permute-start(f32[2,128,128]{2,1,0:T(8,128)S(1)} %get-tuple-element.46.refs_2_), channel_id=1, source_target_pairs={{0,1},{1,0},{2,3},{3,2},{4,5},{5,4},{6,7},{7,6},{8,9},{9,8},{10,11... | collective-permute-start | bytes 393224 | tf_op jit(solution)/shard_map/ppermute | solution.py:321
  41.5 1.2 %collective-permute-done.15.refs_3_ = s16[272,128]{1,0:T(8,128)(2,1)S(1)} collective-permute-done((s16[272,128]{1,0:T(8,128)(2,1)S(1)}, s16[272,128]{1,0:T(8,128)(2,1)S(1)}, u32[]{:S(2)}, u32[]{:S(2)}) %collective-permute-start.15) | collective-permute-done | bytes 69664 | tf_op jit(solution)/shard_map/ppermute | solution.py:324
  42.7 0.0 collective-permute-start.19
  42.7 0.0 collective-permute-done.20.other_ref
  42.7 0.2 shard_map.98.refs_8_
  42.9 0.0 collective-permute-done.16.refs_4_
  42.9 0.0 collective-permute-done.17.refs_5_
  42.9 1.1 %collective-permute-done.19.refs_7_ = s16[272,128]{1,0:T(8,128)(2,1)S(1)} collective-permute-done((s16[272,128]{1,0:T(8,128)(2,1)S(1)}, s16[272,128]{1,0:T(8,128)(2,1)S(1)}, u32[]{:S(2)}, u32[]{:S(2)}) %collective-permute-start.19) | collective-permute-done | bytes 69664 | tf_op jit(solution)/shard_map/ppermute | solution.py:321
  44.0 1.7 %shard_map.99 = (f32[33,128,128]{2,1,0:T(8,128)S(1)}, f32[24,128,128]{2,1,0:T(8,128)}) custom-call(s32[24]{0:T(128)S(1)} %get-tuple-element.27.slot_ref, f32[32,128,128]{2,1,0:T(8,128)S(1)} %get-tuple-element.28.scale_ref, f32[4,128,128]{2,1,0:T(8,128)S(1)} %get-tuple-element.40.refs_0_, ...), custom_call_target="tpu_custom_call", output_to_operand_aliasing={{0}: (10, {})} | custom-call | tf_op jit(solution)/shard_map/pallas_call | solution.py:374
  (7 shorter events, 0.0 us)
Async XLA Ops:
  0.0 11.9 %copy-start = (s32[4,3]{1,0:T(4,128)S(1)}, s32[4,3]{1,0:T(4,128)}, u32[]{:S(2)}) copy-start(s32[4,3]{1,0:T(4,128)} %refs_3_.1) | copy-start | bytes 148
  0.0 11.9 %copy-start.1 = (s32[8,3]{0,1:T(4,128)S(1)}, s32[8,3]{0,1:T(4,128)}, u32[]{:S(2)}) copy-start(s32[8,3]{0,1:T(4,128)} %param.10) | copy-start | bytes 292
  0.0 13.3 %collective-permute-start.4 = (bf16[4,3,128,512]{3,2,1,0:T(8,128)(2,1)}, bf16[4,3,128,512]{3,2,1,0:T(8,128)(2,1)S(1)}, u32[]{:S(2)}, u32[]{:S(2)}) collective-permute-start(bf16[4,3,128,512]{3,2,1,0:T(8,128)(2,1)} %refs_0_.1), channel_id=1, source_target_pairs={{0,1},{1,0},{2,3},{3,2},{4,5},{5,4},{6,7},{7,6},{8,9},{9,8},{10,11... | collective-permute-start | bytes 4718600 | tf_op jit(solution)/shard_map/ppermute | solution.py:321
  0.5 3.8 %collective-permute-start.2 = (bf16[1,3,128,512]{3,2,1,0:T(8,128)(2,1)}, bf16[1,3,128,512]{3,2,1,0:T(8,128)(2,1)S(1)}, u32[]{:S(2)}, u32[]{:S(2)}) collective-permute-start(bf16[1,3,128,512]{3,2,1,0:T(8,128)(2,1)} %refs_1_.1), channel_id=1, source_target_pairs={{0,1},{1,0},{2,3},{3,2},{4,5},{5,4},{6,7},{7,6},{8,9},{9,8},{10,11... | collective-permute-start | bytes 1179656 | tf_op jit(solution)/shard_map/ppermute | solution.py:321
  0.5 9.8 %collective-permute-start = (bf16[1,3,128,512]{3,2,1,0:T(8,128)(2,1)}, bf16[1,3,128,512]{3,2,1,0:T(8,128)(2,1)S(1)}, u32[]{:S(2)}, u32[]{:S(2)}) collective-permute-start(bf16[1,3,128,512]{3,2,1,0:T(8,128)(2,1)} %refs_1_.1), channel_id=1, source_target_pairs={{0,8},{1,5},{2,10},{3,7},{8,16},{9,1},{10,18},{11,3},{16,24},{17,9... | collective-permute-start | bytes 1179656 | tf_op jit(solution)/shard_map/ppermute | solution.py:318
  4.3 10.3 %collective-permute-start.3 = (bf16[1,3,128,512]{3,2,1,0:T(8,128)(2,1)S(1)}, bf16[1,3,128,512]{3,2,1,0:T(8,128)(2,1)S(1)}, u32[]{:S(2)}, u32[]{:S(2)}) collective-permute-start(bf16[1,3,128,512]{3,2,1,0:T(8,128)(2,1)S(1)} %collective-permute-done.2.refs_4_), channel_id=1, source_target_pairs={{0,8},{1,5},{2,10},{3,7},{8,16},{9,1},{10,18},{11,3},{16,24},{17,9... | collective-permute-start | bytes 1179656 | tf_op jit(solution)/shard_map/ppermute | solution.py:318
  10.3 7.8 %collective-permute-start.1 = (bf16[1,3,128,512]{3,2,1,0:T(8,128)(2,1)S(1)}, bf16[1,3,128,512]{3,2,1,0:T(8,128)(2,1)S(1)}, u32[]{:S(2)}, u32[]{:S(2)}) collective-permute-start(bf16[1,3,128,512]{3,2,1,0:T(8,128)(2,1)S(1)} %collective-permute-done.refs_0_), channel_id=1, source_target_pairs={{0,8},{1,5},{2,10},{3,7},{8,16},{9,1},{10,18},{11,3},{16,24},{17,9... | collective-permute-start | bytes 1179656 | tf_op jit(solution)/shard_map/ppermute | solution.py:318
  11.9 1.3 %collective-permute-start.5 = (s32[3,8]{1,0:T(4,128)S(1)}, s32[3,8]{1,0:T(4,128)S(1)}, u32[]{:S(2)}, u32[]{:S(2)}) collective-permute-start(s32[3,8]{1,0:T(4,128)S(1)} %bitcast.6), channel_id=1, source_target_pairs={{0,1},{1,0},{2,3},{3,2},{4,5},{5,4},{6,7},{7,6},{8,9},{9,8},{10,11... | collective-permute-start | bytes 296 | tf_op jit(solution)/shard_map/ppermute | solution.py:321
  11.9 1.3 %collective-permute-start.6 = (s32[4,3]{1,0:T(4,128)S(1)}, s32[4,3]{1,0:T(4,128)S(1)}, u32[]{:S(2)}, u32[]{:S(2)}) collective-permute-start(s32[4,3]{1,0:T(4,128)S(1)} %copy-done), channel_id=1, source_target_pairs={{0,1},{1,0},{2,3},{3,2},{4,5},{5,4},{6,7},{7,6},{8,9},{9,8},{10,11... | collective-permute-start | bytes 152 | tf_op jit(solution)/shard_map/ppermute | solution.py:321
  14.6 7.8 %collective-permute-start.8 = (bf16[1,3,128,512]{3,2,1,0:T(8,128)(2,1)S(1)}, bf16[1,3,128,512]{3,2,1,0:T(8,128)(2,1)S(1)}, u32[]{:S(2)}, u32[]{:S(2)}) collective-permute-start(bf16[1,3,128,512]{3,2,1,0:T(8,128)(2,1)S(1)} %collective-permute-done.3.refs_4_), channel_id=1, source_target_pairs={{0,8},{1,5},{2,10},{3,7},{8,16},{9,1},{10,18},{11,3},{16,24},{17,9... | collective-permute-start | bytes 1179656 | tf_op jit(solution)/shard_map/ppermute | solution.py:318
  18.1 8.5 %collective-permute-start.7 = (bf16[1,3,128,512]{3,2,1,0:T(8,128)(2,1)S(1)}, bf16[1,3,128,512]{3,2,1,0:T(8,128)(2,1)S(1)}, u32[]{:S(2)}, u32[]{:S(2)}) collective-permute-start(bf16[1,3,128,512]{3,2,1,0:T(8,128)(2,1)S(1)} %collective-permute-done.1.refs_0_), channel_id=1, source_target_pairs={{0,8},{1,5},{2,10},{3,7},{8,16},{9,1},{10,18},{11,3},{16,24},{17,9... | collective-permute-start | bytes 1179656 | tf_op jit(solution)/shard_map/ppermute | solution.py:318
  20.0 6.0 %collective-permute-start.9 = (s16[784,128]{1,0:T(8,128)(2,1)S(1)}, s16[784,128]{1,0:T(8,128)(2,1)S(1)}, u32[]{:S(2)}, u32[]{:S(2)}) collective-permute-start(s16[784,128]{1,0:T(8,128)(2,1)S(1)} %get-tuple-element.38), channel_id=1, source_target_pairs={{0,2},{1,3},{2,0},{3,1},{4,6},{5,7},{6,4},{7,5},{8,10},{9,11},{10,... | collective-permute-start | bytes 602120 | tf_op jit(solution)/shard_map/ppermute | solution.py:324
  22.4 8.4 %collective-permute-start.10 = (bf16[1,3,128,512]{3,2,1,0:T(8,128)(2,1)S(1)}, bf16[1,3,128,512]{3,2,1,0:T(8,128)(2,1)S(1)}, u32[]{:S(2)}, u32[]{:S(2)}) collective-permute-start(bf16[1,3,128,512]{3,2,1,0:T(8,128)(2,1)S(1)} %collective-permute-done.8.refs_4_), channel_id=1, source_target_pairs={{0,8},{1,5},{2,10},{3,7},{8,16},{9,1},{10,18},{11,3},{16,24},{17,9... | collective-permute-start | bytes 1179656 | tf_op jit(solution)/shard_map/ppermute | solution.py:318
  26.6 8.4 %collective-permute-start.12 = (bf16[1,3,128,512]{3,2,1,0:T(8,128)(2,1)S(1)}, bf16[1,3,128,512]{3,2,1,0:T(8,128)(2,1)S(1)}, u32[]{:S(2)}, u32[]{:S(2)}) collective-permute-start(bf16[1,3,128,512]{3,2,1,0:T(8,128)(2,1)S(1)} %collective-permute-done.7.refs_0_), channel_id=1, source_target_pairs={{0,8},{1,5},{2,10},{3,7},{8,16},{9,1},{10,18},{11,3},{16,24},{17,9... | collective-permute-start | bytes 1179656 | tf_op jit(solution)/shard_map/ppermute | solution.py:318
  28.4 5.0 %collective-permute-start.13 = (s16[528,128]{1,0:T(8,128)(2,1)S(1)}, s16[528,128]{1,0:T(8,128)(2,1)S(1)}, u32[]{:S(2)}, u32[]{:S(2)}) collective-permute-start(s16[528,128]{1,0:T(8,128)(2,1)S(1)} %get-tuple-element.42), channel_id=1, source_target_pairs={{0,2},{1,3},{2,0},{3,1},{4,6},{5,7},{6,4},{7,5},{8,10},{9,11},{10,... | collective-permute-start | bytes 405512 | tf_op jit(solution)/shard_map/ppermute | solution.py:324
  33.5 9.2 %collective-permute-start.20 = (f32[10,128,128]{2,1,0:T(8,128)S(1)}, f32[10,128,128]{2,1,0:T(8,128)S(1)}, u32[]{:S(2)}, u32[]{:S(2)}) collective-permute-start(f32[10,128,128]{2,1,0:T(8,128)S(1)} %shard_map.96.mine_ref), channel_id=1, source_target_pairs={{0,1},{1,0},{2,3},{3,2},{4,5},{5,4},{6,7},{7,6},{8,9},{9,8},{10,11... | collective-permute-start | bytes 1966088 | tf_op jit(solution)/shard_map/ppermute | solution.py:321
  35.0 1.9 %collective-permute-start.14 = (bf16[1,3,128,512]{3,2,1,0:T(8,128)(2,1)S(1)}, bf16[1,3,128,512]{3,2,1,0:T(8,128)(2,1)S(1)}, u32[]{:S(2)}, u32[]{:S(2)}) collective-permute-start(bf16[1,3,128,512]{3,2,1,0:T(8,128)(2,1)S(1)} %collective-permute-done.12.refs_0_), channel_id=1, source_target_pairs={{0,1},{1,0},{2,3},{3,2},{4,5},{5,4},{6,7},{7,6},{8,9},{9,8},{10,11... | collective-permute-start | bytes 1179656 | tf_op jit(solution)/shard_map/ppermute | solution.py:321
  35.0 6.0 %collective-permute-start.11 = (s16[528,128]{1,0:T(8,128)(2,1)S(1)}, s16[528,128]{1,0:T(8,128)(2,1)S(1)}, u32[]{:S(2)}, u32[]{:S(2)}) collective-permute-start(s16[528,128]{1,0:T(8,128)(2,1)S(1)} %get-tuple-element.41), channel_id=1, source_target_pairs={{0,2},{1,3},{2,0},{3,1},{4,6},{5,7},{6,4},{7,5},{8,10},{9,11},{10,... | collective-permute-start | bytes 405512 | tf_op jit(solution)/shard_map/ppermute | solution.py:324
  36.7 6.2 %collective-permute-start.16 = (f32[4,128,128]{2,1,0:T(8,128)S(1)}, f32[4,128,128]{2,1,0:T(8,128)S(1)}, u32[]{:S(2)}, u32[]{:S(2)}) collective-permute-start(f32[4,128,128]{2,1,0:T(8,128)S(1)} %get-tuple-element.40.refs_0_), channel_id=1, source_target_pairs={{0,1},{1,0},{2,3},{3,2},{4,5},{5,4},{6,7},{7,6},{8,9},{9,8},{10,11... | collective-permute-start | bytes 786440 | tf_op jit(solution)/shard_map/ppermute | solution.py:321
  38.3 4.4 %collective-permute-start.15 = (s16[272,128]{1,0:T(8,128)(2,1)S(1)}, s16[272,128]{1,0:T(8,128)(2,1)S(1)}, u32[]{:S(2)}, u32[]{:S(2)}) collective-permute-start(s16[272,128]{1,0:T(8,128)(2,1)S(1)} %get-tuple-element.47), channel_id=1, source_target_pairs={{0,2},{1,3},{2,0},{3,1},{4,6},{5,7},{6,4},{7,5},{8,10},{9,11},{10,... | collective-permute-start | bytes 208904 | tf_op jit(solution)/shard_map/ppermute | solution.py:324
  41.0 1.9 %collective-permute-start.17 = (s16[528,128]{1,0:T(8,128)(2,1)S(1)}, s16[528,128]{1,0:T(8,128)(2,1)S(1)}, u32[]{:S(2)}, u32[]{:S(2)}) collective-permute-start(s16[528,128]{1,0:T(8,128)(2,1)S(1)} %collective-permute-done.11.refs_1_), channel_id=1, source_target_pairs={{0,1},{1,0},{2,3},{3,2},{4,5},{5,4},{6,7},{7,6},{8,9},{9,8},{10,11... | collective-permute-start | bytes 405512 | tf_op jit(solution)/shard_map/ppermute | solution.py:321
  41.0 1.9 %collective-permute-start.18 = (f32[2,128,128]{2,1,0:T(8,128)S(1)}, f32[2,128,128]{2,1,0:T(8,128)S(1)}, u32[]{:S(2)}, u32[]{:S(2)}) collective-permute-start(f32[2,128,128]{2,1,0:T(8,128)S(1)} %get-tuple-element.46.refs_2_), channel_id=1, source_target_pairs={{0,1},{1,0},{2,3},{3,2},{4,5},{5,4},{6,7},{7,6},{8,9},{9,8},{10,11... | collective-permute-start | bytes 393224 | tf_op jit(solution)/shard_map/ppermute | solution.py:321
  42.7 1.3 %collective-permute-start.19 = (s16[272,128]{1,0:T(8,128)(2,1)S(1)}, s16[272,128]{1,0:T(8,128)(2,1)S(1)}, u32[]{:S(2)}, u32[]{:S(2)}) collective-permute-start(s16[272,128]{1,0:T(8,128)(2,1)S(1)} %collective-permute-done.15.refs_3_), channel_id=1, source_target_pairs={{0,1},{1,0},{2,3},{3,2},{4,5},{5,4},{6,7},{7,6},{8,9},{9,8},{10,11... | collective-permute-start | bytes 208904 | tf_op jit(solution)/shard_map/ppermute | solution.py:321
